TPU v7x, 32 devices: a whole 2x2x4 slice. The times are simulated.
32 devices in a mesh: head: 4 (over z), blk: 8 (over y, x, core).
Axes of the slice: x: 2, y: 2, z: 4, core: 2. Of those that a mesh axis runs over, the one named last changes fastest.
Arguments:
- tokens: bfloat16 [32768, 768], P(('blk', 'head')), may hold values from -6 to 6
- w_query: bfloat16 [768, 768], P(('head', 'blk')), may hold values from -0.21875 to 0.21875
- w_key: bfloat16 [768, 768], P(('head', 'blk')), may hold values from -0.21875 to 0.21875
- w_value: bfloat16 [768, 768], P(('head', 'blk')), may hold values from -0.21875 to 0.21875
- w_attn: bfloat16 [768, 768], P(('head', 'blk')), may hold values from -3.5 to 3.5
- w_inner: bfloat16 [768, 3072], P(('head', 'blk')), may hold values from -0.21875 to 0.21875
- w_outer: bfloat16 [3072, 768], P(('head', 'blk')), may hold values from -0.109375 to 0.109375
- bias_query: bfloat16 [768], P(('head', 'blk')), may hold values from -3 to 3
- bias_value: bfloat16 [768], P(('head', 'blk')), may hold values from -3 to 3
- bias_attn: bfloat16 [768], P(('head', 'blk')), may hold values from -3 to 3
- gain_one: bfloat16 [768], P(('head', 'blk')), may hold values from 0.5 to 1.5
- offset_one: bfloat16 [768], P(('head', 'blk')), may hold values from -3 to 3
- bias_inner: bfloat16 [3072], P(('head', 'blk')), may hold values from -3 to 3
- bias_outer: bfloat16 [768], P(('head', 'blk')), may hold values from -3 to 3
- gain_two: bfloat16 [768], P(('head', 'blk')), may hold values from 0.5 to 1.5
- offset_two: bfloat16 [768], P(('head', 'blk')), may hold values from -3 to 3
- out_grad: bfloat16 [32768, 768], P(('blk', 'head')), may hold values from -6 to 6
- segment_ids: int32 [32768], replicated, may hold values from 0 to 163, as said below
- random_blocks: int32 [12, 512, 3], replicated, may hold values from 0 to 511, as said below
Outputs:
- output_rows: bfloat16 [32768, 768], P(('blk', 'head'))
- grad_tokens: float32 [32768, 768], P(('blk', 'head'))
- grad_w_query: float32 [768, 768], P(('head', 'blk'))
- grad_w_key: float32 [768, 768], P(('head', 'blk'))
- grad_w_value: float32 [768, 768], P(('head', 'blk'))
- grad_w_attn: float32 [768, 768], P(('head', 'blk'))
- grad_w_inner: float32 [768, 3072], P(('head', 'blk'))
- grad_w_outer: float32 [3072, 768], P(('head', 'blk'))
- grad_bias_query: float32 [768], P(('head', 'blk'))
- grad_bias_value: float32 [768], P(('head', 'blk'))
- grad_bias_attn: float32 [768], P(('head', 'blk'))
- grad_gain_one: float32 [768], P(('head', 'blk'))
- grad_offset_one: float32 [768], P(('head', 'blk'))
- grad_bias_inner: float32 [3072], P(('head', 'blk'))
- grad_bias_outer: float32 [768], P(('head', 'blk'))
- grad_gain_two: float32 [768], P(('head', 'blk'))
- grad_offset_two: float32 [768], P(('head', 'blk'))
Inputs may be any that keep to these rules, and one draw needn't show every extreme that they name: `segment_ids`: numbers never fall along the tokens; a document holds at most 2000 tokens, the first of every sequence exactly 2000, and every document but the last of its sequence 200 or more; no document crosses a boundary of the sequences of 32768 tokens, and different sequences have different numbers; the last document of all has the largest number. `random_blocks`: entry [h, b, r] is a block from the first to the last block that holds tokens of the document of block b's first token.
All inputs are finite; a program needn't handle non-finite values.
Results may differ from a plain program's by a relative error of at most 0.015.
Values may be sent and summed in bfloat16 or wider, within the bound.
A program may use at most 192 MiB of HBM per device.

v0:
```python
from functools import partial

import jax
import jax.numpy as jnp
from jax import lax
from jax.sharding import PartitionSpec as P

HEAD_DIM = 64
BLOCK = 64
RANDOM = 3
MARGIN = 2048


epsilon = 1e-06
masked_value = -1e30
row_limit = 512
query_scale = 0.125
highest_precision = lax.Precision.HIGHEST


def extended(block, sides, width):
    for axis, dim in sides:
        count = lax.axis_size(axis)
        forward = [(i, i + 1) for i in range(count - 1)]
        backward = [(target, source) for source, target in forward]
        low = lax.ppermute(
            lax.slice_in_dim(block, block.shape[dim] - width, None, axis=dim), axis, forward
        )
        high = lax.ppermute(lax.slice_in_dim(block, 0, width, axis=dim), axis, backward)
        block = jnp.concatenate([low, block, high], axis=dim)
    return block


def passed_along(x, axis, by):
    peers = lax.axis_size(axis)
    pairs = [(i, i + by) for i in range(peers) if 0 <= i + by < peers]
    return lax.ppermute(x, axis, pairs)


def layer_norm(values, gain_vec, offset):
    centred = values - jnp.mean(values, axis=-1, keepdims=True)
    spread = jnp.mean(centred * centred, axis=-1, keepdims=True)
    return centred * lax.rsqrt(spread + epsilon) * gain_vec + offset


def fetch_weights(shards):
    return (
        lax.all_gather(shards[0], ("head", "blk"), axis=0, tiled=True),
        lax.all_gather(shards[1], ("head", "blk"), axis=0, tiled=True),
        lax.all_gather(shards[2], ("head", "blk"), axis=0, tiled=True),
        lax.all_gather(shards[3], ("head", "blk"), axis=0, tiled=True),
        lax.all_gather(shards[4], ("head", "blk"), axis=0, tiled=True),
        lax.all_gather(shards[5], ("head", "blk"), axis=0, tiled=True),
        lax.all_gather(shards[6], ("head", "blk"), axis=0, tiled=True),
        lax.all_gather(shards[7], ("head", "blk"), axis=0, tiled=True),
        lax.all_gather(shards[8], ("head", "blk"), axis=0, tiled=True),
        lax.all_gather(shards[9], ("head", "blk"), axis=0, tiled=True),
        lax.all_gather(shards[10], ("head", "blk"), axis=0, tiled=True),
        lax.all_gather(shards[11], ("head", "blk"), axis=0, tiled=True),
        lax.all_gather(shards[12], ("head", "blk"), axis=0, tiled=True),
        lax.all_gather(shards[13], ("head", "blk"), axis=0, tiled=True),
        lax.all_gather(shards[14], ("head", "blk"), axis=0, tiled=True),
    )


def choose_tiles(block_ids, first_start, randoms, total_blocks):
    doc_first_block = first_start // BLOCK
    fixed_rows = jnp.stack(
        [block_ids - 1, block_ids, block_ids + 1, doc_first_block, doc_first_block + 1], axis=-1
    )
    head_count = randoms.shape[1]
    fixed_rows = jnp.broadcast_to(fixed_rows[:, None, :], (fixed_rows.shape[0], head_count, 5))
    tile_rows = jnp.concatenate([fixed_rows, randoms], axis=-1)
    tile_count = tile_rows.shape[-1]
    inside = (tile_rows >= 0) & (tile_rows < total_blocks)
    earlier = jnp.arange(tile_count)[None, :] < jnp.arange(tile_count)[:, None]
    repeat = jnp.any((tile_rows[..., :, None] == tile_rows[..., None, :]) & earlier, axis=-1)
    return (jnp.clip(tile_rows, 0, total_blocks - 1), inside & jnp.logical_not(repeat))


def row_selector(tile_rows, ext_blocks, dtype):
    return (tile_rows[..., None] == jnp.arange(ext_blocks, dtype=jnp.int32)).astype(dtype)


def tile_plan(segment_ids, random_blocks, group_rows, head_count):
    total_tokens = segment_ids.shape[0]
    total_blocks = total_tokens // BLOCK
    group_blocks = group_rows // BLOCK
    margin_blocks = MARGIN // BLOCK
    ext_blocks = group_blocks + 2 * margin_blocks
    first_block = lax.axis_index("blk") * group_blocks
    padded_ids = jnp.concatenate(
        [jnp.full((MARGIN,), -1, jnp.int32), segment_ids, jnp.full((MARGIN,), -2, jnp.int32)]
    )
    ext_segs = lax.dynamic_slice_in_dim(padded_ids, first_block * BLOCK, group_rows + 2 * MARGIN)
    window = first_block * BLOCK - MARGIN + jnp.arange(group_rows + MARGIN, dtype=jnp.int32)
    window_segs = ext_segs[: group_rows + MARGIN]
    starts = jnp.concatenate([jnp.ones((1,), jnp.bool_), window_segs[1:] != window_segs[:-1]]) | (
        window <= 0
    )
    doc_start = lax.cummax(jnp.where(starts, window, -total_tokens))
    first_start = doc_start[MARGIN::BLOCK]
    block_ids = first_block + jnp.arange(group_blocks, dtype=jnp.int32)
    head_start = lax.axis_index("head") * head_count
    randoms = lax.dynamic_slice(
        random_blocks, (head_start, first_block, jnp.int32(0)), (head_count, group_blocks, RANDOM)
    )
    tile_rows, tile_valid = choose_tiles(
        block_ids, first_start, jnp.transpose(randoms, (1, 0, 2)), total_blocks
    )
    local_rows = jnp.clip(tile_rows - (first_block - margin_blocks), 0, ext_blocks - 1)
    selector = row_selector(local_rows, ext_blocks, jnp.float32)
    seg_table = ext_segs.reshape(ext_blocks, BLOCK).astype(jnp.float32)
    seg_keys = jnp.einsum("nhte,eb->nhtb", selector, seg_table, precision=highest_precision).astype(
        jnp.int32
    )
    seg_query = ext_segs[MARGIN : MARGIN + group_rows].reshape(group_blocks, BLOCK)
    return (local_rows, tile_valid, seg_query, seg_keys)


def pick_tiles(tile_table, tile_rows):
    ext_blocks = tile_table.shape[1]
    selector = row_selector(tile_rows, ext_blocks, tile_table.dtype)
    flat_table = tile_table.reshape(tile_table.shape[0], ext_blocks, -1)
    picked = jnp.einsum("nhte,hef->nhtf", selector, flat_table, preferred_element_type=jnp.float32)
    return picked.astype(tile_table.dtype).reshape(tile_rows.shape + tile_table.shape[2:])


def add_tiles(tile_table, tile_rows, tile_grads):
    ext_blocks = tile_table.shape[1]
    selector = row_selector(tile_rows, ext_blocks, jnp.float32)
    flat_grads = tile_grads.reshape(tile_rows.shape + (-1,))
    added = jnp.einsum("nhte,nhtf->hef", selector, flat_grads, precision=highest_precision)
    return tile_table + added.reshape(tile_table.shape)


def masked_scores(query_blocks, key_tiles, tile_valid, seg_query, seg_keys):
    scores = jnp.einsum(
        "nqhd,nhjtd->nhqjt", query_blocks, key_tiles, preferred_element_type=jnp.float32
    )
    allowed = tile_valid[:, :, None, :, None] & (
        seg_keys[:, :, None, :, :] == seg_query[:, None, :, None, None]
    )
    scores = jnp.where(allowed, scores, masked_value)
    return scores.reshape(scores.shape[0], scores.shape[1], scores.shape[2], -1)


def attend_forward(key_table, value_table, step_item):
    query_blocks, tile_rows, tile_valid, seg_query, seg_keys = step_item
    key_tiles = pick_tiles(key_table, tile_rows)
    value_tiles = pick_tiles(value_table, tile_rows)
    scores = masked_scores(query_blocks, key_tiles, tile_valid, seg_query, seg_keys)
    highest = jnp.max(scores, axis=-1, keepdims=True)
    raised = jnp.exp(scores - highest)
    totals = jnp.sum(raised, axis=-1, keepdims=True)
    prob_rows = (raised / totals).astype(jnp.bfloat16)
    values_flat = value_tiles.reshape(
        prob_rows.shape[0], prob_rows.shape[1], prob_rows.shape[3], -1
    )
    attended = jnp.einsum(
        "nhqk,nhkd->nqhd", prob_rows, values_flat, preferred_element_type=jnp.float32
    )
    return (attended.astype(jnp.bfloat16), (highest + jnp.log(totals))[..., 0])


def attend_backward(key_table, value_table, accum_pair, step_item):
    query_blocks, grad_out, log_total, tile_rows, tile_valid, seg_query, seg_keys = step_item
    key_tiles = pick_tiles(key_table, tile_rows)
    value_tiles = pick_tiles(value_table, tile_rows)
    scores = masked_scores(query_blocks, key_tiles, tile_valid, seg_query, seg_keys)
    prob_rows = jnp.exp(scores - log_total[..., None])
    flat_shape = (prob_rows.shape[0], prob_rows.shape[1], prob_rows.shape[3], -1)
    keys_flat = key_tiles.reshape(flat_shape)
    values_flat = value_tiles.reshape(flat_shape)
    grad_probs = jnp.einsum(
        "nqhd,nhkd->nhqk", grad_out, values_flat, preferred_element_type=jnp.float32
    )
    balance = jnp.sum(prob_rows * grad_probs, axis=-1, keepdims=True)
    grad_scores = (prob_rows * (grad_probs - balance)).astype(jnp.bfloat16)
    grad_query = jnp.einsum(
        "nhqk,nhkd->nqhd", grad_scores, keys_flat, preferred_element_type=jnp.float32
    )
    grad_keys = jnp.einsum(
        "nhqk,nqhd->nhkd", grad_scores, query_blocks, preferred_element_type=jnp.float32
    )
    grad_values = jnp.einsum(
        "nhqk,nqhd->nhkd",
        prob_rows.astype(jnp.bfloat16),
        grad_out,
        preferred_element_type=jnp.float32,
    )
    key_accum, value_accum = accum_pair
    key_accum = add_tiles(key_accum, tile_rows, grad_keys.reshape(key_tiles.shape))
    value_accum = add_tiles(value_accum, tile_rows, grad_values.reshape(value_tiles.shape))
    return ((key_accum, value_accum), grad_query.astype(jnp.bfloat16))


def forward_pass(tokens, full_params, segment_ids, random_blocks):
    (
        w_query,
        w_key,
        w_value,
        w_attn,
        w_inner,
        w_outer,
        bias_query,
        bias_value,
        bias_attn,
        gain_one,
        offset_one,
        bias_inner,
        bias_outer,
        gain_two,
        offset_two,
    ) = full_params
    queries = (
        query_scale * (jnp.dot(tokens, w_query, preferred_element_type=jnp.float32) + bias_query)
    ).astype(jnp.bfloat16)
    key_rows = jnp.dot(tokens, w_key, preferred_element_type=jnp.float32).astype(jnp.bfloat16)
    value_rows = (jnp.dot(tokens, w_value, preferred_element_type=jnp.float32) + bias_value).astype(
        jnp.bfloat16
    )
    by_heads = lax.all_to_all(
        jnp.stack([queries, key_rows, value_rows]), "head", split_axis=2, concat_axis=1, tiled=True
    )
    group_rows = by_heads.shape[1]
    head_cols = by_heads.shape[2]
    head_count = head_cols // HEAD_DIM
    group_blocks = group_rows // BLOCK
    widened = extended(by_heads[1:], (("blk", 1),), MARGIN)
    ext_blocks = widened.shape[1] // BLOCK
    tables = jnp.transpose(
        widened.reshape(2, ext_blocks, BLOCK, head_count, HEAD_DIM), (0, 3, 1, 2, 4)
    )
    tile_rows, tile_valid, seg_query, seg_keys = tile_plan(
        segment_ids, random_blocks, group_rows, head_count
    )
    step_blocks = min(group_blocks, row_limit // BLOCK)
    step_count = group_blocks // step_blocks
    step_items = (
        by_heads[0].reshape(step_count, step_blocks, BLOCK, head_count, HEAD_DIM),
        tile_rows.reshape(step_count, step_blocks, head_count, -1),
        tile_valid.reshape(step_count, step_blocks, head_count, -1),
        seg_query.reshape(step_count, step_blocks, BLOCK),
        seg_keys.reshape(step_count, step_blocks, head_count, -1, BLOCK),
    )
    attended, log_total = lax.map(partial(attend_forward, tables[0], tables[1]), step_items)
    attended_rows = lax.all_to_all(
        attended.reshape(group_rows, head_cols), "head", split_axis=0, concat_axis=1, tiled=True
    )
    attn_out = jnp.dot(attended_rows, w_attn, preferred_element_type=jnp.float32) + bias_attn
    first_norm, norm_one_back = jax.vjp(
        layer_norm,
        tokens.astype(jnp.float32) + attn_out,
        gain_one.astype(jnp.float32),
        offset_one.astype(jnp.float32),
    )
    first_low = first_norm.astype(jnp.bfloat16)
    inner_pre = jnp.dot(first_low, w_inner, preferred_element_type=jnp.float32) + bias_inner
    activated, gelu_back = jax.vjp(partial(jax.nn.gelu, approximate=True), inner_pre)
    activ_low = activated.astype(jnp.bfloat16)
    outer_out = jnp.dot(activ_low, w_outer, preferred_element_type=jnp.float32) + bias_outer
    result, norm_two_back = jax.vjp(
        layer_norm,
        first_norm + outer_out,
        gain_two.astype(jnp.float32),
        offset_two.astype(jnp.float32),
    )
    saved_state = (
        attended_rows,
        first_low,
        activ_low,
        gelu_back,
        norm_one_back,
        norm_two_back,
        step_items,
        log_total,
        tables,
        full_params,
    )
    return (result, saved_state)


def backward_pass(tokens, out_grad, saved_state):
    (
        attended_rows,
        first_low,
        activ_low,
        gelu_back,
        norm_one_back,
        norm_two_back,
        step_items,
        log_total,
        tables,
        full_params,
    ) = saved_state
    (
        w_query,
        w_key,
        w_value,
        w_attn,
        w_inner,
        w_outer,
        bias_query,
        bias_value,
        bias_attn,
        gain_one,
        offset_one,
        bias_inner,
        bias_outer,
        gain_two,
        offset_two,
    ) = full_params
    grad_second, grad_gain_two, grad_offset_two = norm_two_back(out_grad.astype(jnp.float32))
    grad_outer = grad_second.astype(jnp.bfloat16)
    grad_w_outer = jnp.dot(activ_low.T, grad_outer, preferred_element_type=jnp.float32)
    grad_bias_outer = jnp.sum(grad_outer.astype(jnp.float32), axis=0)
    grad_inner = gelu_back(jnp.dot(grad_outer, w_outer.T, preferred_element_type=jnp.float32))[
        0
    ].astype(jnp.bfloat16)
    grad_w_inner = jnp.dot(first_low.T, grad_inner, preferred_element_type=jnp.float32)
    grad_bias_inner = jnp.sum(grad_inner.astype(jnp.float32), axis=0)
    grad_first = grad_second + jnp.dot(grad_inner, w_inner.T, preferred_element_type=jnp.float32)
    grad_first_sum, grad_gain_one, grad_offset_one = norm_one_back(grad_first)
    grad_attn = grad_first_sum.astype(jnp.bfloat16)
    grad_w_attn = jnp.dot(attended_rows.T, grad_attn, preferred_element_type=jnp.float32)
    grad_bias_attn = jnp.sum(grad_attn.astype(jnp.float32), axis=0)
    grad_attended = jnp.dot(grad_attn, w_attn.T, preferred_element_type=jnp.float32).astype(
        jnp.bfloat16
    )
    grad_heads = lax.all_to_all(grad_attended, "head", split_axis=1, concat_axis=0, tiled=True)
    query_steps = step_items[0]
    head_cols = grad_heads.shape[1]
    zero_table = jnp.zeros(tables.shape[1:], jnp.float32)
    back_items = (
        query_steps,
        grad_heads.reshape(query_steps.shape),
        log_total,
        step_items[1],
        step_items[2],
        step_items[3],
        step_items[4],
    )
    (grad_key_table, grad_value_table), grad_queries = lax.scan(
        partial(attend_backward, tables[0], tables[1]), (zero_table, zero_table), back_items
    )
    grad_wide = jnp.transpose(
        jnp.stack([grad_key_table, grad_value_table]), (0, 2, 3, 1, 4)
    ).reshape(2, -1, head_cols)
    group_rows = grad_wide.shape[1] - 2 * MARGIN
    from_above = passed_along(grad_wide[:, :MARGIN].astype(jnp.bfloat16), "blk", -1).astype(
        jnp.float32
    )
    from_below = passed_along(
        grad_wide[:, MARGIN + group_rows :].astype(jnp.bfloat16), "blk", 1
    ).astype(jnp.float32)
    centre = grad_wide[:, MARGIN : MARGIN + group_rows]
    centre = centre.at[:, :MARGIN].add(from_below).at[:, group_rows - MARGIN :].add(from_above)
    grad_stack = jnp.concatenate(
        [grad_queries.reshape(1, group_rows, head_cols), centre.astype(jnp.bfloat16)]
    )
    grad_rows = lax.all_to_all(grad_stack, "head", split_axis=1, concat_axis=2, tiled=True)
    grad_scaled, grad_keyed, grad_valued = (grad_rows[0], grad_rows[1], grad_rows[2])
    grad_w_query = query_scale * jnp.dot(tokens.T, grad_scaled, preferred_element_type=jnp.float32)
    grad_bias_query = query_scale * jnp.sum(grad_scaled.astype(jnp.float32), axis=0)
    grad_w_key = jnp.dot(tokens.T, grad_keyed, preferred_element_type=jnp.float32)
    grad_w_value = jnp.dot(tokens.T, grad_valued, preferred_element_type=jnp.float32)
    grad_bias_value = jnp.sum(grad_valued.astype(jnp.float32), axis=0)
    grad_tokens = (
        grad_first_sum
        + query_scale * jnp.dot(grad_scaled, w_query.T, preferred_element_type=jnp.float32)
        + jnp.dot(grad_keyed, w_key.T, preferred_element_type=jnp.float32)
        + jnp.dot(grad_valued, w_value.T, preferred_element_type=jnp.float32)
    )
    grad_sums = (
        lax.psum_scatter(grad_w_query, ("head", "blk"), scatter_dimension=0, tiled=True),
        lax.psum_scatter(grad_w_key, ("head", "blk"), scatter_dimension=0, tiled=True),
        lax.psum_scatter(grad_w_value, ("head", "blk"), scatter_dimension=0, tiled=True),
        lax.psum_scatter(grad_w_attn, ("head", "blk"), scatter_dimension=0, tiled=True),
        lax.psum_scatter(grad_w_inner, ("head", "blk"), scatter_dimension=0, tiled=True),
        lax.psum_scatter(grad_w_outer, ("head", "blk"), scatter_dimension=0, tiled=True),
        lax.psum_scatter(grad_bias_query, ("head", "blk"), scatter_dimension=0, tiled=True),
        lax.psum_scatter(grad_bias_value, ("head", "blk"), scatter_dimension=0, tiled=True),
        lax.psum_scatter(grad_bias_attn, ("head", "blk"), scatter_dimension=0, tiled=True),
        lax.psum_scatter(grad_gain_one, ("head", "blk"), scatter_dimension=0, tiled=True),
        lax.psum_scatter(grad_offset_one, ("head", "blk"), scatter_dimension=0, tiled=True),
        lax.psum_scatter(grad_bias_inner, ("head", "blk"), scatter_dimension=0, tiled=True),
        lax.psum_scatter(grad_bias_outer, ("head", "blk"), scatter_dimension=0, tiled=True),
        lax.psum_scatter(grad_gain_two, ("head", "blk"), scatter_dimension=0, tiled=True),
        lax.psum_scatter(grad_offset_two, ("head", "blk"), scatter_dimension=0, tiled=True),
    )
    return (grad_tokens, grad_sums)


def per_device(
    tokens,
    w_query,
    w_key,
    w_value,
    w_attn,
    w_inner,
    w_outer,
    bias_query,
    bias_value,
    bias_attn,
    gain_one,
    offset_one,
    bias_inner,
    bias_outer,
    gain_two,
    offset_two,
    out_grad,
    segment_ids,
    random_blocks,
):
    shards = (
        w_query,
        w_key,
        w_value,
        w_attn,
        w_inner,
        w_outer,
        bias_query,
        bias_value,
        bias_attn,
        gain_one,
        offset_one,
        bias_inner,
        bias_outer,
        gain_two,
        offset_two,
    )
    first_result = forward_pass(tokens, fetch_weights(shards), segment_ids, random_blocks)[0]
    shards_again, tokens_again, first_result = lax.optimization_barrier(
        (shards, tokens, first_result)
    )
    saved_state = forward_pass(
        tokens_again, fetch_weights(shards_again), segment_ids, random_blocks
    )[1]
    grad_tokens, grad_sums = backward_pass(tokens, out_grad, saved_state)
    return (first_result.astype(jnp.bfloat16), grad_tokens) + tuple(grad_sums)


def solution(mesh):
    return jax.shard_map(
        per_device,
        mesh=mesh,
        in_specs=(
            P(("blk", "head"), None),
            P(("head", "blk"), None),
            P(("head", "blk"), None),
            P(("head", "blk"), None),
            P(("head", "blk"), None),
            P(("head", "blk"), None),
            P(("head", "blk"), None),
            P(("head", "blk")),
            P(("head", "blk")),
            P(("head", "blk")),
            P(("head", "blk")),
            P(("head", "blk")),
            P(("head", "blk")),
            P(("head", "blk")),
            P(("head", "blk")),
            P(("head", "blk")),
            P(("blk", "head"), None),
            P(),
            P(),
        ),
        out_specs=(
            P(("blk", "head"), None),
            P(("blk", "head"), None),
            P(("head", "blk"), None),
            P(("head", "blk"), None),
            P(("head", "blk"), None),
            P(("head", "blk"), None),
            P(("head", "blk"), None),
            P(("head", "blk"), None),
            P(("head", "blk")),
            P(("head", "blk")),
            P(("head", "blk")),
            P(("head", "blk")),
            P(("head", "blk")),
            P(("head", "blk")),
            P(("head", "blk")),
            P(("head", "blk")),
            P(("head", "blk")),
        ),
        check_vma=False,
    )
```

profile of v0, /device:TPU:0, one launch (start us, length us, event | category | flops | bytes accessed | tf_op | source)
XLA Modules:
  0.0 3220.5 jit_solution(18443448868598315937)
XLA Ops:
  18.2 43.0 %all-reduce.28 = (bf16[768]{0:T(1024)(128)(2,1)S(1)}, bf16[768]{0:T(1024)(128)(2,1)S(1)}, bf16[768]{0:T(1024)(128)(2,1)}, bf16[3072]{0:T(1024)(128)(2,1)}, bf16[...) all-reduce(bf16[768]{0:T(1024)(128)(2,1)S(1)} %dynamic-update-slice, ...), channel_id=1, replica_groups=mesh['head'=4,'blk'=8] {'head','blk'}, use_global_device_ids=true, to_apply=%add.1 | all-reduce | flops 9216 | bytes 36864
  71.1 52.9 %all-gather.13.cloned.1.call-done = bf16[768,768]{1,0:T(8,128)(2,1)} async-done(((bf16[24,768]{1,0:T(8,128)(2,1)}), bf16[768,768]{1,0:T(8,128)(2,1)}) %all-gather.13.cloned.1.call-update) | async-done | bytes 1179664 | tf_op jit(solution)/shard_map/all_gather | solution.py:48
  127.1 52.8 %all-gather.17.cloned.1.call-done = bf16[768,768]{1,0:T(8,128)(2,1)} async-done(((bf16[24,768]{1,0:T(8,128)(2,1)}), bf16[768,768]{1,0:T(8,128)(2,1)}) %all-gather.17.cloned.1.call-update) | async-done | bytes 1179664 | tf_op jit(solution)/shard_map/all_gather | solution.py:50
  203.9 144.9 %all-to-all-done = bf16[3,1024,768]{1,0,2:T(4,128)(2,1)} async-done(((bf16[3,1024,768]{1,0,2:T(4,128)(2,1)}), bf16[3,1024,768]{1,0,2:T(4,128)(2,1)}, u32[]{:S(2)}, u32[]{:S(2)}) %all-to-all-start) | async-done | bytes 4718624 | tf_op jit(solution)/shard_map/all_to_all | solution.py:223
  381.2 18.0 reshape.448
  427.0 344.5 %while.39 = (s32[]{:T(128)}, bf16[8,8,64,3,64]{2,1,0,4,3:T(8,128)(2,1)}, s32[8,8,3,8]{3,1,2,0:T(8,128)S(1)}, bf16[1,3,128,64,64]{2,4,3,1,0:T(8,128)(2,1)}, pred[...) while((s32[]{:T(128)}, ...), condition=%wide.region_6.7_spmd, body=%wide.region_3.6_spmd.sunk | while | flops 612774912 | bytes 75095856 | solution.py:247
  783.9 19.2 all-to-all-done.1
  808.7 18.7 fusion.156
  833.6 81.7 %all-reduce.27 = (bf16[768]{0:T(1024)(128)(2,1)S(1)}, bf16[768]{0:T(1024)(128)(2,1)S(1)}, bf16[768]{0:T(1024)(128)(2,1)}, bf16[768]{0:T(1024)(128)(2,1)}, bf16[7...) all-reduce(bf16[768]{0:T(1024)(128)(2,1)S(1)} %dynamic-update-slice, ...), channel_id=1, replica_groups=mesh['head'=4,'blk'=8] {'head','blk'}, use_global_device_ids=true, to_apply=%add.11 | all-reduce | flops 8448 | bytes 33792
  929.8 52.9 %all-gather.25.cloned.1.call-done = bf16[768,768]{1,0:T(8,128)(2,1)} async-done(((bf16[24,768]{1,0:T(8,128)(2,1)}), bf16[768,768]{1,0:T(8,128)(2,1)}) %all-gather.25.cloned.1.call-update) | async-done | bytes 1179664 | tf_op jit(solution)/shard_map/all_gather | solution.py:48
  985.9 52.8 %all-gather.29.cloned.1.call-done = bf16[768,768]{1,0:T(8,128)(2,1)} async-done(((bf16[24,768]{1,0:T(8,128)(2,1)}), bf16[768,768]{1,0:T(8,128)(2,1)}) %all-gather.29.cloned.1.call-update) | async-done | bytes 1179664 | tf_op jit(solution)/shard_map/all_gather | solution.py:50
  1061.8 145.6 %all-to-all-done.2 = bf16[3,1024,768]{1,0,2:T(4,128)(2,1)} async-done(((bf16[3,1024,768]{1,0,2:T(4,128)(2,1)}), bf16[3,1024,768]{1,0,2:T(4,128)(2,1)}, u32[]{:S(2)}, u32[]{:S(2)}) %all-to-all-start.2) | async-done | bytes 4718624 | tf_op jit(solution)/shard_map/all_to_all | solution.py:223
  1240.3 18.0 reshape.450
  1286.1 293.4 %while.40 = (s32[]{:T(128)}, bf16[8,8,64,3,64]{2,1,0,4,3:T(8,128)(2,1)}, f32[8,8,3,64]{3,2,1,0:T(4,128)}, s32[8,8,3,8]{3,1,2,0:T(8,128)S(1)}, bf16[1,3,128,64,64...) while((s32[]{:T(128)}, ...), condition=%wide.region_14.15_spmd, body=%wide.region_11.14_spmd.sunk | while | flops 612776448 | bytes 62738184 | solution.py:247
  1593.1 21.4 all-to-all-done.3
  1631.7 12.9 fusion.160
  1650.1 16.4 convert_reduce_fusion
  1707.0 13.8 fusion.142
  1740.2 768.3 %while.41 = (s32[]{:T(128)}, f32[3,128,64,64]{1,3,2,0:T(8,128)}, f32[3,128,64,64]{1,3,2,0:T(8,128)}, bf16[8,8,64,3,64]{2,1,0,4,3:T(8,128)(2,1)}, s32[8,8,3,8]{3,...) while((s32[]{:T(128)}, f32[3,128,64,64]{1,3,2,0:T(8,128)}, ...), condition=%wide.region_25.26_spmd.clone, body=%wide.region_23.25_spmd.clone.sunk | while | flops 3339385344 | bytes 191108560 | solution.py:344
  2013.1 11.9 select_add_fusion.3
  2508.5 12.0 maximum_bitcast_fusion
  2520.5 17.8 copy.560
  2538.3 20.8 reshape.453
  2566.5 30.8 collective-permute-start.4
  2613.1 29.2 collective-permute-done.5
  2653.1 12.7 copy.561
  2665.8 182.2 %all_to_all.99 = bf16[3,4096,192]{2,0,1:T(4,128)(2,1)} all-to-all(bf16[3,4096,192]{2,0,1:T(4,128)(2,1)} %copy.561), channel_id=1, replica_groups=mesh['head'=4,'blk'=8] {'head'}, dimensions={1} | all-to-all | bytes 9437184 | tf_op jit(solution)/shard_map/all_to_all | solution.py:362
  2848.0 13.7 copy.611
  2896.2 73.0 %all-reduce.26 = (f32[768]{0:T(1024)S(1)}, f32[768]{0:T(1024)S(1)}, f32[768]{0:T(1024)S(1)}, f32[768]{0:T(1024)S(1)}, f32[768]{0:T(1024)S(1)}, /*index=5*/f32[30...) all-reduce(f32[768]{0:T(1024)S(1)} %mul.301, ...), channel_id=8, replica_groups=mesh['head'=4,'blk'=8] {'head','blk'}, use_global_device_ids=true, to_apply=%region_33.34.clone | all-reduce | flops 9216 | bytes 73728
  2983.2 21.7 reduce-scatter.21.cloned.1.call-done
  3004.9 103.9 %reduce-scatter.19.cloned.1.call-done = f32[24,768]{1,0:T(8,128)} async-done(((f32[768,768]{1,0:T(8,128)}), f32[24,768]{1,0:T(8,128)}) %reduce-scatter.19.cloned.1.call-update) | async-done | bytes 73744
  3108.8 104.6 %reduce-scatter.23.cloned.1.call-done = f32[24,768]{1,0:T(8,128)} async-done(((f32[768,768]{1,0:T(8,128)}), f32[24,768]{1,0:T(8,128)}) %reduce-scatter.23.cloned.1.call-update) | async-done | bytes 73744
  (1026 shorter events, 1795.3 us)
Async XLA Ops:
  7.2 354.9 %copy-start = (s32[12,512,3]{1,2,0:T(4,128)S(1)}, s32[12,512,3]{1,2,0:T(4,128)}, u32[]{:S(2)}) copy-start(s32[12,512,3]{1,2,0:T(4,128)} %param.47) | copy-start | bytes 221188
  7.2 60.8 %all-gather.15.cloned.1.call-start = ((), (), s32[]{:S(2)}) async-start(), calls=%async_computation.13 | async-start | bytes 1216512 | tf_op jit(solution)/shard_map/all_gather | solution.py:49
  7.9 116.0 %all-gather.13.cloned.1.call-start = ((), (), s32[]{:S(2)}) async-start(), calls=%async_computation.12 | async-start | bytes 1216512 | tf_op jit(solution)/shard_map/all_gather | solution.py:48
  8.7 171.2 %all-gather.17.cloned.1.call-start = ((), (), s32[]{:S(2)}) async-start(), calls=%async_computation.14 | async-start | bytes 1216512 | tf_op jit(solution)/shard_map/all_gather | solution.py:50
  9.4 774.5 %all-gather.19.cloned.1.call-start = ((), (), s32[]{:S(2)}) async-start(), calls=%async_computation.15 | async-start | bytes 1216512 | tf_op jit(solution)/shard_map/all_gather | solution.py:51
  10.0 798.7 %all-gather.21.cloned.1.call-start = ((), (), s32[]{:S(2)}) async-start(), calls=%async_computation.16 | async-start | bytes 4866048 | tf_op jit(solution)/shard_map/all_gather | solution.py:52
  196.6 152.2 %all-to-all-start = ((bf16[3,1024,768]{1,0,2:T(4,128)(2,1)}), bf16[3,1024,768]{1,0,2:T(4,128)(2,1)}, u32[]{:S(2)}, u32[]{:S(2)}) async-start(bf16[3,1024,768]{1,0,2:T(4,128)(2,1)} %copy.528), calls=%async_computation | async-start | bytes 12582912 | tf_op jit(solution)/shard_map/all_to_all | solution.py:223
  202.0 606.7 %all-gather.23.cloned.1.call-start = ((), (), s32[]{:S(2)}) async-start(), calls=%async_computation.17 | async-start | bytes 4866048 | tf_op jit(solution)/shard_map/all_gather | solution.py:53
  358.0 18.3 collective-permute-start
  360.5 15.8 collective-permute-start.1
  778.0 25.2 all-to-all-start.1
  781.7 145.0 %all-gather.27.cloned.1.call-start = ((), (), s32[]{:S(2)}) async-start(), calls=%async_computation.19 | async-start | bytes 1216512 | tf_op jit(solution)/shard_map/all_gather | solution.py:49
  829.6 153.1 %all-gather.25.cloned.1.call-start = ((), (), s32[]{:S(2)}) async-start(), calls=%async_computation.18 | async-start | bytes 1216512 | tf_op jit(solution)/shard_map/all_gather | solution.py:48
  830.4 208.3 %all-gather.29.cloned.1.call-start = ((), (), s32[]{:S(2)}) async-start(), calls=%async_computation.20 | async-start | bytes 1216512 | tf_op jit(solution)/shard_map/all_gather | solution.py:50
  831.1 762.0 %all-gather.31.cloned.1.call-start = ((), (), s32[]{:S(2)}) async-start(), calls=%async_computation.21 | async-start | bytes 1216512 | tf_op jit(solution)/shard_map/all_gather | solution.py:51
  1055.3 152.1 %all-to-all-start.2 = ((bf16[3,1024,768]{1,0,2:T(4,128)(2,1)}), bf16[3,1024,768]{1,0,2:T(4,128)(2,1)}, u32[]{:S(2)}, u32[]{:S(2)}) async-start(bf16[3,1024,768]{1,0,2:T(4,128)(2,1)} %copy.541), calls=%async_computation.2 | async-start | bytes 12582912 | tf_op jit(solution)/shard_map/all_to_all | solution.py:223
  1060.6 560.0 %all-gather.33.cloned.1.call-start = ((), (), s32[]{:S(2)}) async-start(), calls=%async_computation.22 | async-start | bytes 4866048 | tf_op jit(solution)/shard_map/all_gather | solution.py:52
  1061.4 570.4 %all-gather.35.cloned.1.call-start = ((), (), s32[]{:S(2)}) async-start(), calls=%async_computation.23 | async-start | bytes 4866048 | tf_op jit(solution)/shard_map/all_gather | solution.py:53
  1216.6 18.8 collective-permute-start.2
  1219.2 16.2 collective-permute-start.3
  1588.5 26.0 all-to-all-start.3
  1592.9 1390.3 %reduce-scatter.13.cloned.1.call-start = ((), (), s32[]{:S(2)}) async-start(), calls=%async_computation.24 | async-start | bytes 2433024 | tf_op jit(solution)/shard_map/reduce_scatter | solution.py:379
  1687.2 1296.0 %reduce-scatter.15.cloned.1.call-start = ((), (), s32[]{:S(2)}) async-start(), calls=%async_computation.25 | async-start | bytes 9732096 | tf_op jit(solution)/shard_map/reduce_scatter | solution.py:380
  1702.6 26.0 all-to-all-start.4
  1707.0 1276.3 %reduce-scatter.17.cloned.1.call-start = ((), (), s32[]{:S(2)}) async-start(), calls=%async_computation.26 | async-start | bytes 9732096 | tf_op jit(solution)/shard_map/reduce_scatter | solution.py:381
  1720.8 1284.1 %reduce-scatter.21.cloned.1.call-start = ((), (), s32[]{:S(2)}) async-start(), calls=%async_computation.28 | async-start | bytes 2433024
  2566.5 41.9 %collective-permute-start.4 = (bf16[2,2048,192]{1,2,0:T(8,128)(2,1)}, bf16[2,2048,192]{1,2,0:T(8,128)(2,1)}, u32[]{:S(2)}, u32[]{:S(2)}) collective-permute-start(bf16[2,2048,192]{1,2,0:T(8,128)(2,1)} %get-tuple-element.805), channel_id=1, source_target_pairs={{0,1},{1,2},{2,3},{3,4},{4,5},{5,6},{6,7},{8,9},{9,10},{10,11},{11... | collective-permute-start | bytes 4718600 | tf_op jit(solution)/shard_map/ppermute | solution.py:37
  2597.3 45.1 %collective-permute-start.5 = (bf16[2,2048,192]{1,2,0:T(8,128)(2,1)}, bf16[2,2048,192]{1,2,0:T(8,128)(2,1)}, u32[]{:S(2)}, u32[]{:S(2)}) collective-permute-start(bf16[2,2048,192]{1,2,0:T(8,128)(2,1)} %get-tuple-element.804), channel_id=1, source_target_pairs={{1,0},{2,1},{3,2},{4,3},{5,4},{6,5},{7,6},{9,8},{10,9},{11,10},{12... | collective-permute-start | bytes 4718600 | tf_op jit(solution)/shard_map/ppermute | solution.py:37
  2873.6 235.2 %reduce-scatter.19.cloned.1.call-start = ((), (), s32[]{:S(2)}) async-start(), calls=%async_computation.27 | async-start | bytes 2433024
  2882.8 330.6 %reduce-scatter.23.cloned.1.call-start = ((), (), s32[]{:S(2)}) async-start(), calls=%async_computation.29 | async-start | bytes 2433024
  2892.5 81.9 %copy-start.31 = (bf16[1,1024,4,192]{1,3,2,0:T(8,128)(2,1)S(1)}, bf16[1,1024,4,192]{1,3,2,0:T(8,128)(2,1)}, u32[]{:S(2)}) copy-start(bf16[1,1024,4,192]{1,3,2,0:T(8,128)(2,1)} %copy-done.30) | copy-start | bytes 4718596
  2979.6 233.8 %copy-start.1 = (s32[12,512,3]{1,2,0:T(4,128)S(1)}, s32[12,512,3]{1,2,0:T(4,128)}, u32[]{:S(2)}) copy-start(s32[12,512,3]{1,2,0:T(4,128)} %param.47) | copy-start | bytes 221188
  (157 other events, 744.2 us)
Sparse Core Ops, SparseCore 0:
  10.9 56.9 all-gather.14
  70.9 53.0 all-gather.12
  126.9 52.9 all-gather.16
  182.6 86.1 all-gather.18
  271.6 127.3 all-gather.20
  401.7 62.4 all-gather.22
  829.7 96.8 all-gather.26
  929.6 53.1 all-gather.24
  985.6 52.9 all-gather.28
  1041.4 86.0 all-gather.30
  1130.4 127.1 all-gather.32
  1260.4 62.4 all-gather.34
  1687.3 141.9 reduce-scatter.12
  1836.7 134.3 reduce-scatter.14
  1977.4 134.9 reduce-scatter.16
  2873.7 131.1 reduce-scatter.20
  3010.6 98.1 reduce-scatter.18
  3115.4 97.9 reduce-scatter.22
where the time goes:
time: 3240 us; the launch traced here: 3220 us
  local copies, waits for them, and re-layouts  1020 us (31%)
  waiting for transfers between devices  834 us (26%)
  matrix products  717 us (22%)
  blocking collectives  380 us (12%)
  other arithmetic  177 us (5%)
  starting transfers between devices  64.6 us (2%)
    all_to_all x2, waiting for transfers between devices, forward_pass(): lax.all_to_all(jnp.stack([queries, key_rows, value_rows]), 'head', split_...  290 us
    unnamed x21, waiting for transfers between devices  237 us
    unnamed x3, blocking collectives  198 us
    all_to_all x1, blocking collectives, backward_pass(): lax.all_to_all(grad_stack, 'head', split_axis=1, concat_axis=2, tiled=True)  182 us
    dot_general x24, matrix products, masked_scores(): jnp.einsum('nqhd,nhjtd->nhqjt', query_blocks, key_tiles, preferred_elemen...  145 us
    dot_general x48, matrix products, pick_tiles(): jnp.einsum('nhte,hef->nhtf', selector, flat_table, preferred_element_type...  143 us
    reshape x24, local copies, waits for them, and re-layouts, masked_scores(): return scores.reshape(scores.shape[0], scores.shape[1], scores.shape[2], -1)  137 us
    reshape x24, local copies, waits for them, and re-layouts, pick_tiles(): picked.astype(tile_table.dtype)  114 us
  transfers between devices with their start and end apart: 29, of which 15 were waited for; matrix products, arithmetic and copies ran while one was open for 55% of the time, Pallas kernels for 0%

commit v1 on v0

v1 whole, which is shorter than its diff:
```python
from functools import partial

import jax
import jax.numpy as jnp
from jax import lax
from jax.experimental import pallas as pl
from jax.experimental.pallas import tpu as pltpu
from jax.sharding import PartitionSpec as P

HEAD_DIM = 64
BLOCK = 64
RANDOM = 3
TILES = 5 + RANDOM
REACH = 2
GROUP = 4

epsilon = 1e-06
masked_value = -1e30
query_scale = 0.125
far_away = -(1 << 24)
f32, bf16 = jnp.float32, jnp.bfloat16


def mm(a, b):
    return jnp.dot(a, b, preferred_element_type=f32)


def mm_nt(a, b):
    return lax.dot_general(a, b, (((1,), (1,)), ((), ())), preferred_element_type=f32)


def mm_tn(a, b):
    return lax.dot_general(a, b, (((0,), (0,)), ((), ())), preferred_element_type=f32)


def head_mask(rows, cols, first):
    lanes = lax.broadcasted_iota(jnp.int32, (rows, cols), 1)
    return (lanes >= first) & (lanes < first + HEAD_DIM)


def stacked_by_head(tile):
    rows, cols = tile.shape
    return jnp.concatenate(
        [
            jnp.where(head_mask(rows, cols, h * HEAD_DIM), tile, jnp.zeros_like(tile))
            for h in range(cols // HEAD_DIM)
        ],
        axis=0,
    )


def own_head_columns(stacked):
    cols = stacked.shape[1]
    total = None
    for h in range(cols // HEAD_DIM):
        part = stacked[h * BLOCK : (h + 1) * BLOCK]
        part = jnp.where(head_mask(BLOCK, cols, h * HEAD_DIM), part, 0.0)
        total = part if total is None else total + part
    return total


def block_rows(row):
    return pl.ds(pl.multiple_of(row * BLOCK, BLOCK), BLOCK)


def gathered(table_ref, fixed_row, random_row):
    tiles = [table_ref[block_rows(fixed_row(t)), :] for t in range(5)]
    low = head_mask(BLOCK, 2 * HEAD_DIM, 0)
    for t in range(RANDOM):
        halves = []
        for pair in range(GROUP // 2):
            cols = pl.ds(pair * 2 * HEAD_DIM, 2 * HEAD_DIM)
            a = table_ref[block_rows(random_row(2 * pair, t)), cols]
            b = table_ref[block_rows(random_row(2 * pair + 1, t)), cols]
            halves.append(jnp.where(low, a, b))
        tiles.append(jnp.concatenate(halves, axis=1))
    return jnp.concatenate(tiles, axis=0)


def row_readers(rows_ref, blocks):
    group, i = pl.program_id(0), pl.program_id(1)

    def fixed_row(t):
        return rows_ref[(group * GROUP * blocks + i) * TILES + t]

    def random_row(h, t):
        return rows_ref[((group * GROUP + h) * blocks + i) * TILES + 5 + t]

    return fixed_row, random_row


def attend_kernel(blocks, rows_ref, q_ref, k_ref, v_ref, base_ref, doc_ref, out_ref, p_ref):
    fixed_row, random_row = row_readers(rows_ref, blocks)
    keys = gathered(k_ref, fixed_row, random_row)
    values = gathered(v_ref, fixed_row, random_row)
    scores = mm_nt(keys, stacked_by_head(q_ref[...]))
    lo = doc_ref[0, 0:1, :]
    hi = doc_ref[0, 1:2, :]
    within = lax.broadcasted_iota(jnp.int32, (BLOCK, GROUP * BLOCK), 0)
    masked = []
    for t in range(TILES):
        place = within + base_ref[0, 0, t : t + 1, :]
        allowed = (place >= lo) & (place < hi)
        masked.append(jnp.where(allowed, scores[t * BLOCK : (t + 1) * BLOCK], masked_value))
    scores = jnp.concatenate(masked, axis=0)
    raised = jnp.exp(scores - jnp.max(scores, axis=0, keepdims=True))
    probs = (raised * (1.0 / jnp.sum(raised, axis=0, keepdims=True))).astype(bf16)
    p_ref[0, 0] = probs
    out_ref[...] = own_head_columns(mm_tn(probs, values)).astype(bf16)


def attend_back_kernel(
    blocks,
    rows_ref,
    q_ref,
    g_ref,
    k_ref,
    v_ref,
    p_ref,
    dq_ref,
    dk_ref,
    dv_ref,
    dk_sum,
    dv_sum,
):
    i = pl.program_id(1)

    @pl.when(i == 0)
    def _():
        dk_sum[...] = jnp.zeros_like(dk_sum)
        dv_sum[...] = jnp.zeros_like(dv_sum)

    fixed_row, random_row = row_readers(rows_ref, blocks)
    keys = gathered(k_ref, fixed_row, random_row)
    values = gathered(v_ref, fixed_row, random_row)
    queries = stacked_by_head(q_ref[...])
    grads = stacked_by_head(g_ref[...])
    probs = p_ref[0, 0]
    grad_probs = mm_nt(values, grads)
    wide = probs.astype(f32)
    balance = jnp.sum(wide * grad_probs, axis=0, keepdims=True)
    grad_scores = (wide * (grad_probs - balance)).astype(bf16)
    dq_ref[...] = (query_scale * own_head_columns(mm_tn(grad_scores, keys))).astype(bf16)
    grad_keys = mm(grad_scores, queries)
    grad_values = mm(probs, grads)
    for total, part in ((dk_sum, grad_keys), (dv_sum, grad_values)):
        for t in range(5):
            total[block_rows(fixed_row(t)), :] += part[t * BLOCK : (t + 1) * BLOCK]
        for t in range(RANDOM):
            rows = part[(5 + t) * BLOCK : (6 + t) * BLOCK]
            for h in range(GROUP):
                first = (h // 2) * 2 * HEAD_DIM
                mine = head_mask(BLOCK, 2 * HEAD_DIM, (h % 2) * HEAD_DIM)
                total[block_rows(random_row(h, t)), pl.ds(first, 2 * HEAD_DIM)] += jnp.where(
                    mine, rows[:, first : first + 2 * HEAD_DIM], 0.0
                )

    @pl.when(i == blocks - 1)
    def _():
        dk_ref[...] = dk_sum[...].astype(bf16)
        dv_ref[...] = dv_sum[...].astype(bf16)


def attend(rows, queries, keys, values, bases, docs):
    tokens, width = queries.shape
    ext = keys.shape[0]
    blocks, cols = tokens // BLOCK, GROUP * HEAD_DIM
    groups = width // cols
    tile = pl.BlockSpec((BLOCK, cols), lambda g, i, r: (i, g))
    table = pl.BlockSpec((ext, cols), lambda g, i, r: (0, g))
    return pl.pallas_call(
        partial(attend_kernel, blocks),
        grid_spec=pltpu.PrefetchScalarGridSpec(
            num_scalar_prefetch=1,
            grid=(groups, blocks),
            in_specs=[
                tile,
                table,
                table,
                pl.BlockSpec((1, 1, TILES, cols), lambda g, i, r: (g, i, 0, 0)),
                pl.BlockSpec((1, 8, cols), lambda g, i, r: (i, 0, 0)),
            ],
            out_specs=[
                tile,
                pl.BlockSpec((1, 1, TILES * BLOCK, cols), lambda g, i, r: (g, i, 0, 0)),
            ],
        ),
        out_shape=[
            jax.ShapeDtypeStruct((tokens, width), bf16),
            jax.ShapeDtypeStruct((groups, blocks, TILES * BLOCK, cols), bf16),
        ],
        compiler_params=pltpu.CompilerParams(vmem_limit_bytes=40 << 20),
        cost_estimate=pl.CostEstimate(
            flops=4 * groups * blocks * TILES * BLOCK * cols * cols,
            bytes_accessed=4 * ext * width + 2 * groups * blocks * TILES * BLOCK * cols,
            transcendentals=groups * blocks * TILES * BLOCK * cols,
        ),
    )(rows, queries, keys, values, bases, docs)


def attend_back(rows, queries, grads, keys, values, probs):
    tokens, width = queries.shape
    ext = keys.shape[0]
    blocks, cols = tokens // BLOCK, GROUP * HEAD_DIM
    groups = width // cols
    tile = pl.BlockSpec((BLOCK, cols), lambda g, i, r: (i, g))
    table = pl.BlockSpec((ext, cols), lambda g, i, r: (0, g))
    return pl.pallas_call(
        partial(attend_back_kernel, blocks),
        grid_spec=pltpu.PrefetchScalarGridSpec(
            num_scalar_prefetch=1,
            grid=(groups, blocks),
            in_specs=[
                tile,
                tile,
                table,
                table,
                pl.BlockSpec((1, 1, TILES * BLOCK, cols), lambda g, i, r: (g, i, 0, 0)),
            ],
            out_specs=[tile, table, table],
            scratch_shapes=[pltpu.VMEM((ext, cols), f32), pltpu.VMEM((ext, cols), f32)],
        ),
        out_shape=[
            jax.ShapeDtypeStruct((tokens, width), bf16),
            jax.ShapeDtypeStruct((ext, width), bf16),
            jax.ShapeDtypeStruct((ext, width), bf16),
        ],
        compiler_params=pltpu.CompilerParams(vmem_limit_bytes=56 << 20),
        cost_estimate=pl.CostEstimate(
            flops=10 * groups * blocks * TILES * BLOCK * cols * cols,
            bytes_accessed=8 * ext * width + 2 * groups * blocks * TILES * BLOCK * cols,
            transcendentals=0,
        ),
    )(rows, queries, grads, keys, values, probs)


def tile_plan(segment_ids, random_blocks, tokens):
    heads, total_blocks, _ = random_blocks.shape
    blocks = tokens // BLOCK
    chunk = lax.axis_index("blk") * lax.axis_size("head") + lax.axis_index("head")
    margin = REACH * tokens
    padded = jnp.concatenate(
        [
            jnp.full((margin,), -1, jnp.int32),
            segment_ids,
            jnp.full((margin,), jnp.iinfo(jnp.int32).max, jnp.int32),
        ]
    )
    near = lax.dynamic_slice_in_dim(padded, chunk * tokens, tokens + 2 * margin)
    own = near[margin : margin + tokens]
    begins = jnp.sum((near[None, :] < own[:, None]).astype(jnp.int32), axis=1)
    ends = jnp.sum((near[None, :] <= own[:, None]).astype(jnp.int32), axis=1)
    docs = jnp.stack([begins, ends]).reshape(2, blocks, BLOCK)
    docs = jnp.tile(jnp.transpose(docs, (1, 0, 2)), (1, 4, GROUP))
    first = begins[::BLOCK] // BLOCK
    here = REACH * blocks + jnp.arange(blocks, dtype=jnp.int32)
    fixed = jnp.stack([here - 1, here, here + 1, first, first + 1], axis=-1)
    picked = lax.dynamic_slice_in_dim(random_blocks, chunk * blocks, blocks, axis=1)
    picked = picked - (chunk - REACH) * blocks
    rows = jnp.concatenate(
        [jnp.broadcast_to(fixed[None], (heads, blocks, 5)), picked], axis=-1
    )
    earlier = jnp.arange(TILES)[None, :] < jnp.arange(TILES)[:, None]
    repeat = jnp.any((rows[..., :, None] == rows[..., None, :]) & earlier, axis=-1)
    bases = jnp.where(repeat, far_away, rows * BLOCK)
    rows = jnp.clip(rows, 0, (1 + 2 * REACH) * blocks - 1)
    bases = bases.reshape(heads // GROUP, GROUP, blocks, TILES)
    bases = jnp.repeat(jnp.transpose(bases, (0, 2, 3, 1)), BLOCK, axis=-1)
    return rows.reshape(-1), bases, docs


def side_pairs(blk, head, far):
    pairs = []
    for b in range(blk):
        for h in range(head):
            down = h < head // 2
            if far and h not in (0, head - 1):
                continue
            source = b - 1 if down else b + 1
            if 0 <= source < blk:
                pairs.append((h * blk + source, h * blk + b))
    return pairs


def widen(tokens_rows, blk, head):
    rows = tokens_rows.shape[0]
    h = lax.axis_index("head")
    line = lax.all_gather(tokens_rows, "head", axis=0, tiled=True)
    low = h < head // 2
    near = lax.dynamic_slice_in_dim(line, jnp.where(low, head - 1, 0) * rows, rows)
    far = lax.dynamic_slice_in_dim(line, jnp.where(low, head - 2, 1) * rows, rows)
    near = lax.ppermute(near, ("head", "blk"), side_pairs(blk, head, False))
    far = lax.ppermute(far, ("head", "blk"), side_pairs(blk, head, True))
    whole = jnp.concatenate([far, near, line, near, far], axis=0)
    return lax.dynamic_slice_in_dim(whole, h * rows, (1 + 2 * REACH) * rows)


def narrow(wide_rows, rows, blk, head):
    h = lax.axis_index("head")
    low = h < head // 2
    frame = jnp.zeros(((head + 2 * REACH) * rows, wide_rows.shape[1]), wide_rows.dtype)
    frame = lax.dynamic_update_slice_in_dim(frame, wide_rows, h * rows, 0)
    near = lax.dynamic_slice_in_dim(frame, jnp.where(low, 1, head + REACH) * rows, rows)
    far = lax.dynamic_slice_in_dim(frame, jnp.where(low, 0, head + REACH + 1) * rows, rows)
    back = [(t, s) for s, t in side_pairs(blk, head, False)]
    near = lax.ppermute(near, ("head", "blk"), back)
    back = [(t, s) for s, t in side_pairs(blk, head, True)]
    far = lax.ppermute(far, ("head", "blk"), back)
    line = frame[REACH * rows : (REACH + head) * rows].reshape(head, rows, -1)
    place = jnp.arange(head, dtype=jnp.int32)[:, None, None]
    line = line + jnp.where(place == jnp.where(low, head - 1, 0), near[None], 0)
    line = line + jnp.where(place == jnp.where(low, head - 2, 1), far[None], 0)
    return lax.psum_scatter(line.reshape(head * rows, -1), "head", scatter_dimension=0, tiled=True)


def layer_norm(values, gain_vec, offset):
    centred = values - jnp.mean(values, axis=-1, keepdims=True)
    spread = jnp.mean(centred * centred, axis=-1, keepdims=True)
    return centred * lax.rsqrt(spread + epsilon) * gain_vec + offset


def whole(shard):
    return lax.all_gather(shard, ("head", "blk"), axis=0, tiled=True)


def shared_out(grad):
    return lax.psum_scatter(grad.astype(bf16), ("head", "blk"), scatter_dimension=0, tiled=True).astype(f32)


def per_device(blk, head, tokens, *rest):
    weights, vectors, (out_grad, segment_ids, random_blocks) = rest[:6], rest[6:15], rest[15:]
    rows = tokens.shape[0]
    w_query, w_key, w_value, w_attn, w_inner, w_outer = [whole(w) for w in weights]
    sizes = [v.shape[0] for v in vectors]
    cuts = [sum(sizes[:n]) for n in range(len(sizes) + 1)]
    table = whole(jnp.concatenate(vectors)[None])
    (
        bias_query,
        bias_value,
        bias_attn,
        gain_one,
        offset_one,
        bias_inner,
        bias_outer,
        gain_two,
        offset_two,
    ) = [table[:, a:b].reshape(-1).astype(f32) for a, b in zip(cuts[:-1], cuts[1:])]

    rows_of, bases, docs = tile_plan(segment_ids, random_blocks, rows)
    wide = widen(tokens, blk, head)
    queries = (query_scale * (mm(tokens, w_query) + bias_query)).astype(bf16)
    keys = mm(wide, w_key).astype(bf16)
    values = (mm(wide, w_value) + bias_value).astype(bf16)
    attended, probs = attend(rows_of, queries, keys, values, bases, docs)

    first_norm, norm_one_back = jax.vjp(
        layer_norm, tokens.astype(f32) + mm(attended, w_attn) + bias_attn, gain_one, offset_one
    )
    first_low = first_norm.astype(bf16)
    inner = mm(first_low, w_inner) + bias_inner
    activated, gelu_back = jax.vjp(partial(jax.nn.gelu, approximate=True), inner)
    activ_low = activated.astype(bf16)
    outer = mm(activ_low, w_outer) + bias_outer
    result, norm_two_back = jax.vjp(layer_norm, first_norm + outer, gain_two, offset_two)

    grad_second, grad_gain_two, grad_offset_two = norm_two_back(out_grad.astype(f32))
    grad_outer = grad_second.astype(bf16)
    grad_inner = gelu_back(mm_nt(grad_outer, w_outer))[0].astype(bf16)
    grad_first = grad_second + mm_nt(grad_inner, w_inner)
    grad_first_sum, grad_gain_one, grad_offset_one = norm_one_back(grad_first)
    grad_attn = grad_first_sum.astype(bf16)
    grad_attended = mm_nt(grad_attn, w_attn).astype(bf16)
    grad_w_outer = shared_out(mm_tn(activ_low, grad_outer))
    grad_w_inner = shared_out(mm_tn(first_low, grad_inner))
    grad_w_attn = shared_out(mm_tn(attended, grad_attn))

    grad_scaled, grad_keyed, grad_valued = attend_back(
        rows_of, queries, grad_attended, keys, values, probs
    )
    grad_wide = mm_nt(grad_keyed, w_key) + mm_nt(grad_valued, w_value)
    grad_tokens = (
        grad_first_sum
        + mm_nt(grad_scaled, w_query)
        + narrow(grad_wide.astype(bf16), rows, blk, head).astype(f32)
    )
    grad_w_query = shared_out(mm_tn(tokens, grad_scaled))
    grad_w_key = shared_out(mm_tn(wide, grad_keyed))
    grad_w_value = shared_out(mm_tn(wide, grad_valued))

    def total(grads):
        return jnp.sum(grads.astype(f32), axis=0)

    sums = (
        total(grad_scaled),
        total(grad_valued),
        total(grad_attn),
        grad_gain_one,
        grad_offset_one,
        total(grad_inner),
        total(grad_outer),
        grad_gain_two,
        grad_offset_two,
    )
    packed = jnp.concatenate([s.reshape(blk * head, -1) for s in sums], axis=1)
    packed = lax.psum_scatter(packed, ("head", "blk"), scatter_dimension=0, tiled=True)
    vector_grads = tuple(packed[0, a:b] for a, b in zip(cuts[:-1], cuts[1:]))
    return (
        result.astype(bf16),
        grad_tokens,
        grad_w_query,
        grad_w_key,
        grad_w_value,
        grad_w_attn,
        grad_w_inner,
        grad_w_outer,
    ) + vector_grads


def solution(mesh):
    row = P(("blk", "head"), None)
    matrix = P(("head", "blk"), None)
    vector = P(("head", "blk"))
    return jax.shard_map(
        partial(per_device, mesh.shape["blk"], mesh.shape["head"]),
        mesh=mesh,
        in_specs=(row,) + (matrix,) * 6 + (vector,) * 9 + (row, P(), P()),
        out_specs=(row, row) + (matrix,) * 6 + (vector,) * 9,
        check_vma=False,
    )
```

time: 3240 us -> 1360 us (0.42)
  local copies, waits for them, and re-layouts: 1020 us -> 82.3 us
  matrix products: 717 us -> 167 us
  blocking collectives: 380 us -> 122 us
  other arithmetic: 177 us -> 34.5 us
  Pallas kernels: 0 us -> 104 us
  starting transfers between devices: 64.6 us -> 9.67 us
    dot_general x160 -> x18, matrix products: 717 us -> 167 us  [the longest x6 61.5 us: mm_nt(): lax.dot_general(a, b, (((1,), (1,)), ((), ())), preferred_element_type=f32)]
    reshape x101 -> x10, local copies, waits for them, and re-layouts: 547 us -> 1.17 us  [the longest x9 0.71 us: per_device(): packed = jnp.concatenate([s.reshape(blk * head, -1) for s in sums], axis=1)]
    reduce_scatter x3 -> x6, waiting for transfers between devices: 0.01 us -> 526 us  [the longest x5 416 us: shared_out(): lax.psum_scatter(grad.astype(bf16), ('head', 'blk'), scatter_dimension=0,...]
    all_to_all x5 -> x0, waiting for transfers between devices: 339 us -> none  [the longest x2 290 us: forward_pass(): lax.all_to_all(jnp.stack([queries, key_rows, value_rows]), 'head', split_...]
    unnamed x21 -> x15, waiting for transfers between devices: 237 us -> 4.45 us
    all_to_all x1 -> x0, blocking collectives: 182 us -> none  [backward_pass(): lax.all_to_all(grad_stack, 'head', split_axis=1, concat_axis=2, tiled=True)]
    pallas_call x0 -> x2, Pallas kernels: none -> 104 us  [the longest x1 59.9 us: attend_back(): pl.pallas_call(partial(attend_back_kernel, blocks), grid_spec=pltpu.Prefe...]
    add x11 -> x2, other arithmetic: 88.4 us -> 7.14 us  [the longest x1 7.14 us: narrow(): line = line + jnp.where(place == jnp.where(low, head - 2, 1), far[None], 0)]
  transfers between devices with their start and end apart: 29 -> 18, of which waited for: 15 -> 12; matrix products, arithmetic and copies ran while one was open for 55% -> 16% of each run, Pallas kernels for 0% -> 3%
where the time goes in v1:
time: 1360 us; the launch traced here: 1350 us
  waiting for transfers between devices  814 us (60%)
  matrix products  167 us (12%)
  blocking collectives  122 us (9%)
  Pallas kernels  104 us (8%)
  local copies, waits for them, and re-layouts  82.3 us (6%)
  other arithmetic  34.5 us (3%)
  between operations  15.2 us (1%)
    reduce_scatter x5, waiting for transfers between devices, shared_out(): lax.psum_scatter(grad.astype(bf16), ('head', 'blk'), scatter_dimension=0,...  416 us
    all_gather x6, waiting for transfers between devices, whole(): return lax.all_gather(shard, ('head', 'blk'), axis=0, tiled=True)  171 us
    unnamed x2, blocking collectives  122 us
    reduce_scatter x1, waiting for transfers between devices, narrow(): lax.psum_scatter(line.reshape(head * rows, -1), 'head', scatter_dimension...  110 us
    all_gather x1, waiting for transfers between devices, widen(): line = lax.all_gather(tokens_rows, 'head', axis=0, tiled=True)  110 us
    dot_general x6, matrix products, mm_nt(): lax.dot_general(a, b, (((1,), (1,)), ((), ())), preferred_element_type=f32)  61.5 us
    pallas_call x1, Pallas kernels, attend_back(): pl.pallas_call(partial(attend_back_kernel, blocks), grid_spec=pltpu.Prefe...  59.9 us
    unnamed x85, local copies, waits for them, and re-layouts  53.3 us
  transfers between devices with their start and end apart: 18, of which 12 were waited for; matrix products, arithmetic and copies ran while one was open for 16% of the time, Pallas kernels for 3%

profile of v1, /device:TPU:0, one launch (start us, length us, event | category | flops | bytes accessed | tf_op | source)
XLA Modules:
  0.0 1348.0 jit_solution(4944993471133078180)
XLA Ops:
  17.9 109.8 %all-gather.11.cloned.1.call-done = bf16[4096,768]{1,0:T(8,128)(2,1)} async-done(((bf16[1024,768]{1,0:T(8,128)(2,1)}), bf16[4096,768]{1,0:T(8,128)(2,1)}) %all-gather.11.cloned.1.call-update) | async-done | bytes 6291472 | tf_op jit(solution)/shard_map/all_gather | solution.py:288
  142.2 62.2 %all-reduce = bf16[9216]{0:T(1024)(128)(2,1)S(1)} all-reduce(bf16[9216]{0:T(1024)(128)(2,1)S(1)} %dynamic-update-slice), channel_id=2, replica_groups=mesh['head'=4,'blk'=8] {'head','blk'}, use_global_device_ids=true, to_apply=%add | all-reduce | flops 9216 | bytes 36864
  217.8 5.8 constant_dynamic-update-slice_fusion.2
  229.0 10.5 all-gather.13.cloned.1.call-done
  239.5 10.9 convolution_convert_fusion.k_ref
  250.3 44.9 %all-gather.15.cloned.1.call-done = bf16[768,768]{1,0:T(8,128)(2,1)} async-done(((bf16[24,768]{1,0:T(8,128)(2,1)}), bf16[768,768]{1,0:T(8,128)(2,1)}) %all-gather.15.cloned.1.call-update) | async-done | bytes 1179664 | tf_op jit(solution)/shard_map/all_gather | solution.py:323
  295.2 11.0 add_convert_fusion.1.v_ref
  306.3 43.7 %shard_map.314 = (bf16[1024,768]{1,0:T(8,128)(2,1)S(1)}, bf16[3,16,512,256]{3,2,1,0:T(8,128)(2,1)}) custom-call(s32[1536]{0:T(1024)S(1)} %min.12.rows_ref, bf16[1024,768]{1,0:T(8,128)(2,1)S(1)} %copy-done.2, bf16[5120,768]{1,0:T(8,128)(2,1)S(1)} %copy-done.1, bf16[5120,768]{1,0:T(8,128)(2,1)} %add_convert_fusion.1.v_ref, ...), custom_call_target="tpu_custom_call" | custom-call | flops 6442450944 | bytes 28311552 | tf_op jit(solution)/shard_map/pallas_call | solution.py:171
  356.7 59.8 %all-gather.19.cloned.1.call-done = bf16[768,3072]{1,0:T(8,128)(2,1)} async-done(((bf16[24,3072]{1,0:T(8,128)(2,1)}), bf16[768,3072]{1,0:T(8,128)(2,1)}) %all-gather.19.cloned.1.call-update) | async-done | bytes 4718608 | tf_op jit(solution)/shard_map/all_gather | solution.py:323
  416.6 11.1 fusion.38
  427.6 54.3 %all-gather.21.cloned.1.call-done = bf16[3072,768]{1,0:T(8,128)(2,1)} async-done(((bf16[96,768]{1,0:T(8,128)(2,1)}), bf16[3072,768]{1,0:T(8,128)(2,1)}) %all-gather.21.cloned.1.call-update) | async-done | bytes 4718608 | tf_op jit(solution)/shard_map/all_gather | solution.py:323
  482.0 11.8 fusion.43
  501.0 18.0 %convert_reduce_fusion.3 = (f32[3072]{0:T(1024)S(1)}, bf16[1024,3072]{1,0:T(8,128)(2,1)}) fusion(f32[1024,3072]{1,0:T(8,128)} %fusion.38, f32[3072]{0:T(1024)S(1)} %reshape.289, bf16[1024,768]{0,1:T(8,128)(2,1)S(1)} %get-tuple-element.106, bf16[3072,768]{1,0:T(8,128)(2,1)} %all-gather.21.cloned.1.call-done), kind=kOutput, calls=%fused_computation.14 | convolution fusion | flops 4904186880 | bytes 25190400 | tf_op jit(solution)/shard_map/dot_general | solution.py:29
  519.0 9.0 multiply_reduce_fusion
  533.8 59.9 %shard_map.315 = (bf16[1024,768]{1,0:T(8,128)(2,1)}, bf16[5120,768]{1,0:T(8,128)(2,1)}, bf16[5120,768]{1,0:T(8,128)(2,1)}) custom-call(s32[1536]{0:T(1024)} %copy-done, bf16[1024,768]{1,0:T(8,128)(2,1)} %multiply_convert_fusion.1.q_ref, bf16[1024,768]{1,0:T(8,128)(2,1)} %convolution_convert_fusion.3.g_ref, bf16[5120,768]{1,0:T(8,128)(2,1)} %convolution_convert_fusion.k_ref, ...), custom_call_target="tpu_custom_call" | custom-call | flops 16106127360 | bytes 44040192 | tf_op jit(solution)/shard_map/pallas_call | solution.py:208
  602.5 11.9 fusion.20
  614.5 12.1 fusion.23
  626.6 9.8 convolution_convert_fusion.2
  637.8 13.2 convolution_convert_fusion.1
  652.3 12.4 fusion.44
  664.7 6.2 broadcast_in_dim.118
  670.9 14.2 %fusion.7 = bf16[8192,768]{0,1:T(8,128)(2,1)} fusion(bf16[8192,768]{0,1:T(8,128)(2,1)} %broadcast_in_dim.118, s32[]{:T(128)S(6)} %select_n.63, f32[5120,768]{0,1:T(8,128)} %fusion.44, bf16[5120,768]{1,0:T(8,128)(2,1)} %get-tuple-element.26, bf16[768,768]{1,0:T(8,128)(2,1)S(1)} %copy-done.27), kind=kOutput, calls=%fused_computation.17 | convolution fusion | flops 6047662080 | bytes 32636932 | tf_op jit(solution)/shard_map/dot_general | solution.py:29
  697.1 7.1 copy.94
  708.6 9.7 copy.96
  718.4 7.1 fusion.8
  735.4 60.2 %all-reduce.1 = f32[32,288]{1,0:T(8,128)S(1)} all-reduce(f32[32,288]{1,0:T(8,128)S(1)} %concatenate.27), channel_id=10, replica_groups=mesh['head'=4,'blk'=8] {'head','blk'}, use_global_device_ids=true, to_apply=%region_27.28.clone | all-reduce | flops 9216 | bytes 73728
  799.9 95.9 %reduce-scatter.12.cloned.1.call-done = bf16[24,768]{1,0:T(8,128)(2,1)} async-done(((bf16[768,768]{1,0:T(8,128)(2,1)}), bf16[24,768]{1,0:T(8,128)(2,1)}) %reduce-scatter.12.cloned.1.call-update) | async-done | bytes 36880 | tf_op jit(solution)/shard_map/reduce_scatter | solution.py:327
  897.2 99.0 %reduce-scatter.14.cloned.1.call-done = bf16[24,768]{1,0:T(8,128)(2,1)} async-done(((bf16[768,768]{1,0:T(8,128)(2,1)}), bf16[24,768]{1,0:T(8,128)(2,1)}) %reduce-scatter.14.cloned.1.call-update) | async-done | bytes 36880 | tf_op jit(solution)/shard_map/reduce_scatter | solution.py:327
  997.6 110.0 %reduce-scatter.18.cloned.1.call-done = bf16[24,3072]{1,0:T(8,128)(2,1)} async-done(((bf16[768,3072]{1,0:T(8,128)(2,1)}), bf16[24,3072]{1,0:T(8,128)(2,1)}) %reduce-scatter.18.cloned.1.call-update) | async-done | bytes 147472 | tf_op jit(solution)/shard_map/reduce_scatter | solution.py:327
  1109.3 110.9 %reduce-scatter.20.cloned.1.call-done = bf16[96,768]{1,0:T(8,128)(2,1)} async-done(((bf16[3072,768]{1,0:T(8,128)(2,1)}), bf16[96,768]{1,0:T(8,128)(2,1)}) %reduce-scatter.20.cloned.1.call-update) | async-done | bytes 147472 | tf_op jit(solution)/shard_map/reduce_scatter | solution.py:327
  1221.8 110.4 %reduce-scatter.10.cloned.1.call-done = bf16[1024,768]{0,1:T(8,128)(2,1)} async-done(((bf16[4096,768]{0,1:T(8,128)(2,1)}), bf16[1024,768]{0,1:T(8,128)(2,1)}) %reduce-scatter.10.cloned.1.call-update) | async-done | bytes 1572880 | tf_op jit(solution)/shard_map/reduce_scatter | solution.py:313
  1332.2 5.3 convert_add_fusion
  (211 shorter events, 114.8 us)
Async XLA Ops:
  7.2 120.5 %all-gather.11.cloned.1.call-start = ((), (), s32[]{:S(2)}) async-start(), calls=%async_computation.8 | async-start | bytes 7864320 | tf_op jit(solution)/shard_map/all_gather | solution.py:288
  7.9 200.6 %all-gather.9.cloned.1.call-start = ((), (), s32[]{:S(2)}) async-start(), calls=%async_computation.7 | async-start | bytes 1216512 | tf_op jit(solution)/shard_map/all_gather | solution.py:323
  8.7 230.8 %all-gather.13.cloned.1.call-start = ((), (), s32[]{:S(2)}) async-start(), calls=%async_computation.9 | async-start | bytes 1216512 | tf_op jit(solution)/shard_map/all_gather | solution.py:323
  9.4 285.8 %all-gather.15.cloned.1.call-start = ((), (), s32[]{:S(2)}) async-start(), calls=%async_computation.10 | async-start | bytes 1216512 | tf_op jit(solution)/shard_map/all_gather | solution.py:323
  10.0 341.2 %all-gather.17.cloned.1.call-start = ((), (), s32[]{:S(2)}) async-start(), calls=%async_computation.11 | async-start | bytes 1216512 | tf_op jit(solution)/shard_map/all_gather | solution.py:323
  10.6 406.0 %all-gather.19.cloned.1.call-start = ((), (), s32[]{:S(2)}) async-start(), calls=%async_computation.12 | async-start | bytes 4866048 | tf_op jit(solution)/shard_map/all_gather | solution.py:323
  11.1 470.8 %all-gather.21.cloned.1.call-start = ((), (), s32[]{:S(2)}) async-start(), calls=%async_computation.13 | async-start | bytes 4866048 | tf_op jit(solution)/shard_map/all_gather | solution.py:323
  11.9 784.9 %reduce-scatter.22.cloned.1.call-start = ((), (), s32[]{:S(2)}) async-start(), calls=%async_computation.20 | async-start | bytes 1216512
  17.9 121.0 %copy-start.9 = (bf16[1024,768]{1,0:T(8,128)(2,1)S(1)}, bf16[1024,768]{1,0:T(8,128)(2,1)}, u32[]{:S(2)}) copy-start(bf16[1024,768]{1,0:T(8,128)(2,1)} %param.19) | copy-start | bytes 4718596
  131.5 80.9 %collective-permute-start = (bf16[1024,768]{1,0:T(8,128)(2,1)}, bf16[1024,768]{1,0:T(8,128)(2,1)}, u32[]{:S(2)}, u32[]{:S(2)}) collective-permute-start(bf16[1024,768]{1,0:T(8,128)(2,1)} %get-tuple-element.116), channel_id=1, source_target_pairs={{25,24},{0,1},{26,25},{1,2},{27,26},{2,3},{28,27},{3,4},{29,28},{4... | collective-permute-start | bytes 4718600 | tf_op jit(solution)/shard_map/ppermute | solution.py:293
  135.2 79.9 %collective-permute-start.1 = (bf16[1024,768]{1,0:T(8,128)(2,1)}, bf16[1024,768]{1,0:T(8,128)(2,1)}, u32[]{:S(2)}, u32[]{:S(2)}) collective-permute-start(bf16[1024,768]{1,0:T(8,128)(2,1)} %get-tuple-element.115), channel_id=1, source_target_pairs={{17,16},{25,24},{0,1},{8,9},{18,17},{26,25},{1,2},{9,10},{19,18},{... | collective-permute-start | bytes 4718600 | tf_op jit(solution)/shard_map/ppermute | solution.py:292
  204.8 101.4 %copy-start = (s32[1536]{0:T(1024)}, s32[1536]{0:T(1024)S(1)}, u32[]{:S(2)}) copy-start(s32[1536]{0:T(1024)S(1)} %min.12.rows_ref) | copy-start | bytes 18436
  295.2 11.0 copy-start.1
  295.2 11.0 copy-start.2
  427.6 66.2 %copy-start.6 = (bf16[1024,768]{0,1:T(8,128)(2,1)S(1)}, bf16[1024,768]{0,1:T(8,128)(2,1)}, u32[]{:S(2)}) copy-start(bf16[1024,768]{0,1:T(8,128)(2,1)} %copy.79) | copy-start | bytes 4718596
  497.7 21.3 %slice-start.3 = ((s8[4718592]{0:T(1024)(128)(4,1)}), s8[4194304]{0:T(1024)(128)(4,1)S(1)}, s32[]{:S(2)}) async-start(s8[4718592]{0:T(1024)(128)(4,1)} %bitcast.80), calls=%async_computation.24 | async-start | bytes 8388608
  501.0 18.0 %copy-start.12 = (bf16[1024,768]{0,1:T(8,128)(2,1)}, bf16[1024,768]{0,1:T(8,128)(2,1)S(1)}, u32[]{:S(2)}) copy-start(bf16[1024,768]{0,1:T(8,128)(2,1)S(1)} %get-tuple-element.106) | copy-start | bytes 4718596
  501.0 18.0 %copy-start.4 = (f32[1024,768]{0,1:T(8,128)S(1)}, f32[1024,768]{0,1:T(8,128)}, u32[]{:S(2)}) copy-start(f32[1024,768]{0,1:T(8,128)} %copy-done.3) | copy-start | bytes 9437188
  501.0 18.0 %slice-start.4 = ((s8[4718592]{0:T(1024)(128)(4,1)}), s8[524288]{0:T(1024)(128)(4,1)S(1)}, s32[]{:S(2)}) async-start(s8[4718592]{0:T(1024)(128)(4,1)} %bitcast.80), calls=%async_computation.25 | async-start | bytes 1048576
  533.8 59.9 %copy-start.10 = (bf16[1024,768]{1,0:T(8,128)(2,1)S(1)}, bf16[1024,768]{1,0:T(8,128)(2,1)}, u32[]{:S(2)}) copy-start(bf16[1024,768]{1,0:T(8,128)(2,1)} %param.19) | copy-start | bytes 4718596
  599.9 198.6 %reduce-scatter.16.cloned.1.call-start = ((), (), s32[]{:S(2)}) async-start(), calls=%async_computation.17 | async-start | bytes 1216512 | tf_op jit(solution)/shard_map/reduce_scatter | solution.py:327
  602.5 293.3 %reduce-scatter.12.cloned.1.call-start = ((), (), s32[]{:S(2)}) async-start(), calls=%async_computation.15 | async-start | bytes 1216512 | tf_op jit(solution)/shard_map/reduce_scatter | solution.py:327
  614.4 381.8 %reduce-scatter.14.cloned.1.call-start = ((), (), s32[]{:S(2)}) async-start(), calls=%async_computation.16 | async-start | bytes 1216512 | tf_op jit(solution)/shard_map/reduce_scatter | solution.py:327
  614.5 12.1 copy-start.5
  626.6 481.1 %reduce-scatter.18.cloned.1.call-start = ((), (), s32[]{:S(2)}) async-start(), calls=%async_computation.18 | async-start | bytes 4866048 | tf_op jit(solution)/shard_map/reduce_scatter | solution.py:327
  636.4 583.7 %reduce-scatter.20.cloned.1.call-start = ((), (), s32[]{:S(2)}) async-start(), calls=%async_computation.19 | async-start | bytes 4866048 | tf_op jit(solution)/shard_map/reduce_scatter | solution.py:327
  651.0 681.1 %reduce-scatter.10.cloned.1.call-start = ((), (), s32[]{:S(2)}) async-start(), calls=%async_computation.14 | async-start | bytes 7864320 | tf_op jit(solution)/shard_map/reduce_scatter | solution.py:313
  687.2 5.3 collective-permute-start.2
  688.5 15.8 %collective-permute-start.3 = (bf16[1024,768]{0,1:T(8,128)(2,1)S(1)}, bf16[1024,768]{0,1:T(8,128)(2,1)S(1)}, u32[]{:S(2)}, u32[]{:S(2)}) collective-permute-start(bf16[1024,768]{0,1:T(8,128)(2,1)S(1)} %get-tuple-element.114), channel_id=1, source_target_pairs={{24,25},{1,0},{25,26},{2,1},{26,27},{3,2},{27,28},{4,3},{28,29},{5... | collective-permute-start | bytes 4718600 | tf_op jit(solution)/shard_map/ppermute | solution.py:308
  697.1 21.2 %slice-start = ((s8[12582912]{0:T(1024)(128)(4,1)}), s8[4194304]{0:T(1024)(128)(4,1)S(1)}, s32[]{:S(2)}) async-start(s8[12582912]{0:T(1024)(128)(4,1)} %bitcast.74), calls=%async_computation.21 | async-start | bytes 8388608
  697.1 21.2 %slice-start.1 = ((s8[12582912]{0:T(1024)(128)(4,1)}), s8[4194304]{0:T(1024)(128)(4,1)S(1)}, s32[]{:S(2)}) async-start(s8[12582912]{0:T(1024)(128)(4,1)} %bitcast.74), calls=%async_computation.22 | async-start | bytes 8388608
  731.8 600.4 %copy-start.8 = (f32[1024,768]{0,1:T(8,128)S(1)}, f32[1024,768]{0,1:T(8,128)}, u32[]{:S(2)}) copy-start(f32[1024,768]{0,1:T(8,128)} %copy-done.7) | copy-start | bytes 9437188
  (20 other events, 105.1 us)
Sparse Core Ops, SparseCore 0:
  9.6 118.0 all-gather.10
  130.6 52.7 all-gather.8
  186.3 53.1 all-gather.12
  242.2 52.9 all-gather.14
  298.0 53.2 all-gather.16
  354.0 62.5 all-gather.18
  419.5 62.4 all-gather.20
  600.0 95.1 reduce-scatter.21
  700.3 95.1 reduce-scatter.15
  800.5 95.2 reduce-scatter.11
  900.9 95.2 reduce-scatter.13
  1001.5 106.0 reduce-scatter.17
  1114.0 106.0 reduce-scatter.19
  1222.3 109.8 reduce-scatter.9

commit v2 on v1

--- a/solution.py
+++ b/solution.py
@@ -313,6 +313,572 @@
     return lax.psum_scatter(line.reshape(head * rows, -1), "head", scatter_dimension=0, tiled=True)
 
 
+LINE = 4
+CORES = 2
+PIECES = 4
+MESH = pl.DeviceIdType.MESH
+NEAR_SLOT = (1, 0, 4, 3)
+FAR_SLOT = (0, None, None, 4)
+
+
+def remote(source, target, send, recv, head, blk):
+    return pltpu.make_async_remote_copy(
+        src_ref=source,
+        dst_ref=target,
+        send_sem=send,
+        recv_sem=recv,
+        device_id=(head, blk),
+        device_id_type=MESH,
+    )
+
+
+def at_each_head(h, body):
+    for hh in range(LINE):
+        pl.when(h == hh)(partial(body, hh))
+
+
+def greet_plane_and_line(h, b, blk):
+    barrier = pltpu.get_barrier_semaphore()
+    for d in range(1, LINE):
+        pl.semaphore_signal(
+            barrier, inc=1, device_id=((h + d) % LINE, b), device_id_type=MESH
+        )
+    for d in range(1, blk):
+        pl.semaphore_signal(barrier, inc=1, device_id=(h, (b + d) % blk), device_id_type=MESH)
+    pl.semaphore_wait(barrier, LINE - 1 + blk - 1)
+
+
+def gather_kernel(blk, count, *refs):
+    x_ref, shards = refs[0], refs[1 : 1 + count]
+    wide, spill, fulls = refs[1 + count], refs[2 + count], refs[3 + count : 3 + 2 * count]
+    local, zs, zr, cs, cr, ss, sr, us, ur, ds, dr, ns, nr, fs, fr = refs[3 + 2 * count :]
+    h, b = lax.axis_index("head"), lax.axis_index("blk")
+    chips = blk // CORES
+    chip, core = b // CORES, b % CORES
+    sibling = chip * CORES + 1 - core
+    rows = x_ref.shape[0] // PIECES
+
+    def piece(ref, p):
+        return ref.at[pl.ds(p * rows, rows)]
+
+    def place(hh, j):
+        slot = 2 + j - hh
+        return wide.at[slot] if 0 <= slot < 5 else spill
+
+    def own(a):
+        return pltpu.make_async_copy(shards[a], fulls[a].at[h, b], local.at[a])
+
+    def along(a, d):
+        return remote(
+            shards[a], fulls[a].at[h, b], zs.at[a, d - 1], zr.at[a, d - 1], (h + d) % LINE, b
+        )
+
+    def along_arrives(a, d):
+        src = (h - d + LINE) % LINE
+        return remote(
+            shards[a], fulls[a].at[src, b], zs.at[a, d - 1], zr.at[a, d - 1], (h + d) % LINE, b
+        )
+
+    def over(a, e):
+        part = fulls[a].at[:, b]
+        there = ((chip + e) % chips) * CORES + core
+        return remote(part, part, cs.at[a, e - 1], cr.at[a, e - 1], h, there)
+
+    def over_arrives(a, e):
+        there = ((chip - e + chips) % chips) * CORES + core
+        part = fulls[a].at[:, there]
+        return remote(part, part, cs.at[a, e - 1], cr.at[a, e - 1], h, there)
+
+    def across(a, e):
+        part = fulls[a].at[:, ((chip - e + chips) % chips) * CORES + core]
+        return remote(part, part, ss.at[a, e], sr.at[a, e], h, sibling)
+
+    def across_arrives(a, e):
+        part = fulls[a].at[:, ((chip - e + chips) % chips) * CORES + 1 - core]
+        return remote(part, part, ss.at[a, e], sr.at[a, e], h, sibling)
+
+    def spread(a):
+        for d in range(1, LINE):
+            along_arrives(a, d).wait_recv()
+        own(a).wait()
+        for e in range(1, chips):
+            over(a, e).start()
+        across(a, 0).start()
+
+    def hand_over(a):
+        for e in range(1, chips):
+            over_arrives(a, e).wait_recv()
+            across(a, e).start()
+
+    def up(hh, j, p):
+        source = x_ref if j == hh else place(hh, j)
+        return remote(
+            piece(source, p), piece(place(hh + 1, j), p), us.at[j, p], ur.at[j, p], (h + 1) % LINE, b
+        )
+
+    def up_arrives(hh, j, p):
+        target = piece(place(hh, j), p)
+        return remote(target, target, us.at[j, p], ur.at[j, p], (h + 1) % LINE, b)
+
+    def down(hh, j, p):
+        source = x_ref if j == hh else place(hh, j)
+        return remote(
+            piece(source, p), piece(place(hh - 1, j), p), ds.at[j, p], dr.at[j, p], (h + 3) % LINE, b
+        )
+
+    def down_arrives(hh, j, p):
+        target = piece(place(hh, j), p)
+        return remote(target, target, ds.at[j, p], dr.at[j, p], (h + 3) % LINE, b)
+
+    def sides(hh, j):
+        near, far = (3, 2) if hh < 2 else (0, 1)
+        if j == near:
+            return [(NEAR_SLOT[hh], ns, nr)]
+        if j == far and FAR_SLOT[hh] is not None:
+            return [(FAR_SLOT[hh], fs, fr)]
+        return []
+
+    def side(hh, j, p, slot, send, recv):
+        target = (b + 1) % blk if hh < 2 else (b + blk - 1) % blk
+        return remote(
+            piece(place(hh, j), p), piece(wide.at[slot], p), send.at[p], recv.at[p], h, target
+        )
+
+    def sends_side(hh):
+        return b < blk - 1 if hh < 2 else b > 0
+
+    def gets_side(hh):
+        return b > 0 if hh < 2 else b < blk - 1
+
+    def side_slots(hh):
+        found = [(NEAR_SLOT[hh], ns, nr)]
+        if FAR_SLOT[hh] is not None:
+            found.append((FAR_SLOT[hh], fs, fr))
+        return found
+
+    def fill(n, slot):
+        return pltpu.make_async_copy(x_ref, wide.at[slot], local.at[count + 1 + n])
+
+    def own_rows():
+        return pltpu.make_async_copy(x_ref, wide.at[2], local.at[count])
+
+    def begin(hh):
+        for p in range(PIECES):
+            if hh < LINE - 1:
+                up(hh, hh, p).start()
+            if hh > 0:
+                down(hh, hh, p).start()
+
+        @pl.when(jnp.logical_not(gets_side(hh)))
+        def _():
+            for n, (slot, _, _) in enumerate(side_slots(hh)):
+                fill(n, slot).start()
+
+    def pass_on(distance, hh):
+        for p in range(PIECES):
+            for j, arrives, onward, ends in (
+                (hh - distance, up_arrives, up, hh == LINE - 1),
+                (hh + distance, down_arrives, down, hh == 0),
+            ):
+                if not 0 <= j < LINE:
+                    continue
+                arrives(hh, j, p).wait_recv()
+                if not ends:
+                    onward(hh, j, p).start()
+                for slot, send, recv in sides(hh, j):
+
+                    @pl.when(sends_side(hh))
+                    def _(slot=slot, send=send, recv=recv):
+                        side(hh, j, p, slot, send, recv).start()
+
+    def finish(hh):
+        for p in range(PIECES):
+            for j in range(LINE):
+                if j <= hh < LINE - 1:
+                    up(hh, j, p).wait_send()
+                if j >= hh > 0:
+                    down(hh, j, p).wait_send()
+
+        @pl.when(sends_side(hh))
+        def _():
+            for j in range(LINE):
+                for slot, send, recv in sides(hh, j):
+                    for p in range(PIECES):
+                        side(hh, j, p, slot, send, recv).wait_send()
+
+        @pl.when(gets_side(hh))
+        def _():
+            for slot, send, recv in side_slots(hh):
+                for p in range(PIECES):
+                    target = piece(wide.at[slot], p)
+                    remote(target, target, send.at[p], recv.at[p], h, (b + 1) % blk).wait_recv()
+
+        @pl.when(jnp.logical_not(gets_side(hh)))
+        def _():
+            for n, (slot, _, _) in enumerate(side_slots(hh)):
+                fill(n, slot).wait()
+
+    own_rows().start()
+    for a in range(count):
+        own(a).start()
+    greet_plane_and_line(h, b, blk)
+    for a in range(count):
+        for d in range(1, LINE):
+            along(a, d).start()
+    at_each_head(h, begin)
+    for a in range(count):
+        spread(a)
+    at_each_head(h, partial(pass_on, 1))
+    for a in range(count - 2):
+        hand_over(a)
+    at_each_head(h, partial(pass_on, 2))
+    hand_over(count - 2)
+    at_each_head(h, partial(pass_on, 3))
+    hand_over(count - 1)
+    for a in range(count):
+        for d in range(1, LINE):
+            along(a, d).wait_send()
+        for e in range(1, chips):
+            over(a, e).wait_send()
+        for e in range(chips):
+            across(a, e).wait_send()
+            across_arrives(a, e).wait_recv()
+    own_rows().wait()
+    at_each_head(h, finish)
+
+
+def gather(tokens, shards, blk):
+    rows, width = tokens.shape
+    count, chips = len(shards), blk // CORES
+    anywhere = pl.BlockSpec(memory_space=pl.ANY)
+    dma = pltpu.SemaphoreType.DMA
+    outs = pl.pallas_call(
+        partial(gather_kernel, blk, count),
+        out_shape=[
+            jax.ShapeDtypeStruct((5, rows, width), tokens.dtype),
+            jax.ShapeDtypeStruct((rows, width), tokens.dtype),
+        ]
+        + [jax.ShapeDtypeStruct((LINE, blk) + s.shape, s.dtype) for s in shards],
+        in_specs=[anywhere] * (1 + count),
+        out_specs=[anywhere] * (2 + count),
+        scratch_shapes=[dma((count + 3,))]
+        + [dma((count, LINE - 1))] * 2
+        + [dma((count, chips - 1))] * 2
+        + [dma((count, chips))] * 2
+        + [dma((LINE, PIECES))] * 4
+        + [dma((PIECES,))] * 4,
+        compiler_params=pltpu.CompilerParams(collective_id=0, has_side_effects=True),
+    )(tokens, *shards)
+    return outs[0], outs[2:]
+
+
+def reduce_kernel(blk, count, *refs):
+    dx_ref, grads = refs[0], refs[1 : 1 + count]
+    sum_ref, outs = refs[1 + count], refs[2 + count : 2 + 2 * count]
+    rest = refs[2 + 2 * count :]
+    held, from_core, from_chip, from_line = (rest[n * count : (n + 1) * count] for n in range(4))
+    line, arrived, aside = rest[4 * count : 4 * count + 3]
+    load, ss, sr, cs, cr, zs, zr, xl, us, ur, ds, dr, ns, nr, fs, fr = rest[4 * count + 3 :]
+    h, b = lax.axis_index("head"), lax.axis_index("blk")
+    chips = blk // CORES
+    chip, core = b // CORES, b % CORES
+    sibling = chip * CORES + 1 - core
+    rows = dx_ref.shape[1] // PIECES
+
+    def mine(a, k):
+        return pltpu.make_async_copy(grads[a].at[:, k * CORES + core], held[a].at[k], load.at[a, k])
+
+    def across(a, k):
+        return remote(
+            grads[a].at[:, k * CORES + 1 - core],
+            from_core[a].at[k],
+            ss.at[a, k],
+            sr.at[a, k],
+            h,
+            sibling,
+        )
+
+    def over(a, e):
+        k = (chip + e) % chips
+        return remote(
+            held[a].at[k],
+            from_chip[a].at[e - 1],
+            cs.at[a, e - 1],
+            cr.at[a, e - 1],
+            h,
+            k * CORES + core,
+        )
+
+    def along(a, d):
+        there = (h + d) % LINE
+        return remote(
+            held[a].at[chip, there],
+            from_line[a].at[d - 1],
+            zs.at[a, d - 1],
+            zr.at[a, d - 1],
+            there,
+            b,
+        )
+
+    def add_cores(a, k):
+        def one(n, carry):
+            held[a][k, n] = (held[a][k, n].astype(f32) + from_core[a][k, n].astype(f32)).astype(
+                held[a].dtype
+            )
+            return carry
+
+        lax.fori_loop(0, LINE, one, 0)
+
+    def to_chips(a):
+        for k in range(chips):
+            mine(a, k).wait()
+            across(a, k).wait_recv()
+        for e in range(1, chips):
+            add_cores(a, (chip + e) % chips)
+            over(a, e).start()
+        add_cores(a, chip)
+
+    def to_line(a):
+        for e in range(1, chips):
+            over(a, e).wait_recv()
+
+        def one(n, carry):
+            total = held[a][chip, n].astype(f32)
+            for e in range(1, chips):
+                total = total + from_chip[a][e - 1, n].astype(f32)
+            held[a][chip, n] = total.astype(held[a].dtype)
+            return carry
+
+        lax.fori_loop(0, LINE, one, 0)
+        for d in range(1, LINE):
+            along(a, d).start()
+
+    def to_owner(a):
+        for d in range(1, LINE):
+            along(a, d).wait_recv()
+        total = held[a][chip, h].astype(f32)
+        for d in range(1, LINE):
+            total = total + from_line[a][d - 1].astype(f32)
+        outs[a][...] = total
+
+    def part(p):
+        return pl.ds(p * rows, rows)
+
+    def piece(ref, p):
+        return ref.at[part(p)]
+
+    def add_rows(target, j, source, n, p):
+        def one(step, carry):
+            some = pl.ds(p * rows + step * 64, 64)
+            target[j, some] = (
+                target[j, some].astype(f32) + source[n, some].astype(f32)
+            ).astype(target.dtype)
+            return carry
+
+        lax.fori_loop(0, rows // 64, one, 0)
+
+    def slot_of(hh, j):
+        slot = 2 + j - hh
+        return slot if 0 <= slot < 5 else None
+
+    def fetch(hh, j):
+        return pltpu.make_async_copy(dx_ref.at[slot_of(hh, j)], line.at[j], xl.at[j])
+
+    def arrival(hh, j, upward):
+        return arrived.at[LINE if j == hh and not upward else j]
+
+    def up(hh, j, p):
+        return remote(
+            piece(line.at[j], p),
+            piece(arrival(hh + 1, j, True), p),
+            us.at[j, p],
+            ur.at[j, p],
+            (h + 1) % LINE,
+            b,
+        )
+
+    def up_arrives(hh, j, p):
+        here = piece(arrival(hh, j, True), p)
+        return remote(here, here, us.at[j, p], ur.at[j, p], (h + 1) % LINE, b)
+
+    def down(hh, j, p):
+        return remote(
+            piece(line.at[j], p),
+            piece(arrival(hh - 1, j, False), p),
+            ds.at[j, p],
+            dr.at[j, p],
+            (h + 3) % LINE,
+            b,
+        )
+
+    def down_arrives(hh, j, p):
+        here = piece(arrival(hh, j, False), p)
+        return remote(here, here, ds.at[j, p], dr.at[j, p], (h + 3) % LINE, b)
+
+    def side_parts(hh):
+        near, far = (3, 2) if hh < 2 else (0, 1)
+        found = [(NEAR_SLOT[hh], near, 0, ns, nr)]
+        if FAR_SLOT[hh] is not None:
+            found.append((FAR_SLOT[hh], far, 1, fs, fr))
+        return found
+
+    def side(hh, slot, n, send, recv, p):
+        target = (b + blk - 1) % blk if hh < 2 else (b + 1) % blk
+        return remote(
+            piece(dx_ref.at[slot], p), piece(aside.at[n], p), send.at[p], recv.at[p], h, target
+        )
+
+    def sends_side(hh):
+        return b > 0 if hh < 2 else b < blk - 1
+
+    def gets_side(hh):
+        return b < blk - 1 if hh < 2 else b > 0
+
+    def begin(hh):
+        @pl.when(sends_side(hh))
+        def _():
+            for p in range(PIECES):
+                for slot, _, n, send, recv in side_parts(hh):
+                    side(hh, slot, n, send, recv, p).start()
+
+        for j in range(LINE):
+            if slot_of(hh, j) is not None:
+                fetch(hh, j).start()
+        for j in range(LINE):
+            if slot_of(hh, j) is not None:
+                fetch(hh, j).wait()
+            else:
+                line[j] = jnp.zeros(line.shape[1:], line.dtype)
+        for p in range(PIECES):
+            if hh == 0:
+                up(hh, 1, p).start()
+            if hh == LINE - 1:
+                down(hh, 2, p).start()
+
+    def take_sides(hh):
+        for p in range(PIECES):
+            for _, j, n, send, recv in side_parts(hh):
+
+                @pl.when(gets_side(hh))
+                def _(j=j, n=n, send=send, recv=recv):
+                    here = piece(aside.at[n], p)
+                    remote(here, here, send.at[p], recv.at[p], h, (b + 1) % blk).wait_recv()
+                    add_rows(line, j, aside, n, p)
+
+                if hh == 0:
+                    up(hh, j, p).start()
+                if hh == LINE - 1:
+                    down(hh, j, p).start()
+
+    def pass_on(first, hh):
+        if hh == 1:
+            moves = [(3, True), (0, False)] if first else [(2, True)]
+        elif hh == 2:
+            moves = [(0, False), (3, True)] if first else [(1, False)]
+        else:
+            moves = []
+        for p in range(PIECES):
+            for j, upward in moves:
+                (up_arrives if upward else down_arrives)(hh, j, p).wait_recv()
+                add_rows(line, j, arrived, j, p)
+                (up if upward else down)(hh, j, p).start()
+
+    def finish(hh):
+        for p in range(PIECES):
+            sources = []
+            if hh > 0:
+                up_arrives(hh, hh, p).wait_recv()
+                sources.append(hh)
+            if hh < LINE - 1:
+                down_arrives(hh, hh, p).wait_recv()
+                sources.append(LINE)
+
+            def one(step, carry, p=p, sources=tuple(sources)):
+                some = pl.ds(p * rows + step * 64, 64)
+                total = line[hh, some].astype(f32)
+                for n in sources:
+                    total = total + arrived[n, some].astype(f32)
+                sum_ref[some] = total
+                return carry
+
+            lax.fori_loop(0, rows // 64, one, 0)
+        for p in range(PIECES):
+            for j in range(LINE):
+                if j > hh:
+                    up(hh, j, p).wait_send()
+                if j < hh:
+                    down(hh, j, p).wait_send()
+
+        @pl.when(sends_side(hh))
+        def _():
+            for p in range(PIECES):
+                for slot, _, n, send, recv in side_parts(hh):
+                    side(hh, slot, n, send, recv, p).wait_send()
+
+    for a in range(count):
+        for k in range(chips):
+            mine(a, k).start()
+    greet_plane_and_line(h, b, blk)
+    for a in range(count):
+        for k in range(chips):
+            across(a, k).start()
+    at_each_head(h, begin)
+    for a in range(count):
+        to_chips(a)
+    at_each_head(h, take_sides)
+    at_each_head(h, partial(pass_on, True))
+    for a in range(count // 2):
+        to_line(a)
+    at_each_head(h, partial(pass_on, False))
+    for a in range(count // 2, count):
+        to_line(a)
+    at_each_head(h, finish)
+    for a in range(count):
+        to_owner(a)
+    for a in range(count):
+        for k in range(chips):
+            across(a, k).wait_send()
+        for e in range(1, chips):
+            over(a, e).wait_send()
+        for d in range(1, LINE):
+            along(a, d).wait_send()
+
+
+def reduce_to_owners(wide_grad, grads, blk):
+    _, rows, width = wide_grad.shape
+    count, chips = len(grads), blk // CORES
+    anywhere = pl.BlockSpec(memory_space=pl.ANY)
+    inside = pl.BlockSpec(memory_space=pltpu.VMEM)
+    dma = pltpu.SemaphoreType.DMA
+    shard = [g.shape[2:] for g in grads]
+    outs = pl.pallas_call(
+        partial(reduce_kernel, blk, count),
+        out_shape=[jax.ShapeDtypeStruct((rows, width), f32)]
+        + [jax.ShapeDtypeStruct(s, f32) for s in shard],
+        in_specs=[anywhere] * (1 + count),
+        out_specs=[inside] * (1 + count),
+        scratch_shapes=[pltpu.VMEM((chips, LINE) + s, g.dtype) for s, g in zip(shard, grads)]
+        + [pltpu.VMEM((chips, LINE) + s, g.dtype) for s, g in zip(shard, grads)]
+        + [pltpu.VMEM((chips - 1, LINE) + s, g.dtype) for s, g in zip(shard, grads)]
+        + [pltpu.VMEM((LINE - 1,) + s, g.dtype) for s, g in zip(shard, grads)]
+        + [
+            pltpu.VMEM((LINE, rows, width), bf16),
+            pltpu.VMEM((LINE + 1, rows, width), bf16),
+            pltpu.VMEM((2, rows, width), bf16),
+        ]
+        + [dma((count, chips))] * 3
+        + [dma((count, chips - 1))] * 2
+        + [dma((count, LINE - 1))] * 2
+        + [dma((LINE,))]
+        + [dma((LINE, PIECES))] * 4
+        + [dma((PIECES,))] * 4,
+        compiler_params=pltpu.CompilerParams(
+            collective_id=1, has_side_effects=True, vmem_limit_bytes=60 << 20
+        ),
+    )(wide_grad, *grads)
+    return outs[0], outs[1:]
+
+
 def layer_norm(values, gain_vec, offset):
     centred = values - jnp.mean(values, axis=-1, keepdims=True)
     spread = jnp.mean(centred * centred, axis=-1, keepdims=True)
@@ -327,13 +893,33 @@
     return lax.psum_scatter(grad.astype(bf16), ("head", "blk"), scatter_dimension=0, tiled=True).astype(f32)
 
 
+def vectors_of(table, sizes):
+    cuts = [sum(sizes[:n]) for n in range(len(sizes) + 1)]
+    return [table[..., a:b] for a, b in zip(cuts[:-1], cuts[1:])]
+
+
+def padded_to(flat, size):
+    return jnp.pad(flat, [(0, 0)] * (flat.ndim - 1) + [(0, size - flat.shape[-1])])
+
+
 def per_device(blk, head, tokens, *rest):
     weights, vectors, (out_grad, segment_ids, random_blocks) = rest[:6], rest[6:15], rest[15:]
     rows = tokens.shape[0]
-    w_query, w_key, w_value, w_attn, w_inner, w_outer = [whole(w) for w in weights]
+    by_kernel = head == LINE and blk == LINE * CORES
     sizes = [v.shape[0] for v in vectors]
-    cuts = [sum(sizes[:n]) for n in range(len(sizes) + 1)]
-    table = whole(jnp.concatenate(vectors)[None])
+    if by_kernel:
+        packed = padded_to(jnp.concatenate(vectors), 16 * 128).reshape(16, 128)
+        order = (0, 1, 2, 3, 4, 5)
+        wide, fulls = gather(tokens, [packed] + [weights[n] for n in order], blk)
+        wide = wide.reshape(-1, tokens.shape[1])
+        w_query, w_key, w_value, w_attn, w_inner, w_outer = [
+            w.reshape(-1, w.shape[-1]) for w in fulls[1:]
+        ]
+        table = fulls[0].reshape(head * blk, -1)
+    else:
+        wide = widen(tokens, blk, head)
+        w_query, w_key, w_value, w_attn, w_inner, w_outer = [whole(w) for w in weights]
+        table = whole(jnp.concatenate(vectors)[None])
     (
         bias_query,
         bias_value,
@@ -344,10 +930,9 @@
         bias_outer,
         gain_two,
         offset_two,
-    ) = [table[:, a:b].reshape(-1).astype(f32) for a, b in zip(cuts[:-1], cuts[1:])]
+    ) = [v.reshape(-1).astype(f32) for v in vectors_of(table, sizes)]
 
     rows_of, bases, docs = tile_plan(segment_ids, random_blocks, rows)
-    wide = widen(tokens, blk, head)
     queries = (query_scale * (mm(tokens, w_query) + bias_query)).astype(bf16)
     keys = mm(wide, w_key).astype(bf16)
     values = (mm(wide, w_value) + bias_value).astype(bf16)
@@ -370,23 +955,9 @@
     grad_first_sum, grad_gain_one, grad_offset_one = norm_one_back(grad_first)
     grad_attn = grad_first_sum.astype(bf16)
     grad_attended = mm_nt(grad_attn, w_attn).astype(bf16)
-    grad_w_outer = shared_out(mm_tn(activ_low, grad_outer))
-    grad_w_inner = shared_out(mm_tn(first_low, grad_inner))
-    grad_w_attn = shared_out(mm_tn(attended, grad_attn))
-
     grad_scaled, grad_keyed, grad_valued = attend_back(
         rows_of, queries, grad_attended, keys, values, probs
     )
-    grad_wide = mm_nt(grad_keyed, w_key) + mm_nt(grad_valued, w_value)
-    grad_tokens = (
-        grad_first_sum
-        + mm_nt(grad_scaled, w_query)
-        + narrow(grad_wide.astype(bf16), rows, blk, head).astype(f32)
-    )
-    grad_w_query = shared_out(mm_tn(tokens, grad_scaled))
-    grad_w_key = shared_out(mm_tn(wide, grad_keyed))
-    grad_w_value = shared_out(mm_tn(wide, grad_valued))
-
     def total(grads):
         return jnp.sum(grads.astype(f32), axis=0)
 
@@ -402,18 +973,33 @@
         grad_offset_two,
     )
     packed = jnp.concatenate([s.reshape(blk * head, -1) for s in sums], axis=1)
-    packed = lax.psum_scatter(packed, ("head", "blk"), scatter_dimension=0, tiled=True)
-    vector_grads = tuple(packed[0, a:b] for a, b in zip(cuts[:-1], cuts[1:]))
+    grad_wide = (mm_nt(grad_keyed, w_key) + mm_nt(grad_valued, w_value)).astype(bf16)
+    grad_rows = grad_first_sum + mm_nt(grad_scaled, w_query)
+    matrix_grads = [
+        mm_tn(tokens, grad_scaled).astype(bf16),
+        mm_tn(wide, grad_keyed).astype(bf16),
+        mm_tn(wide, grad_valued).astype(bf16),
+        mm_tn(attended, grad_attn).astype(bf16),
+        mm_tn(first_low, grad_inner).astype(bf16),
+        mm_tn(activ_low, grad_outer).astype(bf16),
+    ]
+    if by_kernel:
+        shares = [g.reshape(head, blk, -1, g.shape[-1]) for g in matrix_grads]
+        small = padded_to(packed, 8 * 128).reshape(head, blk, 8, 128)
+        wide_sum, sums = reduce_to_owners(
+            grad_wide.reshape(-1, rows, grad_wide.shape[-1]), [small] + shares, blk
+        )
+        matrix_grads = list(sums[1:])
+        packed = sums[0].reshape(-1)
+    else:
+        wide_sum = narrow(grad_wide, rows, blk, head).astype(f32)
+        matrix_grads = [shared_out(g) for g in matrix_grads]
+        packed = lax.psum_scatter(packed, ("head", "blk"), scatter_dimension=0, tiled=True)[0]
     return (
-        result.astype(bf16),
-        grad_tokens,
-        grad_w_query,
-        grad_w_key,
-        grad_w_value,
-        grad_w_attn,
-        grad_w_inner,
-        grad_w_outer,
-    ) + vector_grads
+        (result.astype(bf16), grad_rows + wide_sum)
+        + tuple(matrix_grads)
+        + tuple(vectors_of(packed, sizes))
+    )
 
 
 def solution(mesh):

time: 1360 us -> 653 us (0.48)
  waiting for transfers between devices: 814 us -> 0 us
  Pallas kernels: 104 us -> 456 us
  blocking collectives: 122 us -> 0 us
  local copies, waits for them, and re-layouts: 82.3 us -> 22.4 us
  matrix products: 167 us -> 141 us
  between operations: 15.2 us -> 1.56 us
    reduce_scatter x6 -> x0, waiting for transfers between devices: 526 us -> none  [the longest x5 416 us: shared_out(): lax.psum_scatter(grad.astype(bf16), ('head', 'blk'), scatter_dimension=0,...]
    pallas_call x0 -> x2, Pallas kernels: none -> 350 us  [the longest x1 190 us: reduce_to_owners(): pl.pallas_call(partial(reduce_kernel, blk, count), out_shape=[jax.ShapeDt...]
    all_gather x7 -> x0, waiting for transfers between devices: 281 us -> none  [the longest x6 171 us: whole(): return lax.all_gather(shard, ('head', 'blk'), axis=0, tiled=True)]
    unnamed x2 -> x0, blocking collectives: 122 us -> none
    unnamed x85 -> x77, local copies, waits for them, and re-layouts: 53.3 us -> 10.6 us
    broadcast_in_dim x4 -> x0, local copies, waits for them, and re-layouts: 15.1 us -> none  [the longest x1 6.19 us: narrow(): jnp.zeros(((head + 2 * REACH) * rows, wide_rows.shape[1]), wide_rows.dtype)]
  transfers between devices with their start and end apart: 18 -> 0, of which waited for: 12 -> 0; matrix products, arithmetic and copies ran while one was open for 16% -> 0% of each run, Pallas kernels for 3% -> 0%
where the time goes in v2:
time: 653 us; the launch traced here: 645 us
  Pallas kernels  456 us (70%)
  matrix products  141 us (22%)
  other arithmetic  23.5 us (4%)
  local copies, waits for them, and re-layouts  22.4 us (3%)
    pallas_call x1, Pallas kernels, reduce_to_owners(): pl.pallas_call(partial(reduce_kernel, blk, count), out_shape=[jax.ShapeDt...  190 us
    pallas_call x1, Pallas kernels, gather(): pl.pallas_call(partial(gather_kernel, blk, count), out_shape=[jax.ShapeDt...  160 us
    pallas_call x1, Pallas kernels, attend_back(): pl.pallas_call(partial(attend_back_kernel, blocks), grid_spec=pltpu.Prefe...  59.7 us
    dot_general x6, matrix products, mm_nt(): lax.dot_general(a, b, (((1,), (1,)), ((), ())), preferred_element_type=f32)  54.1 us
    dot_general x6, matrix products, mm_tn(): lax.dot_general(a, b, (((0,), (0,)), ((), ())), preferred_element_type=f32)  48.1 us
    pallas_call x1, Pallas kernels, attend(): pl.pallas_call(partial(attend_kernel, blocks), grid_spec=pltpu.PrefetchSc...  46.3 us
    dot_general x6, matrix products, mm(): return jnp.dot(a, b, preferred_element_type=f32)  38.8 us

profile of v2, /device:TPU:0, one launch (start us, length us, event | category | flops | bytes accessed | tf_op | source)
XLA Modules:
  0.0 644.5 jit_solution(12680557429650293056)
XLA Ops:
  0.7 6.1 concatenate.20
  8.1 4.2 convert_reduce_fusion
  16.0 159.6 %shard_map.314 = (bf16[5,1024,768]{2,1,0:T(8,128)(2,1)}, bf16[1024,768]{1,0:T(8,128)(2,1)}, bf16[4,8,16,128]{3,2,1,0:T(8,128)(2,1)}, bf16[4,8,24,768]{3,2,1,0:T(...) custom-call(bf16[1024,768]{1,0:T(8,128)(2,1)} %refs_0_.1, ...), custom_call_target="tpu_custom_call" | custom-call | tf_op jit(solution)/shard_map/pallas_call | solution.py:555
  177.5 3.3 fusion.12.q_ref
  181.8 8.4 %add_convert_fusion.1.v_ref = bf16[5120,768]{1,0:T(8,128)(2,1)} fusion(bf16[5120,768]{1,0:T(8,128)(2,1)S(1)} %bitcast.93, bf16[768,768]{1,0:T(8,128)(2,1)S(1)} %bitcast.103, f32[768]{0:T(1024)S(1)} %reshape.339), kind=kOutput, calls=%fused_computation.6 | convolution fusion | flops 6047662080 | bytes 16911360 | tf_op jit(solution)/shard_map/dot_general | solution.py:25
  190.2 6.7 %convolution_convert_fusion.k_ref = bf16[5120,768]{1,0:T(8,128)(2,1)S(1)} fusion(bf16[5120,768]{1,0:T(8,128)(2,1)S(1)} %bitcast.94, bf16[768,768]{1,0:T(8,128)(2,1)S(1)} %bitcast.105), kind=kOutput, calls=%fused_computation.16 | convolution fusion | flops 6043729920 | bytes 16908288 | tf_op jit(solution)/shard_map/dot_general | solution.py:25
  197.0 46.3 %shard_map.315 = (bf16[1024,768]{1,0:T(8,128)(2,1)S(1)}, bf16[3,16,512,256]{3,2,1,0:T(8,128)(2,1)}) custom-call(s32[1536]{0:T(1024)S(1)} %min.12.rows_ref, bf16[1024,768]{1,0:T(8,128)(2,1)S(1)} %fusion.12.q_ref, bf16[5120,768]{1,0:T(8,128)(2,1)S(1)} %convolution_convert_fusion.k_ref, bf16[5120,768]{1,0:T(8,128)(2,1)} %add_convert_fusion.1.v_ref, ...), custom_call_target="tpu_custom_call" | custom-call | flops 6442450944 | bytes 28311552 | tf_op jit(solution)/shard_map/pallas_call | solution.py:171
  243.3 1.5 fusion.25
  245.5 8.4 %fusion.20 = f32[1024,3072]{1,0:T(8,128)} fusion(bf16[768,3072]{1,0:T(8,128)(2,1)S(1)} %bitcast.98, f32[1024,768]{1,0:T(8,128)S(1)} %get-tuple-element.97, f32[768]{0:T(1024)S(1)} %reshape.342, f32[768]{0:T(1024)S(1)} %reshape.341, f32[1024]{0:T(1024)S(1)} %fusion.17, f32[1024]{0:T(1024)S(1)} %broadcast_multiply_fusion.1), kind=kOutput, calls=%fused_computation.96 | convolution fusion | flops 4835770368 | bytes 20461568 | tf_op jit(solution)/shard_map/dot_general | solution.py:25
  253.9 10.5 %fusion.26 = (f32[1024]{0:T(1024)S(1)}, f32[1024,768]{1,0:T(8,128)S(1)}) fusion(f32[768]{0:T(1024)S(1)} %reshape.344, bf16[3072,768]{1,0:T(8,128)(2,1)S(1)} %bitcast.102, f32[1024,3072]{1,0:T(8,128)} %fusion.20, f32[3072]{0:T(1024)S(1)} %reshape.343, f32[768]{0:T(1024)S(1)} %reshape.342, f32[768]{0:T(1024)S(1)} %reshape.341, f32[1024]{0:T(1024)S(1)} %fusion.17, ...), kind=kOutput, calls=%fused_computation.101 | convolution fusion | flops 4868799488 | bytes 23626752 | tf_op jit(solution)/shard_map/dot_general | solution.py:25
  265.0 2.0 copy-done.10
  267.0 1.2 fusion.10
  268.4 3.9 fusion.23
  272.3 1.7 copy-done.7
  274.4 14.7 %convert_reduce_fusion.3 = (f32[3072]{0:T(1024)S(1)}, bf16[1024,3072]{1,0:T(8,128)(2,1)S(1)}) fusion(f32[1024,3072]{1,0:T(8,128)} %fusion.20, f32[3072]{0:T(1024)S(1)} %reshape.343, bf16[1024,768]{1,0:T(8,128)(2,1)S(1)} %get-tuple-element.68, bf16[3072,768]{1,0:T(8,128)(2,1)} %bitcast.99), kind=kOutput, calls=%fused_computation.14 | convolution fusion | flops 4904186880 | bytes 25190400 | tf_op jit(solution)/shard_map/dot_general | solution.py:29
  289.2 12.8 %convolution_convert_fusion.1 = bf16[3072,768]{1,0:T(8,128)(2,1)} fusion(bf16[1024,768]{1,0:T(8,128)(2,1)S(1)} %get-tuple-element.68, f32[1024,3072]{1,0:T(8,128)} %fusion.20, f32[3072]{0:T(1024)S(1)} %reshape.343), kind=kOutput, calls=%fused_computation.17 | convolution fusion | flops 4865654784 | bytes 18886656 | tf_op jit(solution)/shard_map/dot_general | solution.py:33
  302.0 8.4 %multiply_reduce_fusion = (f32[768]{0:T(1024)S(1)}, f32[1024]{0:T(1024)S(1)}, f32[768]{0:T(1024)S(1)}, f32[1024,768]{1,0:T(8,128)S(1)}) fusion(f32[1024,768]{1,0:T(8,128)S(1)} %copy-done.6, f32[1024]{0:T(1024)S(1)} %fusion.17, f32[1024]{0:T(1024)S(1)} %broadcast_multiply_fusion.1, f32[768]{0:T(1024)S(1)} %reshape.341, ...), kind=kOutput, calls=%fused_computation.29 | convolution fusion | flops 4839699456 | bytes 20472832 | tf_op jit(solution)/shard_map/dot_general | solution.py:29
  310.4 2.5 fusion.22
  312.9 8.1 %convolution_convert_fusion.2 = bf16[768,3072]{1,0:T(8,128)(2,1)} fusion(bf16[1024,3072]{1,0:T(8,128)(2,1)S(1)} %get-tuple-element.102, f32[1024,768]{1,0:T(8,128)S(1)} %copy-done.6, f32[768]{0:T(1024)S(1)} %reshape.342, f32[768]{0:T(1024)S(1)} %reshape.341, f32[1024]{0:T(1024)S(1)} %fusion.17, f32[1024]{0:T(1024)S(1)} %broadcast_multiply_fusion.1), kind=kOutput, calls=%fused_computation.18 | convolution fusion | flops 4838129664 | bytes 14170112 | tf_op jit(solution)/shard_map/dot_general | solution.py:33
  321.3 2.2 convert_reduce_fusion.6
  323.5 2.5 convolution_convert_fusion.4
  326.1 3.8 convolution_convert_fusion.3.g_ref
  329.9 59.7 %shard_map.316 = (bf16[1024,768]{1,0:T(8,128)(2,1)}, bf16[5120,768]{1,0:T(8,128)(2,1)}, bf16[5120,768]{1,0:T(8,128)(2,1)}) custom-call(s32[1536]{0:T(1024)} %copy-done, bf16[1024,768]{1,0:T(8,128)(2,1)} %copy-done.2, bf16[1024,768]{1,0:T(8,128)(2,1)} %convolution_convert_fusion.3.g_ref, bf16[5120,768]{1,0:T(8,128)(2,1)} %copy-done.1, ...), custom_call_target="tpu_custom_call" | custom-call | flops 16106127360 | bytes 44040192 | tf_op jit(solution)/shard_map/pallas_call | solution.py:208
  389.6 1.7 convert_reduce_fusion.7
  391.3 4.4 convert_reduce_fusion.2
  396.6 12.4 %convolution_convert_fusion.6 = bf16[768,768]{1,0:T(8,128)(2,1)} fusion(bf16[5120,768]{1,0:T(8,128)(2,1)} %bitcast.91, bf16[5120,768]{1,0:T(8,128)(2,1)} %get-tuple-element.49), kind=kOutput, calls=%fused_computation.48 | convolution fusion | flops 6040387584 | bytes 16908288 | tf_op jit(solution)/shard_map/dot_general | solution.py:33
  409.1 9.7 %convolution_convert_fusion.5 = bf16[768,768]{1,0:T(8,128)(2,1)} fusion(bf16[5120,768]{1,0:T(8,128)(2,1)} %bitcast.92, bf16[5120,768]{1,0:T(8,128)(2,1)S(1)} %bitcast.74), kind=kOutput, calls=%fused_computation.47 | convolution fusion | flops 6040387584 | bytes 16908288 | tf_op jit(solution)/shard_map/dot_general | solution.py:33
  418.8 2.5 convolution_convert_fusion.7
  421.3 9.4 %fusion.27 = f32[5120,768]{1,0:T(8,128)} fusion(bf16[5120,768]{1,0:T(8,128)(2,1)S(1)} %bitcast.110, bf16[768,768]{1,0:T(8,128)(2,1)S(1)} %bitcast.106), kind=kOutput, calls=%fused_computation.102 | convolution fusion | flops 6039797760 | bytes 24772608 | tf_op jit(solution)/shard_map/dot_general | solution.py:29
  430.7 11.9 %add_convert_fusion = bf16[5120,768]{1,0:T(8,128)(2,1)} fusion(f32[5120,768]{1,0:T(8,128)} %fusion.27, bf16[5120,768]{1,0:T(8,128)(2,1)S(1)} %bitcast.74, bf16[768,768]{1,0:T(8,128)(2,1)S(1)} %bitcast.104), kind=kOutput, calls=%fused_computation.5 | convolution fusion | flops 6047662080 | bytes 32636928 | tf_op jit(solution)/shard_map/dot_general | solution.py:29
  442.6 190.5 %shard_map.317 = (f32[1024,768]{1,0:T(8,128)}, f32[8,128]{1,0:T(8,128)}, f32[24,768]{1,0:T(8,128)}, f32[24,768]{1,0:T(8,128)}, f32[24,768]{1,0:T(8,128)}, /*inde...) custom-call(bf16[5,1024,768]{2,1,0:T(8,128)(2,1)} %bitcast.75, f32[4,8,8,128]{3,2,1,0:T(8,128)} %copy.64, ...), custom_call_target="tpu_custom_call" | custom-call | tf_op jit(solution)/shard_map/pallas_call | solution.py:854
  633.2 5.9 add_add_fusion.2
  (142 shorter events, 16.1 us)
Async XLA Ops:
  14.3 182.6 %copy-start = (s32[1536]{0:T(1024)}, s32[1536]{0:T(1024)S(1)}, u32[]{:S(2)}) copy-start(s32[1536]{0:T(1024)S(1)} %min.12.rows_ref) | copy-start | bytes 18436
  177.5 4.1 copy-start.20
  177.5 4.3 copy-start.21
  181.8 15.1 %copy-start.2 = (bf16[1024,768]{1,0:T(8,128)(2,1)}, bf16[1024,768]{1,0:T(8,128)(2,1)S(1)}, u32[]{:S(2)}) copy-start(bf16[1024,768]{1,0:T(8,128)(2,1)S(1)} %fusion.12.q_ref) | copy-start | bytes 4718596
  181.8 8.4 %copy-start.23 = (bf16[4,8,24,768]{3,2,1,0:T(8,128)(2,1)S(1)}, bf16[4,8,24,768]{3,2,1,0:T(8,128)(2,1)}, u32[]{:S(2)}) copy-start(bf16[4,8,24,768]{3,2,1,0:T(8,128)(2,1)} %get-tuple-element.41) | copy-start | bytes 3538948
  196.9 46.3 %copy-start.1 = (bf16[5120,768]{1,0:T(8,128)(2,1)}, bf16[5120,768]{1,0:T(8,128)(2,1)S(1)}, u32[]{:S(2)}) copy-start(bf16[5120,768]{1,0:T(8,128)(2,1)S(1)} %convolution_convert_fusion.k_ref) | copy-start | bytes 23592964
  196.9 46.3 %copy-start.11 = (bf16[1024,768]{1,0:T(8,128)(2,1)S(1)}, bf16[1024,768]{1,0:T(8,128)(2,1)}, u32[]{:S(2)}) copy-start(bf16[1024,768]{1,0:T(8,128)(2,1)} %refs_0_.1) | copy-start | bytes 4718596
  196.9 46.3 %copy-start.25 = (bf16[4,8,24,768]{3,2,1,0:T(8,128)(2,1)S(1)}, bf16[4,8,24,768]{3,2,1,0:T(8,128)(2,1)}, u32[]{:S(2)}) copy-start(bf16[4,8,24,768]{3,2,1,0:T(8,128)(2,1)} %get-tuple-element.44) | copy-start | bytes 3538948
  243.2 2.3 slice-start.3
  244.8 9.1 %copy-start.5 = (f32[1024,768]{1,0:T(8,128)}, f32[1024,768]{1,0:T(8,128)S(1)}, u32[]{:S(2)}) copy-start(f32[1024,768]{1,0:T(8,128)S(1)} %get-tuple-element.97) | copy-start | bytes 9437188
  244.8 9.1 %slice-start.4 = ((s8[4718592]{0:T(1024)(128)(4,1)}), s8[4194304]{0:T(1024)(128)(4,1)S(1)}, s32[]{:S(2)}) async-start(s8[4718592]{0:T(1024)(128)(4,1)} %bitcast.100), calls=%async_computation.4 | async-start | bytes 8388608
  245.5 8.4 %slice-start.5 = ((s8[4718592]{0:T(1024)(128)(4,1)}), s8[524288]{0:T(1024)(128)(4,1)S(1)}, s32[]{:S(2)}) async-start(s8[4718592]{0:T(1024)(128)(4,1)} %bitcast.100), calls=%async_computation.5 | async-start | bytes 1048576
  264.5 3.7 copy-start.3
  264.5 2.5 copy-start.10
  289.1 12.8 %copy-start.6 = (f32[1024,768]{1,0:T(8,128)S(1)}, f32[1024,768]{1,0:T(8,128)}, u32[]{:S(2)}) copy-start(f32[1024,768]{1,0:T(8,128)} %copy-done.5) | copy-start | bytes 9437188
  289.2 12.8 %copy-start.8 = (f32[1024,768]{1,0:T(8,128)S(1)}, f32[1024,768]{1,0:T(8,128)}, u32[]{:S(2)}) copy-start(f32[1024,768]{1,0:T(8,128)} %copy-done.7) | copy-start | bytes 9437188
  395.9 13.1 %slice-start = ((s8[7864320]{0:T(1024)(128)(4,1)}), s8[4194304]{0:T(1024)(128)(4,1)S(1)}, s32[]{:S(2)}) async-start(s8[7864320]{0:T(1024)(128)(4,1)} %bitcast.73), calls=%async_computation | async-start | bytes 8388608
  396.6 12.4 %slice-start.1 = ((s8[7864320]{0:T(1024)(128)(4,1)}), s8[3670016]{0:T(1024)(128)(4,1)S(1)}, s32[]{:S(2)}) async-start(s8[7864320]{0:T(1024)(128)(4,1)} %bitcast.73), calls=%async_computation.1 | async-start | bytes 7340032
  396.6 24.7 %slice-start.6 = ((s8[7864320]{0:T(1024)(128)(4,1)}), s8[4194304]{0:T(1024)(128)(4,1)S(1)}, s32[]{:S(2)}) async-start(s8[7864320]{0:T(1024)(128)(4,1)} %bitcast.109), calls=%async_computation.6 | async-start | bytes 8388608
  409.0 9.7 %copy-start.9 = (bf16[1024,768]{1,0:T(8,128)(2,1)S(1)}, bf16[1024,768]{1,0:T(8,128)(2,1)}, u32[]{:S(2)}) copy-start(bf16[1024,768]{1,0:T(8,128)(2,1)} %get-tuple-element.48) | copy-start | bytes 4718596
  409.1 9.7 %copy-start.12 = (bf16[1024,768]{1,0:T(8,128)(2,1)S(1)}, bf16[1024,768]{1,0:T(8,128)(2,1)}, u32[]{:S(2)}) copy-start(bf16[1024,768]{1,0:T(8,128)(2,1)} %refs_0_.1) | copy-start | bytes 4718596
  409.1 12.2 %slice-start.7 = ((s8[7864320]{0:T(1024)(128)(4,1)}), s8[3670016]{0:T(1024)(128)(4,1)S(1)}, s32[]{:S(2)}) async-start(s8[7864320]{0:T(1024)(128)(4,1)} %bitcast.109), calls=%async_computation.7 | async-start | bytes 7340032
  418.8 2.6 copy-start.24
  421.3 9.4 %copy-start.22 = (bf16[4,8,24,768]{3,2,1,0:T(8,128)(2,1)S(1)}, bf16[4,8,24,768]{3,2,1,0:T(8,128)(2,1)}, u32[]{:S(2)}) copy-start(bf16[4,8,24,768]{3,2,1,0:T(8,128)(2,1)} %get-tuple-element.42) | copy-start | bytes 3538948
  442.6 190.5 %copy-start.4 = (f32[1024,768]{1,0:T(8,128)S(1)}, f32[1024,768]{1,0:T(8,128)}, u32[]{:S(2)}) copy-start(f32[1024,768]{1,0:T(8,128)} %get-tuple-element.72) | copy-start | bytes 9437188
  633.1 6.0 copy-start.19
  633.1 7.1 %copy-start.18 = (f32[24,768]{1,0:T(8,128)S(1)}, f32[24,768]{1,0:T(8,128)}, u32[]{:S(2)}) copy-start(f32[24,768]{1,0:T(8,128)} %get-tuple-element.124) | copy-start | bytes 221188
  633.1 7.8 %copy-start.17 = (f32[24,768]{1,0:T(8,128)S(1)}, f32[24,768]{1,0:T(8,128)}, u32[]{:S(2)}) copy-start(f32[24,768]{1,0:T(8,128)} %get-tuple-element.125) | copy-start | bytes 221188
  633.2 8.4 %copy-start.16 = (f32[24,768]{1,0:T(8,128)S(1)}, f32[24,768]{1,0:T(8,128)}, u32[]{:S(2)}) copy-start(f32[24,768]{1,0:T(8,128)} %get-tuple-element.126) | copy-start | bytes 221188
  633.2 9.0 %copy-start.15 = (f32[24,768]{1,0:T(8,128)S(1)}, f32[24,768]{1,0:T(8,128)}, u32[]{:S(2)}) copy-start(f32[24,768]{1,0:T(8,128)} %get-tuple-element.127) | copy-start | bytes 221188
  633.2 9.6 %copy-start.14 = (f32[24,3072]{1,0:T(8,128)S(1)}, f32[24,3072]{1,0:T(8,128)}, u32[]{:S(2)}) copy-start(f32[24,3072]{1,0:T(8,128)} %get-tuple-element.128) | copy-start | bytes 884740
  633.2 10.4 %copy-start.13 = (f32[96,768]{1,0:T(8,128)S(1)}, f32[96,768]{1,0:T(8,128)}, u32[]{:S(2)}) copy-start(f32[96,768]{1,0:T(8,128)} %get-tuple-element.129) | copy-start | bytes 884740
  (2 other events, 3.9 us)

commit v3 on v2

--- a/solution.py
+++ b/solution.py
@@ -13,10 +13,16 @@
 TILES = 5 + RANDOM
 REACH = 2
 GROUP = 4
+FORWARD_BLOCKS = 4
+BACKWARD_BLOCKS = 4
+ROWS = 256
+PIECE = 768
 
 epsilon = 1e-06
 masked_value = -1e30
 query_scale = 0.125
+gelu_scale = 0.7978845608028654
+gelu_cubic = 0.044715
 far_away = -(1 << 24)
 f32, bf16 = jnp.float32, jnp.bfloat16
 
@@ -77,8 +83,8 @@
     return jnp.concatenate(tiles, axis=0)
 
 
-def row_readers(rows_ref, blocks):
-    group, i = pl.program_id(0), pl.program_id(1)
+def row_readers(rows_ref, blocks, i):
+    group = pl.program_id(0)
 
     def fixed_row(t):
         return rows_ref[(group * GROUP * blocks + i) * TILES + t]
@@ -90,23 +96,25 @@
 
 
 def attend_kernel(blocks, rows_ref, q_ref, k_ref, v_ref, base_ref, doc_ref, out_ref, p_ref):
-    fixed_row, random_row = row_readers(rows_ref, blocks)
-    keys = gathered(k_ref, fixed_row, random_row)
-    values = gathered(v_ref, fixed_row, random_row)
-    scores = mm_nt(keys, stacked_by_head(q_ref[...]))
-    lo = doc_ref[0, 0:1, :]
-    hi = doc_ref[0, 1:2, :]
     within = lax.broadcasted_iota(jnp.int32, (BLOCK, GROUP * BLOCK), 0)
-    masked = []
-    for t in range(TILES):
-        place = within + base_ref[0, 0, t : t + 1, :]
-        allowed = (place >= lo) & (place < hi)
-        masked.append(jnp.where(allowed, scores[t * BLOCK : (t + 1) * BLOCK], masked_value))
-    scores = jnp.concatenate(masked, axis=0)
-    raised = jnp.exp(scores - jnp.max(scores, axis=0, keepdims=True))
-    probs = (raised * (1.0 / jnp.sum(raised, axis=0, keepdims=True))).astype(bf16)
-    p_ref[0, 0] = probs
-    out_ref[...] = own_head_columns(mm_tn(probs, values)).astype(bf16)
+    for u in range(FORWARD_BLOCKS):
+        here = pl.ds(u * BLOCK, BLOCK)
+        readers = row_readers(rows_ref, blocks, pl.program_id(1) * FORWARD_BLOCKS + u)
+        keys = gathered(k_ref, *readers)
+        values = gathered(v_ref, *readers)
+        scores = mm_nt(keys, stacked_by_head(q_ref[here, :]))
+        lo = doc_ref[u, 0:1, :]
+        hi = doc_ref[u, 1:2, :]
+        masked = []
+        for t in range(TILES):
+            place = within + base_ref[0, u, t : t + 1, :]
+            allowed = (place >= lo) & (place < hi)
+            masked.append(jnp.where(allowed, scores[t * BLOCK : (t + 1) * BLOCK], masked_value))
+        scores = jnp.concatenate(masked, axis=0)
+        raised = jnp.exp(scores - jnp.max(scores, axis=0, keepdims=True))
+        probs = (raised * (1.0 / jnp.sum(raised, axis=0, keepdims=True))).astype(bf16)
+        p_ref[0, u] = probs
+        out_ref[here, :] = own_head_columns(mm_tn(probs, values)).astype(bf16)
 
 
 def attend_back_kernel(
@@ -123,39 +131,42 @@
     dk_sum,
     dv_sum,
 ):
-    i = pl.program_id(1)
-
-    @pl.when(i == 0)
+    step = pl.program_id(1)
+
+    @pl.when(step == 0)
     def _():
         dk_sum[...] = jnp.zeros_like(dk_sum)
         dv_sum[...] = jnp.zeros_like(dv_sum)
 
-    fixed_row, random_row = row_readers(rows_ref, blocks)
-    keys = gathered(k_ref, fixed_row, random_row)
-    values = gathered(v_ref, fixed_row, random_row)
-    queries = stacked_by_head(q_ref[...])
-    grads = stacked_by_head(g_ref[...])
-    probs = p_ref[0, 0]
-    grad_probs = mm_nt(values, grads)
-    wide = probs.astype(f32)
-    balance = jnp.sum(wide * grad_probs, axis=0, keepdims=True)
-    grad_scores = (wide * (grad_probs - balance)).astype(bf16)
-    dq_ref[...] = (query_scale * own_head_columns(mm_tn(grad_scores, keys))).astype(bf16)
-    grad_keys = mm(grad_scores, queries)
-    grad_values = mm(probs, grads)
-    for total, part in ((dk_sum, grad_keys), (dv_sum, grad_values)):
-        for t in range(5):
-            total[block_rows(fixed_row(t)), :] += part[t * BLOCK : (t + 1) * BLOCK]
-        for t in range(RANDOM):
-            rows = part[(5 + t) * BLOCK : (6 + t) * BLOCK]
-            for h in range(GROUP):
-                first = (h // 2) * 2 * HEAD_DIM
-                mine = head_mask(BLOCK, 2 * HEAD_DIM, (h % 2) * HEAD_DIM)
-                total[block_rows(random_row(h, t)), pl.ds(first, 2 * HEAD_DIM)] += jnp.where(
-                    mine, rows[:, first : first + 2 * HEAD_DIM], 0.0
-                )
-
-    @pl.when(i == blocks - 1)
+    found = []
+    for u in range(BACKWARD_BLOCKS):
+        here = pl.ds(u * BLOCK, BLOCK)
+        readers = row_readers(rows_ref, blocks, step * BACKWARD_BLOCKS + u)
+        keys = gathered(k_ref, *readers)
+        values = gathered(v_ref, *readers)
+        queries = stacked_by_head(q_ref[here, :])
+        grads = stacked_by_head(g_ref[here, :])
+        probs = p_ref[0, u]
+        grad_probs = mm_nt(values, grads)
+        wide = probs.astype(f32)
+        balance = jnp.sum(wide * grad_probs, axis=0, keepdims=True)
+        grad_scores = (wide * (grad_probs - balance)).astype(bf16)
+        dq_ref[here, :] = (query_scale * own_head_columns(mm_tn(grad_scores, keys))).astype(bf16)
+        found.append((readers, mm(grad_scores, queries), mm(probs, grads)))
+    for (fixed_row, random_row), grad_keys, grad_values in found:
+        for total, part in ((dk_sum, grad_keys), (dv_sum, grad_values)):
+            for t in range(5):
+                total[block_rows(fixed_row(t)), :] += part[t * BLOCK : (t + 1) * BLOCK]
+            for t in range(RANDOM):
+                rows = part[(5 + t) * BLOCK : (6 + t) * BLOCK]
+                for h in range(GROUP):
+                    first = (h // 2) * 2 * HEAD_DIM
+                    mine = head_mask(BLOCK, 2 * HEAD_DIM, (h % 2) * HEAD_DIM)
+                    total[block_rows(random_row(h, t)), pl.ds(first, 2 * HEAD_DIM)] += jnp.where(
+                        mine, rows[:, first : first + 2 * HEAD_DIM], 0.0
+                    )
+
+    @pl.when(step == blocks // BACKWARD_BLOCKS - 1)
     def _():
         dk_ref[...] = dk_sum[...].astype(bf16)
         dv_ref[...] = dv_sum[...].astype(bf16)
@@ -164,25 +175,25 @@
 def attend(rows, queries, keys, values, bases, docs):
     tokens, width = queries.shape
     ext = keys.shape[0]
-    blocks, cols = tokens // BLOCK, GROUP * HEAD_DIM
+    blocks, cols, some = tokens // BLOCK, GROUP * HEAD_DIM, FORWARD_BLOCKS
     groups = width // cols
-    tile = pl.BlockSpec((BLOCK, cols), lambda g, i, r: (i, g))
+    tile = pl.BlockSpec((some * BLOCK, cols), lambda g, i, r: (i, g))
     table = pl.BlockSpec((ext, cols), lambda g, i, r: (0, g))
     return pl.pallas_call(
         partial(attend_kernel, blocks),
         grid_spec=pltpu.PrefetchScalarGridSpec(
             num_scalar_prefetch=1,
-            grid=(groups, blocks),
+            grid=(groups, blocks // some),
             in_specs=[
                 tile,
                 table,
                 table,
-                pl.BlockSpec((1, 1, TILES, cols), lambda g, i, r: (g, i, 0, 0)),
-                pl.BlockSpec((1, 8, cols), lambda g, i, r: (i, 0, 0)),
+                pl.BlockSpec((1, some, TILES, cols), lambda g, i, r: (g, i, 0, 0)),
+                pl.BlockSpec((some, 8, cols), lambda g, i, r: (i, 0, 0)),
             ],
             out_specs=[
                 tile,
-                pl.BlockSpec((1, 1, TILES * BLOCK, cols), lambda g, i, r: (g, i, 0, 0)),
+                pl.BlockSpec((1, some, TILES * BLOCK, cols), lambda g, i, r: (g, i, 0, 0)),
             ],
         ),
         out_shape=[
@@ -190,32 +201,28 @@
             jax.ShapeDtypeStruct((groups, blocks, TILES * BLOCK, cols), bf16),
         ],
         compiler_params=pltpu.CompilerParams(vmem_limit_bytes=40 << 20),
-        cost_estimate=pl.CostEstimate(
-            flops=4 * groups * blocks * TILES * BLOCK * cols * cols,
-            bytes_accessed=4 * ext * width + 2 * groups * blocks * TILES * BLOCK * cols,
-            transcendentals=groups * blocks * TILES * BLOCK * cols,
-        ),
+        name="attend",
     )(rows, queries, keys, values, bases, docs)
 
 
 def attend_back(rows, queries, grads, keys, values, probs):
     tokens, width = queries.shape
     ext = keys.shape[0]
-    blocks, cols = tokens // BLOCK, GROUP * HEAD_DIM
+    blocks, cols, some = tokens // BLOCK, GROUP * HEAD_DIM, BACKWARD_BLOCKS
     groups = width // cols
-    tile = pl.BlockSpec((BLOCK, cols), lambda g, i, r: (i, g))
+    tile = pl.BlockSpec((some * BLOCK, cols), lambda g, i, r: (i, g))
     table = pl.BlockSpec((ext, cols), lambda g, i, r: (0, g))
     return pl.pallas_call(
         partial(attend_back_kernel, blocks),
         grid_spec=pltpu.PrefetchScalarGridSpec(
             num_scalar_prefetch=1,
-            grid=(groups, blocks),
+            grid=(groups, blocks // some),
             in_specs=[
                 tile,
                 tile,
                 table,
                 table,
-                pl.BlockSpec((1, 1, TILES * BLOCK, cols), lambda g, i, r: (g, i, 0, 0)),
+                pl.BlockSpec((1, some, TILES * BLOCK, cols), lambda g, i, r: (g, i, 0, 0)),
             ],
             out_specs=[tile, table, table],
             scratch_shapes=[pltpu.VMEM((ext, cols), f32), pltpu.VMEM((ext, cols), f32)],
@@ -226,12 +233,197 @@
             jax.ShapeDtypeStruct((ext, width), bf16),
         ],
         compiler_params=pltpu.CompilerParams(vmem_limit_bytes=56 << 20),
-        cost_estimate=pl.CostEstimate(
-            flops=10 * groups * blocks * TILES * BLOCK * cols * cols,
-            bytes_accessed=8 * ext * width + 2 * groups * blocks * TILES * BLOCK * cols,
-            transcendentals=0,
-        ),
+        name="attend_back",
     )(rows, queries, grads, keys, values, probs)
+
+
+def normalized(values):
+    centred = values - jnp.mean(values, axis=-1, keepdims=True)
+    root = lax.rsqrt(jnp.mean(centred * centred, axis=-1, keepdims=True) + epsilon)
+    return centred * root, root
+
+
+def norm_back(grad, normal, root, gain):
+    scaled = grad * gain
+    along = jnp.mean(scaled * normal, axis=-1, keepdims=True)
+    return root * (scaled - jnp.mean(scaled, axis=-1, keepdims=True) - normal * along)
+
+
+def gelu_and_slope(u):
+    square = u * u
+    bend = jnp.tanh(gelu_scale * (u + gelu_cubic * (square * u)))
+    half = 0.5 * (1.0 + bend)
+    slope = half + (0.5 * gelu_scale) * u * (1.0 - bend * bend) * (
+        1.0 + (3.0 * gelu_cubic) * square
+    )
+    return u * half, slope
+
+
+def middle_kernel(
+    att_ref,
+    x_ref,
+    og_ref,
+    wa_ref,
+    wi_ref,
+    wo_ref,
+    vec_ref,
+    bi_ref,
+    res_ref,
+    sum_ref,
+    ga_ref,
+    dwa_ref,
+    dwi_ref,
+    dwo_ref,
+    dvec_ref,
+    dbi_ref,
+    normal,
+    root,
+    low,
+    act,
+    slope,
+    inner,
+):
+    step, half = pl.program_id(0), pl.num_programs(0) // 2
+    tokens, width = x_ref.shape
+    slices = [pl.ds(t * ROWS, ROWS) for t in range(tokens // ROWS)]
+    bias_attn, gain_one, offset_one, bias_outer, gain_two, offset_two = (
+        vec_ref[n : n + 1, :] for n in range(6)
+    )
+
+    def row_sum(total, values):
+        part = jnp.sum(values, axis=0, keepdims=True)
+        return part if total is None else total + part
+
+    @pl.when(step == 0)
+    def _():
+        for s in slices:
+            values = x_ref[s, :].astype(f32) + mm(att_ref[s, :], wa_ref[...]) + bias_attn
+            flat, scale = normalized(values)
+            normal[s, :] = flat
+            root[s, :] = jnp.broadcast_to(scale, (ROWS, 128))
+            first = flat * gain_one + offset_one
+            low[s, :] = first.astype(bf16)
+            sum_ref[s, :] = first + bias_outer
+
+    @pl.when(step < half)
+    def _():
+        for s in slices:
+            active, bend = gelu_and_slope(mm(low[s, :], wi_ref[...]) + bi_ref[0])
+            active = active.astype(bf16)
+            act[step, s, :] = active
+            slope[step, s, :] = bend.astype(bf16)
+            sum_ref[s, :] += mm(active, wo_ref[...])
+
+    @pl.when(step == half)
+    def _():
+        outer_sum, gain_sum, offset_sum = None, None, None
+        for s in slices:
+            flat, scale = normalized(sum_ref[s, :])
+            res_ref[s, :] = (flat * gain_two + offset_two).astype(bf16)
+            grad = og_ref[s, :].astype(f32)
+            gain_sum = row_sum(gain_sum, grad * flat)
+            offset_sum = row_sum(offset_sum, grad)
+            second = norm_back(grad, flat, scale, gain_two)
+            sum_ref[s, :] = second
+            second = second.astype(bf16)
+            ga_ref[s, :] = second
+            outer_sum = row_sum(outer_sum, second.astype(f32))
+        dvec_ref[3:4, :] = outer_sum
+        dvec_ref[4:5, :] = gain_sum
+        dvec_ref[5:6, :] = offset_sum
+        dvec_ref[6:8, :] = jnp.zeros((2, width), f32)
+
+    @pl.when(step >= half)
+    def _():
+        now = step - half
+        total = None
+        for s in slices:
+            grad = mm_nt(ga_ref[s, :], wo_ref[...]) * slope[now, s, :].astype(f32)
+            grad = grad.astype(bf16)
+            inner[s, :] = grad
+            total = row_sum(total, grad.astype(f32))
+            sum_ref[s, :] += mm_nt(grad, wi_ref[...])
+        dbi_ref[0] = total
+        for n in range(width // 256):
+            some = pl.ds(n * 256, 256)
+            dwi_ref[some, :] = mm_tn(low[:, some], inner[...]).astype(bf16)
+        for n in range(PIECE // 256):
+            some = pl.ds(n * 256, 256)
+            dwo_ref[some, :] = mm_tn(act[now, :, some], ga_ref[...]).astype(bf16)
+
+    @pl.when(step == 2 * half - 1)
+    def _():
+        attn_sum, gain_sum, offset_sum = None, None, None
+        for s in slices:
+            grad, flat = sum_ref[s, :], normal[s, :]
+            gain_sum = row_sum(gain_sum, grad * flat)
+            offset_sum = row_sum(offset_sum, grad)
+            grad = norm_back(grad, flat, root[s, 0:1], gain_one)
+            sum_ref[s, :] = grad
+            grad = grad.astype(bf16)
+            inner[s, :width] = grad
+            attn_sum = row_sum(attn_sum, grad.astype(f32))
+            ga_ref[s, :] = mm_nt(grad, wa_ref[...]).astype(bf16)
+        dvec_ref[0:1, :] = attn_sum
+        dvec_ref[1:2, :] = gain_sum
+        dvec_ref[2:3, :] = offset_sum
+        for n in range(width // 256):
+            some = pl.ds(n * 256, 256)
+            dwa_ref[some, :] = mm_tn(att_ref[:, some], inner[:, :width]).astype(bf16)
+
+
+def middle(attended, tokens, out_grad, w_attn, w_inner, w_outer, vectors, bias_inner):
+    rows, width = tokens.shape
+    steps = w_inner.shape[1] // PIECE
+    one = pl.Buffered(1)
+    still = pl.BlockSpec((rows, width), lambda i: (0, 0), pipeline_mode=one)
+    square = pl.BlockSpec((width, width), lambda i: (0, 0), pipeline_mode=one)
+    few = pl.BlockSpec((8, width), lambda i: (0, 0))
+    later = lambda i: jnp.maximum(i - steps, 0)
+    return pl.pallas_call(
+        middle_kernel,
+        grid=(2 * steps,),
+        in_specs=[
+            still,
+            still,
+            still,
+            square,
+            pl.BlockSpec((width, PIECE), lambda i: (0, i % steps)),
+            pl.BlockSpec((PIECE, width), lambda i: (i % steps, 0)),
+            few,
+            pl.BlockSpec((1, 1, PIECE), lambda i: (i % steps, 0, 0)),
+        ],
+        out_specs=[
+            still,
+            still,
+            still,
+            square,
+            pl.BlockSpec((width, PIECE), lambda i: (0, later(i))),
+            pl.BlockSpec((PIECE, width), lambda i: (later(i), 0)),
+            few,
+            pl.BlockSpec((1, 1, PIECE), lambda i: (later(i), 0, 0)),
+        ],
+        out_shape=[
+            jax.ShapeDtypeStruct((rows, width), bf16),
+            jax.ShapeDtypeStruct((rows, width), f32),
+            jax.ShapeDtypeStruct((rows, width), bf16),
+            jax.ShapeDtypeStruct(w_attn.shape, bf16),
+            jax.ShapeDtypeStruct(w_inner.shape, bf16),
+            jax.ShapeDtypeStruct(w_outer.shape, bf16),
+            jax.ShapeDtypeStruct((8, width), f32),
+            jax.ShapeDtypeStruct((steps, 1, PIECE), f32),
+        ],
+        scratch_shapes=[
+            pltpu.VMEM((rows, width), f32),
+            pltpu.VMEM((rows, 128), f32),
+            pltpu.VMEM((rows, width), bf16),
+            pltpu.VMEM((steps, rows, PIECE), bf16),
+            pltpu.VMEM((steps, rows, PIECE), bf16),
+            pltpu.VMEM((rows, PIECE), bf16),
+        ],
+        compiler_params=pltpu.CompilerParams(vmem_limit_bytes=60 << 20),
+        name="middle",
+    )(attended, tokens, out_grad, w_attn, w_inner, w_outer, vectors, bias_inner)
 
 
 def tile_plan(segment_ids, random_blocks, tokens):
@@ -827,10 +1019,8 @@
         to_chips(a)
     at_each_head(h, take_sides)
     at_each_head(h, partial(pass_on, True))
-    for a in range(count // 2):
-        to_line(a)
     at_each_head(h, partial(pass_on, False))
-    for a in range(count // 2, count):
+    for a in range(count):
         to_line(a)
     at_each_head(h, finish)
     for a in range(count):
@@ -879,12 +1069,6 @@
     return outs[0], outs[1:]
 
 
-def layer_norm(values, gain_vec, offset):
-    centred = values - jnp.mean(values, axis=-1, keepdims=True)
-    spread = jnp.mean(centred * centred, axis=-1, keepdims=True)
-    return centred * lax.rsqrt(spread + epsilon) * gain_vec + offset
-
-
 def whole(shard):
     return lax.all_gather(shard, ("head", "blk"), axis=0, tiled=True)
 
@@ -938,23 +1122,22 @@
     values = (mm(wide, w_value) + bias_value).astype(bf16)
     attended, probs = attend(rows_of, queries, keys, values, bases, docs)
 
-    first_norm, norm_one_back = jax.vjp(
-        layer_norm, tokens.astype(f32) + mm(attended, w_attn) + bias_attn, gain_one, offset_one
+    rows_vec = jnp.stack(
+        [bias_attn, gain_one, offset_one, bias_outer, gain_two, offset_two, gain_two, gain_two]
     )
-    first_low = first_norm.astype(bf16)
-    inner = mm(first_low, w_inner) + bias_inner
-    activated, gelu_back = jax.vjp(partial(jax.nn.gelu, approximate=True), inner)
-    activ_low = activated.astype(bf16)
-    outer = mm(activ_low, w_outer) + bias_outer
-    result, norm_two_back = jax.vjp(layer_norm, first_norm + outer, gain_two, offset_two)
-
-    grad_second, grad_gain_two, grad_offset_two = norm_two_back(out_grad.astype(f32))
-    grad_outer = grad_second.astype(bf16)
-    grad_inner = gelu_back(mm_nt(grad_outer, w_outer))[0].astype(bf16)
-    grad_first = grad_second + mm_nt(grad_inner, w_inner)
-    grad_first_sum, grad_gain_one, grad_offset_one = norm_one_back(grad_first)
-    grad_attn = grad_first_sum.astype(bf16)
-    grad_attended = mm_nt(grad_attn, w_attn).astype(bf16)
+    result, grad_first_sum, grad_attended, grad_w_attn, grad_w_inner, grad_w_outer, sums_d, sums_ff = (
+        middle(
+            attended,
+            tokens,
+            out_grad,
+            w_attn,
+            w_inner,
+            w_outer,
+            rows_vec,
+            bias_inner.reshape(-1, 1, PIECE),
+        )
+    )
+
     grad_scaled, grad_keyed, grad_valued = attend_back(
         rows_of, queries, grad_attended, keys, values, probs
     )
@@ -964,13 +1147,13 @@
     sums = (
         total(grad_scaled),
         total(grad_valued),
-        total(grad_attn),
-        grad_gain_one,
-        grad_offset_one,
-        total(grad_inner),
-        total(grad_outer),
-        grad_gain_two,
-        grad_offset_two,
+        sums_d[0],
+        sums_d[1],
+        sums_d[2],
+        sums_ff,
+        sums_d[3],
+        sums_d[4],
+        sums_d[5],
     )
     packed = jnp.concatenate([s.reshape(blk * head, -1) for s in sums], axis=1)
     grad_wide = (mm_nt(grad_keyed, w_key) + mm_nt(grad_valued, w_value)).astype(bf16)
@@ -979,9 +1162,9 @@
         mm_tn(tokens, grad_scaled).astype(bf16),
         mm_tn(wide, grad_keyed).astype(bf16),
         mm_tn(wide, grad_valued).astype(bf16),
-        mm_tn(attended, grad_attn).astype(bf16),
-        mm_tn(first_low, grad_inner).astype(bf16),
-        mm_tn(activ_low, grad_outer).astype(bf16),
+        grad_w_attn,
+        grad_w_inner,
+        grad_w_outer,
     ]
     if by_kernel:
         shares = [g.reshape(head, blk, -1, g.shape[-1]) for g in matrix_grads]
@@ -996,7 +1179,7 @@
         matrix_grads = [shared_out(g) for g in matrix_grads]
         packed = lax.psum_scatter(packed, ("head", "blk"), scatter_dimension=0, tiled=True)[0]
     return (
-        (result.astype(bf16), grad_rows + wide_sum)
+        (result, grad_rows + wide_sum)
         + tuple(matrix_grads)
         + tuple(vectors_of(packed, sizes))
     )

time: 653 us -> 582 us (0.89)
  matrix products: 141 us -> 69.7 us
  Pallas kernels: 456 us -> 472 us
  other arithmetic: 23.5 us -> 13 us
    pallas_call x0 -> x1, Pallas kernels: none -> 53 us  [middle(): pl.pallas_call(middle_kernel, grid=(2 * steps,), in_specs=[still, still,...]
    dot_general x6 -> x3, matrix products: 54.1 us -> 27.2 us  [mm_nt(): lax.dot_general(a, b, (((1,), (1,)), ((), ())), preferred_element_type=f32)]
    dot_general x6 -> x3, matrix products: 48.1 us -> 24.5 us  [mm_tn(): lax.dot_general(a, b, (((0,), (0,)), ((), ())), preferred_element_type=f32)]
    dot_general x6 -> x3, matrix products: 38.8 us -> 18 us  [mm(): return jnp.dot(a, b, preferred_element_type=f32)]
    pallas_call x1, Pallas kernels: 59.7 us -> 39.7 us  [attend_back(): pl.pallas_call(partial(attend_back_kernel, blocks), grid_spec=pltpu.Prefe...]
    pallas_call x1, Pallas kernels: 46.3 us -> 28.9 us  [attend(): pl.pallas_call(partial(attend_kernel, blocks), grid_spec=pltpu.PrefetchSc...]
    reduce_sum x5 -> x0, other arithmetic: 8.57 us -> none  [the longest x2 6.44 us: layer_norm(): centred = values - jnp.mean(values, axis=-1, keepdims=True)]
where the time goes in v3:
time: 582 us; the launch traced here: 576 us
  Pallas kernels  472 us (81%)
  matrix products  69.7 us (12%)
  local copies, waits for them, and re-layouts  20.5 us (4%)
  other arithmetic  13 us (2%)
    pallas_call x1, Pallas kernels, reduce_to_owners(): pl.pallas_call(partial(reduce_kernel, blk, count), out_shape=[jax.ShapeDt...  191 us
    pallas_call x1, Pallas kernels, gather(): pl.pallas_call(partial(gather_kernel, blk, count), out_shape=[jax.ShapeDt...  160 us
    pallas_call x1, Pallas kernels, middle(): pl.pallas_call(middle_kernel, grid=(2 * steps,), in_specs=[still, still,...  53 us
    pallas_call x1, Pallas kernels, attend_back(): pl.pallas_call(partial(attend_back_kernel, blocks), grid_spec=pltpu.Prefe...  39.7 us
    pallas_call x1, Pallas kernels, attend(): pl.pallas_call(partial(attend_kernel, blocks), grid_spec=pltpu.PrefetchSc...  28.9 us
    dot_general x3, matrix products, mm_nt(): lax.dot_general(a, b, (((1,), (1,)), ((), ())), preferred_element_type=f32)  27.2 us
    dot_general x3, matrix products, mm_tn(): lax.dot_general(a, b, (((0,), (0,)), ((), ())), preferred_element_type=f32)  24.5 us
    dot_general x3, matrix products, mm(): return jnp.dot(a, b, preferred_element_type=f32)  18 us

profile of v3, /device:TPU:0, one launch (start us, length us, event | category | flops | bytes accessed | tf_op | source)
XLA Modules:
  0.0 576.3 jit_solution(4825486992171667115)
XLA Ops:
  0.7 6.1 %concatenate.20 = bf16[288]{0:T(512)(128)(2,1)S(1)} concatenate(bf16[24]{0:T(256)(128)(2,1)} %param.26, bf16[24]{0:T(256)(128)(2,1)} %param.27, bf16[24]{0:T(256)(128)(2,1)} %param.28, bf16[24]{0:T(256)(128)(2,1)} %param.29, bf16[24]{0:T(256)(128)(2,1)} %param.30, bf16[96]{0:T(256)(128)(2,1)} %param.31, bf16[24]{0:T(256)(128)(2,1)} %param.32, bf16[24]{0:T(256)(128)(2,1)} %param.33, ...), dimensions={0} | concatenate | bytes 1152 | tf_op jit(solution)/shard_map/concatenate | solution.py:1095
  7.4 0.7 fusion.4
  8.1 4.2 convert_reduce_fusion
  12.8 0.8 dynamic-slice_subtract_fusion
  14.8 0.7 broadcast_in_dim.19
  16.0 159.6 %shard_map.314 = (bf16[5,1024,768]{2,1,0:T(8,128)(2,1)}, bf16[1024,768]{1,0:T(8,128)(2,1)}, bf16[4,8,16,128]{3,2,1,0:T(8,128)(2,1)}, bf16[4,8,24,768]{3,2,1,0:T(...) custom-call(bf16[1024,768]{1,0:T(8,128)(2,1)} %x_ref.1, ...), custom_call_target="tpu_custom_call" | custom-call | tf_op jit(solution)/shard_map/pallas_call | solution.py:747
  175.6 0.9 copy.57
  176.7 0.7 reshape.288.bi_ref
  178.8 2.8 fusion.q_ref
  181.7 0.8 copy-done.17
  182.7 8.5 %add_convert_fusion.1.v_ref = bf16[5120,768]{1,0:T(8,128)(2,1)} fusion(bf16[5120,768]{1,0:T(8,128)(2,1)S(1)} %bitcast.82, bf16[768,768]{1,0:T(8,128)(2,1)S(1)} %bitcast.86, f32[768]{0:T(1024)S(1)} %reshape.287), kind=kOutput, calls=%fused_computation.4 | convolution fusion | flops 6047662080 | bytes 16911360 | tf_op jit(solution)/shard_map/dot_general | solution.py:31
  191.2 6.7 %convolution_convert_fusion.k_ref = bf16[5120,768]{1,0:T(8,128)(2,1)S(1)} fusion(bf16[5120,768]{1,0:T(8,128)(2,1)S(1)} %bitcast.83, bf16[768,768]{1,0:T(8,128)(2,1)S(1)} %bitcast.88), kind=kOutput, calls=%fused_computation.5 | convolution fusion | flops 6043729920 | bytes 16908288 | tf_op jit(solution)/shard_map/dot_general | solution.py:31
  197.9 28.9 %attend.1 = (bf16[1024,768]{1,0:T(8,128)(2,1)S(1)}, bf16[3,16,512,256]{3,2,1,0:T(8,128)(2,1)}) custom-call(s32[1536]{0:T(1024)S(1)} %min.12.rows_ref, bf16[1024,768]{1,0:T(8,128)(2,1)S(1)} %fusion.q_ref, bf16[5120,768]{1,0:T(8,128)(2,1)S(1)} %convolution_convert_fusion.k_ref, bf16[5120,768]{1,0:T(8,128)(2,1)} %add_convert_fusion.1.v_ref, ...), custom_call_target="tpu_custom_call" | custom-call | tf_op jit(solution)/shard_map/attend/pallas_call | solution.py:182
  226.8 1.2 copy-done.2
  228.0 53.0 %middle.1 = (bf16[1024,768]{1,0:T(8,128)(2,1)}, f32[1024,768]{1,0:T(8,128)}, bf16[1024,768]{1,0:T(8,128)(2,1)}, bf16[768,768]{1,0:T(8,128)(2,1)}, bf16[768,3072]...) custom-call(bf16[1024,768]{1,0:T(8,128)(2,1)} %copy-done.2, ...), custom_call_target="tpu_custom_call" | custom-call | tf_op jit(solution)/shard_map/middle/pallas_call | solution.py:383
  281.0 39.7 %attend_back.1 = (bf16[1024,768]{1,0:T(8,128)(2,1)}, bf16[5120,768]{1,0:T(8,128)(2,1)}, bf16[5120,768]{1,0:T(8,128)(2,1)}) custom-call(s32[1536]{0:T(1024)} %copy-done.3, bf16[1024,768]{1,0:T(8,128)(2,1)} %copy-done.1, bf16[1024,768]{1,0:T(8,128)(2,1)} %get-tuple-element.57.g_ref, bf16[5120,768]{1,0:T(8,128)(2,1)} %copy-done, ...), custom_call_target="tpu_custom_call" | custom-call | tf_op jit(solution)/shard_map/attend_back/pallas_call | solution.py:215
  320.7 1.7 convert_reduce_fusion.3
  322.4 4.4 convert_reduce_fusion.2
  327.8 0.7 copy.56
  328.5 12.2 %convolution_convert_fusion.2 = bf16[768,768]{1,0:T(8,128)(2,1)} fusion(bf16[5120,768]{1,0:T(8,128)(2,1)} %bitcast.80, bf16[5120,768]{1,0:T(8,128)(2,1)} %get-tuple-element.60), kind=kOutput, calls=%fused_computation.10 | convolution fusion | flops 6040387584 | bytes 16908288 | tf_op jit(solution)/shard_map/dot_general | solution.py:39
  340.7 9.8 %convolution_convert_fusion.1 = bf16[768,768]{1,0:T(8,128)(2,1)} fusion(bf16[5120,768]{1,0:T(8,128)(2,1)} %bitcast.81, bf16[5120,768]{1,0:T(8,128)(2,1)S(1)} %bitcast.60), kind=kOutput, calls=%fused_computation.9 | convolution fusion | flops 6040387584 | bytes 16908288 | tf_op jit(solution)/shard_map/dot_general | solution.py:39
  350.5 2.5 convolution_convert_fusion.3
  353.1 9.5 %fusion.7 = f32[5120,768]{1,0:T(8,128)} fusion(bf16[5120,768]{1,0:T(8,128)(2,1)S(1)} %bitcast.85, bf16[768,768]{1,0:T(8,128)(2,1)S(1)} %bitcast.89), kind=kOutput, calls=%fused_computation.50 | convolution fusion | flops 6039797760 | bytes 24772608 | tf_op jit(solution)/shard_map/dot_general | solution.py:35
  362.6 11.7 %add_convert_fusion = bf16[5120,768]{1,0:T(8,128)(2,1)} fusion(f32[5120,768]{1,0:T(8,128)} %fusion.7, bf16[5120,768]{1,0:T(8,128)(2,1)S(1)} %bitcast.60, bf16[768,768]{1,0:T(8,128)(2,1)S(1)} %bitcast.87), kind=kOutput, calls=%fused_computation.3 | convolution fusion | flops 6047662080 | bytes 32636928 | tf_op jit(solution)/shard_map/dot_general | solution.py:35
  374.3 190.5 %shard_map.315 = (f32[1024,768]{1,0:T(8,128)}, f32[8,128]{1,0:T(8,128)}, f32[24,768]{1,0:T(8,128)}, f32[24,768]{1,0:T(8,128)}, f32[24,768]{1,0:T(8,128)}, /*inde...) custom-call(bf16[5,1024,768]{2,1,0:T(8,128)(2,1)} %bitcast.61, f32[4,8,8,128]{3,2,1,0:T(8,128)} %copy.56, ...), custom_call_target="tpu_custom_call" | custom-call | tf_op jit(solution)/shard_map/pallas_call | solution.py:1044
  564.9 6.0 %add_add_fusion = f32[1024,768]{1,0:T(8,128)} fusion(f32[1024,768]{1,0:T(8,128)} %get-tuple-element.67, f32[1024,768]{1,0:T(8,128)} %get-tuple-element.56, bf16[1024,768]{1,0:T(8,128)(2,1)S(1)} %copy-done.6, bf16[768,768]{1,0:T(8,128)(2,1)S(1)} %bitcast.67), kind=kOutput, calls=%fused_computation.7 | convolution fusion | flops 1209532416 | bytes 12189696 | tf_op jit(solution)/shard_map/dot_general | solution.py:35
  572.1 0.6 copy.64
  572.8 0.6 copy.65
  573.4 0.6 copy.66
  574.0 0.6 copy.67
  574.7 0.7 copy.68
  575.4 0.7 copy.69
  (103 shorter events, 6.6 us)
Async XLA Ops:
  13.9 165.0 %copy-start.4 = (bf16[1024,768]{1,0:T(8,128)(2,1)S(1)}, bf16[1024,768]{1,0:T(8,128)(2,1)}, u32[]{:S(2)}) copy-start(bf16[1024,768]{1,0:T(8,128)(2,1)} %x_ref.1) | copy-start | bytes 4718596
  14.3 183.6 %copy-start.3 = (s32[1536]{0:T(1024)}, s32[1536]{0:T(1024)S(1)}, u32[]{:S(2)}) copy-start(s32[1536]{0:T(1024)S(1)} %min.12.rows_ref) | copy-start | bytes 18436
  178.8 3.6 copy-start.17
  178.8 3.9 copy-start.18
  182.7 15.2 %copy-start.1 = (bf16[1024,768]{1,0:T(8,128)(2,1)}, bf16[1024,768]{1,0:T(8,128)(2,1)S(1)}, u32[]{:S(2)}) copy-start(bf16[1024,768]{1,0:T(8,128)(2,1)S(1)} %fusion.q_ref) | copy-start | bytes 4718596
  182.7 8.5 %copy-start.19 = (bf16[4,8,24,768]{3,2,1,0:T(8,128)(2,1)S(1)}, bf16[4,8,24,768]{3,2,1,0:T(8,128)(2,1)}, u32[]{:S(2)}) copy-start(bf16[4,8,24,768]{3,2,1,0:T(8,128)(2,1)} %get-tuple-element.49) | copy-start | bytes 3538948
  197.9 28.9 %copy-start = (bf16[5120,768]{1,0:T(8,128)(2,1)}, bf16[5120,768]{1,0:T(8,128)(2,1)S(1)}, u32[]{:S(2)}) copy-start(bf16[5120,768]{1,0:T(8,128)(2,1)S(1)} %convolution_convert_fusion.k_ref) | copy-start | bytes 23592964
  226.8 1.2 copy-start.2
  322.4 4.6 copy-start.15
  322.4 4.7 copy-start.14
  327.8 12.9 %slice-start = ((s8[7864320]{0:T(1024)(128)(4,1)}), s8[4194304]{0:T(1024)(128)(4,1)S(1)}, s32[]{:S(2)}) async-start(s8[7864320]{0:T(1024)(128)(4,1)} %bitcast.59), calls=%async_computation | async-start | bytes 8388608
  328.5 12.2 %slice-start.1 = ((s8[7864320]{0:T(1024)(128)(4,1)}), s8[3670016]{0:T(1024)(128)(4,1)S(1)}, s32[]{:S(2)}) async-start(s8[7864320]{0:T(1024)(128)(4,1)} %bitcast.59), calls=%async_computation.1 | async-start | bytes 7340032
  328.5 24.6 %slice-start.2 = ((s8[7864320]{0:T(1024)(128)(4,1)}), s8[4194304]{0:T(1024)(128)(4,1)S(1)}, s32[]{:S(2)}) async-start(s8[7864320]{0:T(1024)(128)(4,1)} %bitcast.84), calls=%async_computation.2 | async-start | bytes 8388608
  340.7 9.8 %copy-start.5 = (bf16[1024,768]{1,0:T(8,128)(2,1)S(1)}, bf16[1024,768]{1,0:T(8,128)(2,1)}, u32[]{:S(2)}) copy-start(bf16[1024,768]{1,0:T(8,128)(2,1)} %x_ref.1) | copy-start | bytes 4718596
  340.7 9.8 %copy-start.6 = (bf16[1024,768]{1,0:T(8,128)(2,1)S(1)}, bf16[1024,768]{1,0:T(8,128)(2,1)}, u32[]{:S(2)}) copy-start(bf16[1024,768]{1,0:T(8,128)(2,1)} %get-tuple-element.59) | copy-start | bytes 4718596
  340.7 12.4 %slice-start.3 = ((s8[7864320]{0:T(1024)(128)(4,1)}), s8[3670016]{0:T(1024)(128)(4,1)S(1)}, s32[]{:S(2)}) async-start(s8[7864320]{0:T(1024)(128)(4,1)} %bitcast.84), calls=%async_computation.3 | async-start | bytes 7340032
  350.5 2.5 copy-start.20
  374.3 190.5 %copy-start.7 = (bf16[4,8,24,768]{3,2,1,0:T(8,128)(2,1)S(1)}, bf16[4,8,24,768]{3,2,1,0:T(8,128)(2,1)}, u32[]{:S(2)}) copy-start(bf16[4,8,24,768]{3,2,1,0:T(8,128)(2,1)} %get-tuple-element.46) | copy-start | bytes 3538948
  564.9 6.1 %copy-start.16 = (f32[8,128]{1,0:T(8,128)S(1)}, f32[8,128]{1,0:T(8,128)}, u32[]{:S(2)}) copy-start(f32[8,128]{1,0:T(8,128)} %get-tuple-element.74) | copy-start | bytes 12292
  564.9 7.3 %copy-start.13 = (f32[24,768]{1,0:T(8,128)S(1)}, f32[24,768]{1,0:T(8,128)}, u32[]{:S(2)}) copy-start(f32[24,768]{1,0:T(8,128)} %get-tuple-element.124) | copy-start | bytes 221188
  564.9 7.9 %copy-start.12 = (f32[24,768]{1,0:T(8,128)S(1)}, f32[24,768]{1,0:T(8,128)}, u32[]{:S(2)}) copy-start(f32[24,768]{1,0:T(8,128)} %get-tuple-element.125) | copy-start | bytes 221188
  564.9 8.5 %copy-start.11 = (f32[24,768]{1,0:T(8,128)S(1)}, f32[24,768]{1,0:T(8,128)}, u32[]{:S(2)}) copy-start(f32[24,768]{1,0:T(8,128)} %get-tuple-element.126) | copy-start | bytes 221188
  564.9 9.1 %copy-start.10 = (f32[24,768]{1,0:T(8,128)S(1)}, f32[24,768]{1,0:T(8,128)}, u32[]{:S(2)}) copy-start(f32[24,768]{1,0:T(8,128)} %get-tuple-element.127) | copy-start | bytes 221188
  564.9 9.8 %copy-start.9 = (f32[24,3072]{1,0:T(8,128)S(1)}, f32[24,3072]{1,0:T(8,128)}, u32[]{:S(2)}) copy-start(f32[24,3072]{1,0:T(8,128)} %get-tuple-element.128) | copy-start | bytes 884740
  564.9 10.5 %copy-start.8 = (f32[96,768]{1,0:T(8,128)S(1)}, f32[96,768]{1,0:T(8,128)}, u32[]{:S(2)}) copy-start(f32[96,768]{1,0:T(8,128)} %get-tuple-element.129) | copy-start | bytes 884740

commit v4 on v3

--- a/solution.py
+++ b/solution.py
@@ -233,6 +233,11 @@
             jax.ShapeDtypeStruct((ext, width), bf16),
         ],
         compiler_params=pltpu.CompilerParams(vmem_limit_bytes=56 << 20),
+        cost_estimate=pl.CostEstimate(
+            flops=10 * groups * blocks * TILES * BLOCK * cols * cols,
+            bytes_accessed=100 << 20,
+            transcendentals=0,
+        ),
         name="attend_back",
     )(rows, queries, grads, keys, values, probs)
 
@@ -426,6 +431,124 @@
     )(attended, tokens, out_grad, w_attn, w_inner, w_outer, vectors, bias_inner)
 
 
+def project_kernel(wide_ref, wk_ref, wv_ref, wq_ref, vec_ref, k_ref, v_ref, q_ref):
+    rows = wide_ref.shape[0]
+    slices = [pl.ds(t * ROWS, ROWS) for t in range(rows // ROWS)]
+    for s in slices:
+        k_ref[s, :] = mm(wide_ref[s, :], wk_ref[...]).astype(bf16)
+        v_ref[s, :] = (mm(wide_ref[s, :], wv_ref[...]) + vec_ref[7:8, :]).astype(bf16)
+
+    @pl.when(pl.program_id(0) == REACH)
+    def _():
+        for s in slices:
+            queries = mm(wide_ref[s, :], wq_ref[...]) + vec_ref[6:7, :]
+            q_ref[s, :] = (query_scale * queries).astype(bf16)
+
+
+def project(wide, w_key, w_value, w_query, vectors, rows):
+    width = wide.shape[1]
+    one = pl.Buffered(1)
+    tile = pl.BlockSpec((rows, width), lambda i: (i, 0))
+    still = pl.BlockSpec((rows, width), lambda i: (0, 0), pipeline_mode=one)
+    square = pl.BlockSpec((width, width), lambda i: (0, 0), pipeline_mode=one)
+    table = jax.ShapeDtypeStruct(wide.shape, bf16)
+    return pl.pallas_call(
+        project_kernel,
+        grid=(1 + 2 * REACH,),
+        in_specs=[tile, square, square, square, pl.BlockSpec((8, width), lambda i: (0, 0))],
+        out_specs=[tile, tile, still],
+        out_shape=[table, table, jax.ShapeDtypeStruct((rows, width), bf16)],
+        compiler_params=pltpu.CompilerParams(vmem_limit_bytes=40 << 20),
+        name="project",
+    )(wide, w_key, w_value, w_query, vectors)
+
+
+def project_back_kernel(
+    wide_ref,
+    dk_ref,
+    dv_ref,
+    dq_ref,
+    wk_ref,
+    wv_ref,
+    wq_ref,
+    first_ref,
+    dx_ref,
+    rows_ref,
+    dwk_ref,
+    dwv_ref,
+    dwq_ref,
+    sums_ref,
+    key_sum,
+    value_sum,
+):
+    step = pl.program_id(0)
+    rows, width = dx_ref.shape
+    slices = [pl.ds(t * ROWS, ROWS) for t in range(rows // ROWS)]
+    columns = [pl.ds(n * 256, 256) for n in range(width // 256)]
+
+    def summed(ref):
+        return jnp.sum(ref[...].astype(f32), axis=0, keepdims=True)
+
+    @pl.when(step == 0)
+    def _():
+        key_sum[...] = jnp.zeros_like(key_sum)
+        value_sum[...] = jnp.zeros_like(value_sum)
+        sums_ref[...] = jnp.zeros_like(sums_ref)
+
+    for s in slices:
+        dx_ref[s, :] = (
+            mm_nt(dk_ref[s, :], wk_ref[...]) + mm_nt(dv_ref[s, :], wv_ref[...])
+        ).astype(bf16)
+    for c in columns:
+        key_sum[c, :] += mm_tn(wide_ref[:, c], dk_ref[...])
+        value_sum[c, :] += mm_tn(wide_ref[:, c], dv_ref[...])
+    sums_ref[0:1, :] += summed(dv_ref)
+
+    @pl.when(step == REACH)
+    def _():
+        for s in slices:
+            rows_ref[s, :] = first_ref[s, :] + mm_nt(dq_ref[s, :], wq_ref[...])
+        for c in columns:
+            dwq_ref[c, :] = mm_tn(wide_ref[:, c], dq_ref[...]).astype(bf16)
+        sums_ref[1:2, :] = summed(dq_ref)
+
+    @pl.when(step == pl.num_programs(0) - 1)
+    def _():
+        dwk_ref[...] = key_sum[...].astype(bf16)
+        dwv_ref[...] = value_sum[...].astype(bf16)
+
+
+def project_back(wide, grad_keyed, grad_valued, grad_scaled, w_key, w_value, w_query, grad_first):
+    rows, width = grad_scaled.shape
+    one = pl.Buffered(1)
+    tile = pl.BlockSpec((rows, width), lambda i: (i, 0))
+    still = pl.BlockSpec((rows, width), lambda i: (0, 0), pipeline_mode=one)
+    square = pl.BlockSpec((width, width), lambda i: (0, 0), pipeline_mode=one)
+    few = pl.BlockSpec((8, width), lambda i: (0, 0))
+    matrix = jax.ShapeDtypeStruct((width, width), bf16)
+    steps = wide.shape[0] // rows
+    return pl.pallas_call(
+        project_back_kernel,
+        grid=(steps,),
+        in_specs=[tile, tile, tile, still, square, square, square, still],
+        out_specs=[tile, still, square, square, square, few],
+        out_shape=[
+            jax.ShapeDtypeStruct(wide.shape, bf16),
+            jax.ShapeDtypeStruct((rows, width), f32),
+            matrix,
+            matrix,
+            matrix,
+            jax.ShapeDtypeStruct((8, width), f32),
+        ],
+        scratch_shapes=[pltpu.VMEM((width, width), f32)] * 2,
+        compiler_params=pltpu.CompilerParams(vmem_limit_bytes=56 << 20),
+        cost_estimate=pl.CostEstimate(
+            flops=8 * wide.shape[0] * width * width, bytes_accessed=40 << 20, transcendentals=0
+        ),
+        name="project_back",
+    )(wide, grad_keyed, grad_valued, grad_scaled, w_key, w_value, w_query, grad_first)
+
+
 def tile_plan(segment_ids, random_blocks, tokens):
     heads, total_blocks, _ = random_blocks.shape
     blocks = tokens // BLOCK
@@ -440,8 +563,9 @@
     )
     near = lax.dynamic_slice_in_dim(padded, chunk * tokens, tokens + 2 * margin)
     own = near[margin : margin + tokens]
-    begins = jnp.sum((near[None, :] < own[:, None]).astype(jnp.int32), axis=1)
-    ends = jnp.sum((near[None, :] <= own[:, None]).astype(jnp.int32), axis=1)
+    before, after = near[: margin + tokens], near[margin:]
+    begins = jnp.sum((before[None, :] < own[:, None]).astype(jnp.int32), axis=1)
+    ends = margin + jnp.sum((after[None, :] <= own[:, None]).astype(jnp.int32), axis=1)
     docs = jnp.stack([begins, ends]).reshape(2, blocks, BLOCK)
     docs = jnp.tile(jnp.transpose(docs, (1, 0, 2)), (1, 4, GROUP))
     first = begins[::BLOCK] // BLOCK
@@ -508,6 +632,7 @@
 LINE = 4
 CORES = 2
 PIECES = 4
+PIECES_BACK = 8
 MESH = pl.DeviceIdType.MESH
 NEAR_SLOT = (1, 0, 4, 3)
 FAR_SLOT = (0, None, None, 4)
@@ -760,14 +885,113 @@
         + [dma((LINE, PIECES))] * 4
         + [dma((PIECES,))] * 4,
         compiler_params=pltpu.CompilerParams(collective_id=0, has_side_effects=True),
+        name="gather",
     )(tokens, *shards)
     return outs[0], outs[2:]
 
 
+def pair_kernel(blk, *refs):
+    grads, outs, (held, arrived), (load, send, recv) = (
+        refs[:3],
+        refs[3:7],
+        (refs[7:10], refs[10:13]),
+        refs[13:],
+    )
+    h, b = lax.axis_index("head"), lax.axis_index("blk")
+    chips = blk // CORES
+    chip, core = b // CORES, b % CORES
+    sibling = chip * CORES + 1 - core
+
+    def mine(a, e):
+        there = ((chip + e) % chips) * CORES + core
+        return pltpu.make_async_copy(grads[a].at[:, there], held[a].at[e], load.at[a, e])
+
+    def across(a, e):
+        there = ((chip + e) % chips) * CORES + 1 - core
+        return remote(
+            grads[a].at[:, there], arrived[a].at[e], send.at[a, e], recv.at[a, e], h, sibling
+        )
+
+    order = [e % chips for e in range(1, chips + 1)]
+    for e in order:
+        for a in range(3):
+            mine(a, e).start()
+    barrier = pltpu.get_barrier_semaphore()
+    pl.semaphore_signal(barrier, inc=1, device_id=(h, sibling), device_id_type=MESH)
+    pl.semaphore_wait(barrier, 1)
+    for e in order:
+        for a in range(3):
+            across(a, e).start()
+    for e in order:
+        for a in range(3):
+            mine(a, e).wait()
+            across(a, e).wait_recv()
+
+        def one(n, carry, e=e):
+            attn, inner, outer = (
+                held[a][e, n].astype(f32) + arrived[a][e, n].astype(f32) for a in range(3)
+            )
+            parts = [inner[:, m * 768 : (m + 1) * 768] for m in range(4)]
+            spare = jnp.zeros((8, 768), f32)
+            outs[e][n, 0:48] = jnp.concatenate([attn, parts[0]], axis=0).astype(bf16)
+            outs[e][n, 48:96] = jnp.concatenate(parts[1:3], axis=0).astype(bf16)
+            outs[e][n, 96:128] = jnp.concatenate([parts[3], spare], axis=0).astype(bf16)
+            outs[e][n, 128:224] = outer.astype(bf16)
+            return carry
+
+        lax.fori_loop(0, LINE, one, 0)
+    for e in order:
+        for a in range(3):
+            across(a, e).wait_send()
+
+
+def pair_sums(grads, blk):
+    chips = blk // CORES
+    shard = [g.shape[2:] for g in grads]
+    dma = pltpu.SemaphoreType.DMA
+    inside = pl.BlockSpec(memory_space=pltpu.VMEM)
+    return pl.pallas_call(
+        partial(pair_kernel, blk),
+        out_shape=[jax.ShapeDtypeStruct((LINE, 224, 768), bf16)] * chips,
+        in_specs=[pl.BlockSpec(memory_space=pl.ANY)] * 3,
+        out_specs=[inside] * chips,
+        scratch_shapes=[pltpu.VMEM((chips, LINE) + s, bf16) for s in shard] * 2
+        + [dma((3, chips))] * 3,
+        compiler_params=pltpu.CompilerParams(
+            collective_id=2, has_side_effects=True, vmem_limit_bytes=56 << 20
+        ),
+        name="pair_sums",
+    )(*grads)
+
+
+def over_plane(sums, blk, head):
+    chips = blk // CORES
+    received = [sums[0]]
+    for e in range(1, chips):
+        pairs = [
+            (
+                h * blk + k * CORES + c,
+                h * blk + ((k + e) % chips) * CORES + c,
+            )
+            for h in range(head)
+            for k in range(chips)
+            for c in range(CORES)
+        ]
+        received.append(lax.ppermute(sums[e], ("head", "blk"), pairs))
+    return received
+
+
+def unpacked(packed):
+    parts = [packed[n * 24 : (n + 1) * 24] for n in range(1, 5)]
+    return packed[:24], jnp.concatenate(parts, axis=1), packed[128:]
+
+
 def reduce_kernel(blk, count, *refs):
-    dx_ref, grads = refs[0], refs[1 : 1 + count]
-    sum_ref, outs = refs[1 + count], refs[2 + count : 2 + 2 * count]
-    rest = refs[2 + 2 * count :]
+    dx_ref, grads, early = refs[0], refs[1 : 1 + count], refs[1 + count : 1 + count + blk // CORES]
+    rest = refs[1 + count + blk // CORES :]
+    sum_ref, outs, early_ref = rest[0], rest[1 : 1 + count], rest[1 + count]
+    early_sum, early_in, es, er = rest[2 + count : 6 + count]
+    rest = rest[6 + count :]
     held, from_core, from_chip, from_line = (rest[n * count : (n + 1) * count] for n in range(4))
     line, arrived, aside = rest[4 * count : 4 * count + 3]
     load, ss, sr, cs, cr, zs, zr, xl, us, ur, ds, dr, ns, nr, fs, fr = rest[4 * count + 3 :]
@@ -775,7 +999,7 @@
     chips = blk // CORES
     chip, core = b // CORES, b % CORES
     sibling = chip * CORES + 1 - core
-    rows = dx_ref.shape[1] // PIECES
+    rows = dx_ref.shape[1] // PIECES_BACK
 
     def mine(a, k):
         return pltpu.make_async_copy(grads[a].at[:, k * CORES + core], held[a].at[k], load.at[a, k])
@@ -853,6 +1077,32 @@
             total = total + from_line[a][d - 1].astype(f32)
         outs[a][...] = total
 
+    def early_along(d):
+        there = (h + d) % LINE
+        return remote(
+            early_sum.at[there], early_in.at[d - 1], es.at[d - 1], er.at[d - 1], there, b
+        )
+
+    def early_to_line():
+        def one(n, carry):
+            total = early[0][n].astype(f32)
+            for ref in early[1:]:
+                total = total + ref[n].astype(f32)
+            early_sum[n] = total.astype(bf16)
+            return carry
+
+        lax.fori_loop(0, LINE, one, 0)
+        for d in range(1, LINE):
+            early_along(d).start()
+
+    def early_to_owner():
+        for d in range(1, LINE):
+            early_along(d).wait_recv()
+        total = early_sum[h].astype(f32)
+        for d in range(1, LINE):
+            total = total + early_in[d - 1].astype(f32)
+        early_ref[...] = total
+
     def part(p):
         return pl.ds(p * rows, rows)
 
@@ -929,7 +1179,7 @@
     def begin(hh):
         @pl.when(sends_side(hh))
         def _():
-            for p in range(PIECES):
+            for p in range(PIECES_BACK):
                 for slot, _, n, send, recv in side_parts(hh):
                     side(hh, slot, n, send, recv, p).start()
 
@@ -941,14 +1191,14 @@
                 fetch(hh, j).wait()
             else:
                 line[j] = jnp.zeros(line.shape[1:], line.dtype)
-        for p in range(PIECES):
+        for p in range(PIECES_BACK):
             if hh == 0:
                 up(hh, 1, p).start()
             if hh == LINE - 1:
                 down(hh, 2, p).start()
 
     def take_sides(hh):
-        for p in range(PIECES):
+        for p in range(PIECES_BACK):
             for _, j, n, send, recv in side_parts(hh):
 
                 @pl.when(gets_side(hh))
@@ -962,21 +1212,20 @@
                 if hh == LINE - 1:
                     down(hh, j, p).start()
 
-    def pass_on(first, hh):
+    def pass_on(hh):
+        moves = []
         if hh == 1:
-            moves = [(3, True), (0, False)] if first else [(2, True)]
-        elif hh == 2:
-            moves = [(0, False), (3, True)] if first else [(1, False)]
-        else:
-            moves = []
-        for p in range(PIECES):
+            moves = [(3, True), (2, True), (0, False)]
+        if hh == 2:
+            moves = [(0, False), (1, False), (3, True)]
+        for p in range(PIECES_BACK):
             for j, upward in moves:
                 (up_arrives if upward else down_arrives)(hh, j, p).wait_recv()
                 add_rows(line, j, arrived, j, p)
                 (up if upward else down)(hh, j, p).start()
 
     def finish(hh):
-        for p in range(PIECES):
+        for p in range(PIECES_BACK):
             sources = []
             if hh > 0:
                 up_arrives(hh, hh, p).wait_recv()
@@ -994,7 +1243,7 @@
                 return carry
 
             lax.fori_loop(0, rows // 64, one, 0)
-        for p in range(PIECES):
+        for p in range(PIECES_BACK):
             for j in range(LINE):
                 if j > hh:
                     up(hh, j, p).wait_send()
@@ -1003,7 +1252,7 @@
 
         @pl.when(sends_side(hh))
         def _():
-            for p in range(PIECES):
+            for p in range(PIECES_BACK):
                 for slot, _, n, send, recv in side_parts(hh):
                     side(hh, slot, n, send, recv, p).wait_send()
 
@@ -1015,14 +1264,17 @@
         for k in range(chips):
             across(a, k).start()
     at_each_head(h, begin)
+    at_each_head(h, take_sides)
+    early_to_line()
     for a in range(count):
         to_chips(a)
-    at_each_head(h, take_sides)
-    at_each_head(h, partial(pass_on, True))
-    at_each_head(h, partial(pass_on, False))
+    at_each_head(h, pass_on)
     for a in range(count):
         to_line(a)
     at_each_head(h, finish)
+    early_to_owner()
+    for d in range(1, LINE):
+        early_along(d).wait_send()
     for a in range(count):
         to_owner(a)
     for a in range(count):
@@ -1034,7 +1286,7 @@
             along(a, d).wait_send()
 
 
-def reduce_to_owners(wide_grad, grads, blk):
+def reduce_to_owners(wide_grad, grads, early, blk):
     _, rows, width = wide_grad.shape
     count, chips = len(grads), blk // CORES
     anywhere = pl.BlockSpec(memory_space=pl.ANY)
@@ -1044,10 +1296,17 @@
     outs = pl.pallas_call(
         partial(reduce_kernel, blk, count),
         out_shape=[jax.ShapeDtypeStruct((rows, width), f32)]
-        + [jax.ShapeDtypeStruct(s, f32) for s in shard],
-        in_specs=[anywhere] * (1 + count),
-        out_specs=[inside] * (1 + count),
-        scratch_shapes=[pltpu.VMEM((chips, LINE) + s, g.dtype) for s, g in zip(shard, grads)]
+        + [jax.ShapeDtypeStruct(s, f32) for s in shard]
+        + [jax.ShapeDtypeStruct(early[0].shape[1:], f32)],
+        in_specs=[anywhere] * (1 + count) + [inside] * chips,
+        out_specs=[inside] * (2 + count),
+        scratch_shapes=[
+            pltpu.VMEM(early[0].shape, bf16),
+            pltpu.VMEM((LINE - 1,) + early[0].shape[1:], bf16),
+            dma((LINE - 1,)),
+            dma((LINE - 1,)),
+        ]
+        + [pltpu.VMEM((chips, LINE) + s, g.dtype) for s, g in zip(shard, grads)]
         + [pltpu.VMEM((chips, LINE) + s, g.dtype) for s, g in zip(shard, grads)]
         + [pltpu.VMEM((chips - 1, LINE) + s, g.dtype) for s, g in zip(shard, grads)]
         + [pltpu.VMEM((LINE - 1,) + s, g.dtype) for s, g in zip(shard, grads)]
@@ -1060,13 +1319,14 @@
         + [dma((count, chips - 1))] * 2
         + [dma((count, LINE - 1))] * 2
         + [dma((LINE,))]
-        + [dma((LINE, PIECES))] * 4
-        + [dma((PIECES,))] * 4,
+        + [dma((LINE, PIECES_BACK))] * 4
+        + [dma((PIECES_BACK,))] * 4,
         compiler_params=pltpu.CompilerParams(
             collective_id=1, has_side_effects=True, vmem_limit_bytes=60 << 20
         ),
-    )(wide_grad, *grads)
-    return outs[0], outs[1:]
+        name="reduce_to_owners",
+    )(wide_grad, *grads, *early)
+    return outs[0], outs[1:-1], outs[-1]
 
 
 def whole(shard):
@@ -1075,11 +1335,6 @@
 
 def shared_out(grad):
     return lax.psum_scatter(grad.astype(bf16), ("head", "blk"), scatter_dimension=0, tiled=True).astype(f32)
-
-
-def vectors_of(table, sizes):
-    cuts = [sum(sizes[:n]) for n in range(len(sizes) + 1)]
-    return [table[..., a:b] for a, b in zip(cuts[:-1], cuts[1:])]
 
 
 def padded_to(flat, size):
@@ -1090,41 +1345,36 @@
     weights, vectors, (out_grad, segment_ids, random_blocks) = rest[:6], rest[6:15], rest[15:]
     rows = tokens.shape[0]
     by_kernel = head == LINE and blk == LINE * CORES
-    sizes = [v.shape[0] for v in vectors]
+    short = [vectors[n] for n in (2, 3, 4, 6, 7, 8, 0, 1)]
     if by_kernel:
-        packed = padded_to(jnp.concatenate(vectors), 16 * 128).reshape(16, 128)
-        order = (0, 1, 2, 3, 4, 5)
-        wide, fulls = gather(tokens, [packed] + [weights[n] for n in order], blk)
+        packed = jnp.concatenate(
+            [
+                padded_to(jnp.stack(short), 128),
+                padded_to(vectors[5][None], 128),
+                jnp.zeros((7, 128), bf16),
+            ]
+        )
+        wide, fulls = gather(tokens, [packed] + list(weights), blk)
         wide = wide.reshape(-1, tokens.shape[1])
         w_query, w_key, w_value, w_attn, w_inner, w_outer = [
             w.reshape(-1, w.shape[-1]) for w in fulls[1:]
         ]
-        table = fulls[0].reshape(head * blk, -1)
+        table = fulls[0].reshape(head * blk, 16, 128)
     else:
         wide = widen(tokens, blk, head)
         w_query, w_key, w_value, w_attn, w_inner, w_outer = [whole(w) for w in weights]
-        table = whole(jnp.concatenate(vectors)[None])
-    (
-        bias_query,
-        bias_value,
-        bias_attn,
-        gain_one,
-        offset_one,
-        bias_inner,
-        bias_outer,
-        gain_two,
-        offset_two,
-    ) = [v.reshape(-1).astype(f32) for v in vectors_of(table, sizes)]
+        packed = jnp.concatenate(
+            [padded_to(jnp.stack(short), 128), padded_to(vectors[5][None], 128)]
+        )
+        table = whole(packed[None])
+    short_rows = jnp.transpose(table[:, :8, : short[0].shape[0]], (1, 0, 2)).astype(f32)
+    short_rows = short_rows.reshape(8, -1)
+    bias_inner = table[:, 8, : vectors[5].shape[0]].astype(f32).reshape(-1, 1, PIECE)
 
     rows_of, bases, docs = tile_plan(segment_ids, random_blocks, rows)
-    queries = (query_scale * (mm(tokens, w_query) + bias_query)).astype(bf16)
-    keys = mm(wide, w_key).astype(bf16)
-    values = (mm(wide, w_value) + bias_value).astype(bf16)
+    keys, values, queries = project(wide, w_key, w_value, w_query, short_rows, rows)
     attended, probs = attend(rows_of, queries, keys, values, bases, docs)
 
-    rows_vec = jnp.stack(
-        [bias_attn, gain_one, offset_one, bias_outer, gain_two, offset_two, gain_two, gain_two]
-    )
     result, grad_first_sum, grad_attended, grad_w_attn, grad_w_inner, grad_w_outer, sums_d, sums_ff = (
         middle(
             attended,
@@ -1133,56 +1383,48 @@
             w_attn,
             w_inner,
             w_outer,
-            rows_vec,
-            bias_inner.reshape(-1, 1, PIECE),
+            short_rows,
+            bias_inner,
         )
     )
 
+    early_grads = [grad_w_attn, grad_w_inner, grad_w_outer]
+    if by_kernel:
+        early = over_plane(
+            pair_sums([g.reshape(head, blk, -1, g.shape[-1]) for g in early_grads], blk), blk, head
+        )
     grad_scaled, grad_keyed, grad_valued = attend_back(
         rows_of, queries, grad_attended, keys, values, probs
     )
-    def total(grads):
-        return jnp.sum(grads.astype(f32), axis=0)
-
-    sums = (
-        total(grad_scaled),
-        total(grad_valued),
-        sums_d[0],
-        sums_d[1],
-        sums_d[2],
-        sums_ff,
-        sums_d[3],
-        sums_d[4],
-        sums_d[5],
+    grad_wide, grad_rows, grad_w_key, grad_w_value, grad_w_query, sums_qv = project_back(
+        wide, grad_keyed, grad_valued, grad_scaled, w_key, w_value, w_query, grad_first_sum
     )
-    packed = jnp.concatenate([s.reshape(blk * head, -1) for s in sums], axis=1)
-    grad_wide = (mm_nt(grad_keyed, w_key) + mm_nt(grad_valued, w_value)).astype(bf16)
-    grad_rows = grad_first_sum + mm_nt(grad_scaled, w_query)
-    matrix_grads = [
-        mm_tn(tokens, grad_scaled).astype(bf16),
-        mm_tn(wide, grad_keyed).astype(bf16),
-        mm_tn(wide, grad_valued).astype(bf16),
-        grad_w_attn,
-        grad_w_inner,
-        grad_w_outer,
-    ]
+    late_grads = [grad_w_query, grad_w_key, grad_w_value]
+    sums = jnp.concatenate([sums_d[:6], sums_qv[1:2], sums_qv[0:1]])
+    sums = jnp.transpose(sums.reshape(8, head * blk, -1), (1, 0, 2))
+    packed = jnp.concatenate(
+        [
+            padded_to(sums, 128),
+            padded_to(sums_ff.reshape(head * blk, 1, -1), 128),
+            jnp.zeros((head * blk, 7, 128), f32),
+        ],
+        axis=1,
+    )
     if by_kernel:
-        shares = [g.reshape(head, blk, -1, g.shape[-1]) for g in matrix_grads]
-        small = padded_to(packed, 8 * 128).reshape(head, blk, 8, 128)
-        wide_sum, sums = reduce_to_owners(
-            grad_wide.reshape(-1, rows, grad_wide.shape[-1]), [small] + shares, blk
-        )
-        matrix_grads = list(sums[1:])
-        packed = sums[0].reshape(-1)
+        shares = [g.reshape(head, blk, -1, g.shape[-1]) for g in late_grads]
+        small = packed.reshape(head, blk, 16, 128)
+        wide_sum, late, early_sum = reduce_to_owners(
+            grad_wide.reshape(-1, rows, grad_wide.shape[-1]), [small] + shares, early, blk
+        )
+        matrix_grads = tuple(late[1:]) + unpacked(early_sum)
+        packed = late[0]
     else:
         wide_sum = narrow(grad_wide, rows, blk, head).astype(f32)
-        matrix_grads = [shared_out(g) for g in matrix_grads]
+        matrix_grads = tuple(shared_out(g) for g in late_grads + early_grads)
         packed = lax.psum_scatter(packed, ("head", "blk"), scatter_dimension=0, tiled=True)[0]
-    return (
-        (result, grad_rows + wide_sum)
-        + tuple(matrix_grads)
-        + tuple(vectors_of(packed, sizes))
-    )
+    order = (6, 7, 0, 1, 2, 8, 3, 4, 5)
+    vector_grads = tuple(packed[n, : v.shape[0]] for n, v in zip(order, vectors))
+    return (result, grad_rows + wide_sum) + matrix_grads + vector_grads
 
 
 def solution(mesh):

time: 582 us -> 550 us (0.945)
  matrix products: 69.7 us -> 0 us
  Pallas kernels: 472 us -> 505 us
  starting transfers between devices: 0 us -> 7.64 us
    pallas_call x0 -> x3, Pallas kernels: none -> 70.3 us  [the longest x1 38 us: project_back(): pl.pallas_call(project_back_kernel, grid=(steps,), in_specs=[tile, tile,...]
    dot_general x9 -> x0, matrix products: 69.7 us -> none  [the longest x3 27.2 us: mm_nt(): lax.dot_general(a, b, (((1,), (1,)), ((), ())), preferred_element_type=f32)]
    pallas_call x1, Pallas kernels: 191 us -> 145 us  [reduce_to_owners(): pl.pallas_call(partial(reduce_kernel, blk, count), out_shape=[jax.ShapeDt...]
    pallas_call x1, Pallas kernels: 53 us -> 61.8 us  [middle(): pl.pallas_call(middle_kernel, grid=(2 * steps,), in_specs=[still, still,...]
    reduce_sum x3 -> x1, other arithmetic: 10.3 us -> 2.59 us  [tile_plan(): jnp.sum((after[None, :] <= own[:, None]).astype(jnp.int32), axis=1)]
    ppermute x0 -> x3, starting transfers between devices: none -> 7.64 us  [over_plane(): received.append(lax.ppermute(sums[e], ('head', 'blk'), pairs))]
  transfers between devices with their start and end apart: 0 -> 3, of which waited for: 0 -> 0; matrix products, arithmetic and copies ran while one was open for 0% -> 0% of each run, Pallas kernels for 0% -> 14%
where the time goes in v4:
time: 550 us; the launch traced here: 545 us
  Pallas kernels  505 us (92%)
  local copies, waits for them, and re-layouts  20.8 us (4%)
  other arithmetic  10.7 us (2%)
  starting transfers between devices  7.64 us (1%)
    pallas_call x1, Pallas kernels, gather(): pl.pallas_call(partial(gather_kernel, blk, count), out_shape=[jax.ShapeDt...  160 us
    pallas_call x1, Pallas kernels, reduce_to_owners(): pl.pallas_call(partial(reduce_kernel, blk, count), out_shape=[jax.ShapeDt...  145 us
    pallas_call x1, Pallas kernels, middle(): pl.pallas_call(middle_kernel, grid=(2 * steps,), in_specs=[still, still,...  61.8 us
    pallas_call x1, Pallas kernels, attend_back(): pl.pallas_call(partial(attend_back_kernel, blocks), grid_spec=pltpu.Prefe...  39.5 us
    pallas_call x1, Pallas kernels, project_back(): pl.pallas_call(project_back_kernel, grid=(steps,), in_specs=[tile, tile,...  38 us
    pallas_call x1, Pallas kernels, attend(): pl.pallas_call(partial(attend_kernel, blocks), grid_spec=pltpu.PrefetchSc...  28.9 us
    pallas_call x1, Pallas kernels, project(): pl.pallas_call(project_kernel, grid=(1 + 2 * REACH,), in_specs=[tile, squ...  17.1 us
    pallas_call x1, Pallas kernels, pair_sums(): pl.pallas_call(partial(pair_kernel, blk), out_shape=[jax.ShapeDtypeStruct...  15.2 us
  transfers between devices with their start and end apart: 3, of which 0 were waited for; matrix products, arithmetic and copies ran while one was open for 0% of the time, Pallas kernels for 14%

profile of v4, /device:TPU:0, one launch (start us, length us, event | category | flops | bytes accessed | tf_op | source)
XLA Modules:
  0.0 545.4 jit_solution(3420129816346762622)
XLA Ops:
  0.7 0.7 fusion.5
  1.5 2.6 convert_reduce_fusion
  4.3 0.8 stack.57
  5.1 1.3 fusion.10.refs_1_
  6.5 159.6 %gather.1 = (bf16[5,1024,768]{2,1,0:T(8,128)(2,1)}, bf16[1024,768]{1,0:T(8,128)(2,1)}, bf16[4,8,16,128]{3,2,1,0:T(8,128)(2,1)}, bf16[4,8,24,768]{3,2,1,0:T(8,128...) custom-call(bf16[1024,768]{1,0:T(8,128)(2,1)} %x_ref.1, ...), custom_call_target="tpu_custom_call" | custom-call | tf_op jit(solution)/shard_map/gather/pallas_call | solution.py:872
  166.1 0.8 slice.98
  166.9 0.8 slice.100
  167.9 0.8 dynamic-slice_subtract_fusion
  171.2 0.7 reshape.201.bi_ref
  171.9 1.3 copy-done.4
  173.2 1.3 copy-done.5
  174.5 17.1 %project.1 = (bf16[5120,768]{1,0:T(8,128)(2,1)S(1)}, bf16[5120,768]{1,0:T(8,128)(2,1)}, bf16[1024,768]{1,0:T(8,128)(2,1)S(1)}) custom-call(bf16[5120,768]{1,0:T(8,128)(2,1)} %bitcast.64, bf16[768,768]{1,0:T(8,128)(2,1)S(1)} %bitcast.61, bf16[768,768]{1,0:T(8,128)(2,1)S(1)} %bitcast.63, bf16[768,768]{1,0:T(8,128)(2,1)S(1)} %bitcast.59, ...), custom_call_target="tpu_custom_call" | custom-call | tf_op jit(solution)/shard_map/project/pallas_call | solution.py:455
  191.6 28.9 %attend.1 = (bf16[1024,768]{1,0:T(8,128)(2,1)S(1)}, bf16[3,16,512,256]{3,2,1,0:T(8,128)(2,1)}) custom-call(s32[1536]{0:T(1024)S(1)} %min.12.rows_ref, bf16[1024,768]{1,0:T(8,128)(2,1)S(1)} %get-tuple-element.62.q_ref, bf16[5120,768]{1,0:T(8,128)(2,1)S(1)} %get-tuple-element.63.k_ref, bf16[5120,768]{1,0:T(8,128)(2,1)} %get-tuple-element.64.v_ref, ...), custom_call_target="tpu_custom_call" | custom-call | tf_op jit(solution)/shard_map/attend/pallas_call | solution.py:182
  220.5 1.2 copy-done.1
  221.6 61.8 %middle.1 = (bf16[1024,768]{1,0:T(8,128)(2,1)}, f32[1024,768]{1,0:T(8,128)}, bf16[1024,768]{1,0:T(8,128)(2,1)}, bf16[768,768]{1,0:T(8,128)(2,1)}, bf16[768,3072]...) custom-call(bf16[1024,768]{1,0:T(8,128)(2,1)} %copy-done.1, ...), custom_call_target="tpu_custom_call" | custom-call | tf_op jit(solution)/shard_map/middle/pallas_call | solution.py:388
  283.4 15.2 %pair_sums.1 = (bf16[4,224,768]{2,1,0:T(8,128)(2,1)}, bf16[4,224,768]{2,1,0:T(8,128)(2,1)}, bf16[4,224,768]{2,1,0:T(8,128)(2,1)}, bf16[4,224,768]{2,1,0:T(8,128)(2,1)}) custom-call(bf16[4,8,24,768]{3,2,1,0:T(8,128)(2,1)} %bitcast.75, bf16[4,8,24,3072]{3,2,1,0:T(8,128)(2,1)} %bitcast.69, bf16[4,8,96,768]{3,2,1,0:T(8,128)(2,1)} %bitcast.70), custom_call_target="tpu_custom_call" | custom-call | tf_op jit(solution)/shard_map/pair_sums/pallas_call | solution.py:953
  298.7 2.9 collective-permute-start
  301.6 2.4 collective-permute-start.1
  304.0 2.3 collective-permute-start.2
  306.3 39.5 %attend_back.1 = (bf16[1024,768]{1,0:T(8,128)(2,1)}, bf16[5120,768]{1,0:T(8,128)(2,1)}, bf16[5120,768]{1,0:T(8,128)(2,1)}) custom-call(s32[1536]{0:T(1024)} %copy-done.7, bf16[1024,768]{1,0:T(8,128)(2,1)} %copy-done.2, bf16[1024,768]{1,0:T(8,128)(2,1)} %get-tuple-element.70.g_ref, bf16[5120,768]{1,0:T(8,128)(2,1)} %copy-done, ...), custom_call_target="tpu_custom_call" | custom-call | flops 16106127360 | bytes 104857600 | tf_op jit(solution)/shard_map/attend_back/pallas_call | solution.py:215
  345.9 38.0 %project_back.1 = (bf16[5120,768]{1,0:T(8,128)(2,1)}, f32[1024,768]{1,0:T(8,128)}, bf16[768,768]{1,0:T(8,128)(2,1)}, bf16[768,768]{1,0:T(8,128)(2,1)}, bf16[768,768]{1,0:T(8,128)(2,1)}, /*index=5*/f32[8,768]{1,0:T(8,128)}) custom-call(bf16[5120,768]{1,0:T(8,128)(2,1)} %bitcast.65, bf16[5120,768]{1,0:T(8,128)(2,1)} %get-tuple-element.72.dk_ref, ...), custom_call_target="tpu_custom_call" | custom-call | flops 24159191040 | bytes 41943040 | tf_op jit(solution)/shard_map/project_back/pallas_call | solution.py:530
  383.9 0.8 fusion.12
  385.1 0.9 copy.57
  386.0 1.1 copy-done.9
  387.5 144.9 %reduce_to_owners.1 = (f32[1024,768]{1,0:T(8,128)}, f32[16,128]{1,0:T(8,128)}, f32[24,768]{1,0:T(8,128)}, f32[24,768]{1,0:T(8,128)}, f32[24,768]{1,0:T(8,128)}, /*index=5*/f32[224,768]{1,0:T(8,128)}) custom-call(bf16[5,1024,768]{2,1,0:T(8,128)(2,1)} %bitcast.66, f32[4,8,16,128]{3,2,1,0:T(8,128)} %bitcast.76, bf16[4,8,24,768]{3,2,1,0:T(8,128)(2,1)} %bitcast.74, ...), custom_call_target="tpu_custom_call" | custom-call | tf_op jit(solution)/shard_map/reduce_to_owners/pallas_call | solution.py:1296
  532.5 1.7 fusion.11
  534.2 1.7 slice.86
  535.9 1.5 slice_bitcast_fusion
  537.4 1.2 slice_bitcast_fusion.3
  538.6 4.0 add.87
  542.5 0.7 pad_maximum_fusion
  543.3 0.6 copy.65
  (73 shorter events, 5.0 us)
Async XLA Ops:
  169.5 2.4 copy-start.3
  170.7 20.9 %copy-start.7 = (s32[1536]{0:T(1024)}, s32[1536]{0:T(1024)S(1)}, u32[]{:S(2)}) copy-start(s32[1536]{0:T(1024)S(1)} %min.12.rows_ref) | copy-start | bytes 18436
  171.2 20.3 %copy-start.6 = (f32[8,768]{1,0:T(8,128)}, f32[8,768]{1,0:T(8,128)S(1)}, u32[]{:S(2)}) copy-start(f32[8,768]{1,0:T(8,128)S(1)} %reshape.200.vec_ref) | copy-start | bytes 73732
  171.9 1.3 copy-start.4
  173.2 1.3 copy-start.5
  191.5 28.9 %copy-start = (bf16[5120,768]{1,0:T(8,128)(2,1)}, bf16[5120,768]{1,0:T(8,128)(2,1)S(1)}, u32[]{:S(2)}) copy-start(bf16[5120,768]{1,0:T(8,128)(2,1)S(1)} %get-tuple-element.63.k_ref) | copy-start | bytes 23592964
  191.5 28.9 %copy-start.2 = (bf16[1024,768]{1,0:T(8,128)(2,1)}, bf16[1024,768]{1,0:T(8,128)(2,1)S(1)}, u32[]{:S(2)}) copy-start(bf16[1024,768]{1,0:T(8,128)(2,1)S(1)} %get-tuple-element.62.q_ref) | copy-start | bytes 4718596
  220.4 1.2 copy-start.1
  298.7 87.3 %collective-permute-start = (bf16[4,224,768]{2,1,0:T(8,128)(2,1)}, bf16[4,224,768]{2,1,0:T(8,128)(2,1)S(1)}, u32[]{:S(2)}, u32[]{:S(2)}) collective-permute-start(bf16[4,224,768]{2,1,0:T(8,128)(2,1)} %get-tuple-element.88), channel_id=1, source_target_pairs={{0,2},{1,3},{2,4},{3,5},{4,6},{5,7},{6,0},{7,1},{8,10},{9,11},{10,... | collective-permute-start | bytes 4128776 | tf_op jit(solution)/shard_map/ppermute | solution.py:980
  301.6 84.4 %collective-permute-start.1 = (bf16[4,224,768]{2,1,0:T(8,128)(2,1)}, bf16[4,224,768]{2,1,0:T(8,128)(2,1)S(1)}, u32[]{:S(2)}, u32[]{:S(2)}) collective-permute-start(bf16[4,224,768]{2,1,0:T(8,128)(2,1)} %get-tuple-element.89), channel_id=1, source_target_pairs={{0,4},{1,5},{2,6},{3,7},{4,0},{5,1},{6,2},{7,3},{8,12},{9,13},{10,... | collective-permute-start | bytes 4128776 | tf_op jit(solution)/shard_map/ppermute | solution.py:980
  304.0 82.1 %collective-permute-start.2 = (bf16[4,224,768]{2,1,0:T(8,128)(2,1)}, bf16[4,224,768]{2,1,0:T(8,128)(2,1)}, u32[]{:S(2)}, u32[]{:S(2)}) collective-permute-start(bf16[4,224,768]{2,1,0:T(8,128)(2,1)} %get-tuple-element.90), channel_id=1, source_target_pairs={{0,6},{1,7},{2,0},{3,1},{4,2},{5,3},{6,4},{7,5},{8,14},{9,15},{10,... | collective-permute-start | bytes 4128776 | tf_op jit(solution)/shard_map/ppermute | solution.py:980
  345.8 38.9 %copy-start.14 = (f32[8,768]{1,0:T(8,128)S(1)}, f32[8,768]{1,0:T(8,128)}, u32[]{:S(2)}) copy-start(f32[8,768]{1,0:T(8,128)} %get-tuple-element.78) | copy-start | bytes 73732
  345.8 39.0 %copy-start.15 = (f32[4,1,768]{2,1,0:T(1,128)S(1)}, f32[4,1,768]{2,1,0:T(1,128)}, u32[]{:S(2)}) copy-start(f32[4,1,768]{2,1,0:T(1,128)} %get-tuple-element.80) | copy-start | bytes 36868
  386.0 1.1 copy-start.9
  386.0 1.5 copy-start.10
  387.5 151.0 %copy-start.8 = (f32[1024,768]{1,0:T(8,128)S(1)}, f32[1024,768]{1,0:T(8,128)}, u32[]{:S(2)}) copy-start(f32[1024,768]{1,0:T(8,128)} %get-tuple-element.76) | copy-start | bytes 9437188
  538.6 4.7 copy-start.13
  538.6 5.4 copy-start.12
  538.6 6.0 %copy-start.11 = (f32[24,768]{1,0:T(8,128)S(1)}, f32[24,768]{1,0:T(8,128)}, u32[]{:S(2)}) copy-start(f32[24,768]{1,0:T(8,128)} %get-tuple-element.143) | copy-start | bytes 221188

commit v5 on v4

--- a/solution.py
+++ b/solution.py
@@ -463,90 +463,58 @@
     )(wide, w_key, w_value, w_query, vectors)
 
 
-def project_back_kernel(
-    wide_ref,
-    dk_ref,
-    dv_ref,
-    dq_ref,
-    wk_ref,
-    wv_ref,
-    wq_ref,
-    first_ref,
-    dx_ref,
-    rows_ref,
-    dwk_ref,
-    dwv_ref,
-    dwq_ref,
-    sums_ref,
-    key_sum,
-    value_sum,
+def tokens_back_kernel(
+    dk_ref, dv_ref, dq_ref, wk_ref, wv_ref, wq_ref, first_ref, dx_ref, rows_ref, sums_ref
 ):
     step = pl.program_id(0)
-    rows, width = dx_ref.shape
+    rows = dx_ref.shape[0]
     slices = [pl.ds(t * ROWS, ROWS) for t in range(rows // ROWS)]
-    columns = [pl.ds(n * 256, 256) for n in range(width // 256)]
 
     def summed(ref):
         return jnp.sum(ref[...].astype(f32), axis=0, keepdims=True)
 
     @pl.when(step == 0)
     def _():
-        key_sum[...] = jnp.zeros_like(key_sum)
-        value_sum[...] = jnp.zeros_like(value_sum)
         sums_ref[...] = jnp.zeros_like(sums_ref)
 
     for s in slices:
         dx_ref[s, :] = (
             mm_nt(dk_ref[s, :], wk_ref[...]) + mm_nt(dv_ref[s, :], wv_ref[...])
         ).astype(bf16)
-    for c in columns:
-        key_sum[c, :] += mm_tn(wide_ref[:, c], dk_ref[...])
-        value_sum[c, :] += mm_tn(wide_ref[:, c], dv_ref[...])
-    sums_ref[0:1, :] += summed(dv_ref)
+    sums_ref[7:8, :] += summed(dv_ref)
 
     @pl.when(step == REACH)
     def _():
         for s in slices:
             rows_ref[s, :] = first_ref[s, :] + mm_nt(dq_ref[s, :], wq_ref[...])
-        for c in columns:
-            dwq_ref[c, :] = mm_tn(wide_ref[:, c], dq_ref[...]).astype(bf16)
-        sums_ref[1:2, :] = summed(dq_ref)
-
-    @pl.when(step == pl.num_programs(0) - 1)
-    def _():
-        dwk_ref[...] = key_sum[...].astype(bf16)
-        dwv_ref[...] = value_sum[...].astype(bf16)
-
-
-def project_back(wide, grad_keyed, grad_valued, grad_scaled, w_key, w_value, w_query, grad_first):
+        sums_ref[6:7, :] = summed(dq_ref)
+
+
+def tokens_back(grad_keyed, grad_valued, grad_scaled, w_key, w_value, w_query, grad_first):
     rows, width = grad_scaled.shape
     one = pl.Buffered(1)
     tile = pl.BlockSpec((rows, width), lambda i: (i, 0))
     still = pl.BlockSpec((rows, width), lambda i: (0, 0), pipeline_mode=one)
     square = pl.BlockSpec((width, width), lambda i: (0, 0), pipeline_mode=one)
     few = pl.BlockSpec((8, width), lambda i: (0, 0))
-    matrix = jax.ShapeDtypeStruct((width, width), bf16)
-    steps = wide.shape[0] // rows
     return pl.pallas_call(
-        project_back_kernel,
-        grid=(steps,),
-        in_specs=[tile, tile, tile, still, square, square, square, still],
-        out_specs=[tile, still, square, square, square, few],
+        tokens_back_kernel,
+        grid=(1 + 2 * REACH,),
+        in_specs=[tile, tile, still, square, square, square, still],
+        out_specs=[tile, still, few],
         out_shape=[
-            jax.ShapeDtypeStruct(wide.shape, bf16),
+            jax.ShapeDtypeStruct(grad_keyed.shape, bf16),
             jax.ShapeDtypeStruct((rows, width), f32),
-            matrix,
-            matrix,
-            matrix,
             jax.ShapeDtypeStruct((8, width), f32),
         ],
-        scratch_shapes=[pltpu.VMEM((width, width), f32)] * 2,
-        compiler_params=pltpu.CompilerParams(vmem_limit_bytes=56 << 20),
+        compiler_params=pltpu.CompilerParams(vmem_limit_bytes=40 << 20),
         cost_estimate=pl.CostEstimate(
-            flops=8 * wide.shape[0] * width * width, bytes_accessed=40 << 20, transcendentals=0
+            flops=4 * grad_keyed.shape[0] * width * width,
+            bytes_accessed=30 << 20,
+            transcendentals=0,
         ),
-        name="project_back",
-    )(wide, grad_keyed, grad_valued, grad_scaled, w_key, w_value, w_query, grad_first)
+        name="tokens_back",
+    )(grad_keyed, grad_valued, grad_scaled, w_key, w_value, w_query, grad_first)
 
 
 def tile_plan(segment_ids, random_blocks, tokens):
@@ -981,25 +949,84 @@
     return received
 
 
-def unpacked(packed):
-    parts = [packed[n * 24 : (n + 1) * 24] for n in range(1, 5)]
-    return packed[:24], jnp.concatenate(parts, axis=1), packed[128:]
-
-
 def reduce_kernel(blk, count, *refs):
-    dx_ref, grads, early = refs[0], refs[1 : 1 + count], refs[1 + count : 1 + count + blk // CORES]
-    rest = refs[1 + count + blk // CORES :]
-    sum_ref, outs, early_ref = rest[0], rest[1 : 1 + count], rest[1 + count]
-    early_sum, early_in, es, er = rest[2 + count : 6 + count]
-    rest = rest[6 + count :]
+    dx_ref, small_ref, wide_ref, sides_refs = refs[0], refs[1], refs[2], refs[3:6]
+    early = refs[6 : 6 + blk // CORES]
+    rest = refs[6 + blk // CORES :]
+    sum_ref, outs, early_outs = rest[0], rest[1 : 1 + count], rest[1 + count : 4 + count]
+    early_sum, early_in, es, er = rest[4 + count : 8 + count]
+    totals, (wide_in, key_in, value_in, fed) = rest[8 + count : 11 + count], rest[11 + count : 15 + count]
+    rest = rest[15 + count :]
     held, from_core, from_chip, from_line = (rest[n * count : (n + 1) * count] for n in range(4))
     line, arrived, aside = rest[4 * count : 4 * count + 3]
     load, ss, sr, cs, cr, zs, zr, xl, us, ur, ds, dr, ns, nr, fs, fr = rest[4 * count + 3 :]
+    grads = (small_ref,) + tuple(totals)
     h, b = lax.axis_index("head"), lax.axis_index("blk")
     chips = blk // CORES
     chip, core = b // CORES, b % CORES
     sibling = chip * CORES + 1 - core
     rows = dx_ref.shape[1] // PIECES_BACK
+
+    feed_rows = wide_in.shape[1]
+    feeds = wide_ref.shape[0] // feed_rows
+    per_chunk = feeds // (1 + 2 * REACH)
+    query_ref, key_ref, value_ref = sides_refs
+
+    def feed(step, slot):
+        some = pl.ds(step * feed_rows, feed_rows)
+        return [
+            pltpu.make_async_copy(source.at[some], target.at[slot], fed.at[n, slot])
+            for n, (source, target) in enumerate(
+                ((wide_ref, wide_in), (key_ref, key_in), (value_ref, value_in))
+            )
+        ]
+
+    def add_product(total, left, right, fresh):
+        half = left.shape[1] // 2
+        for n in range(2):
+            lines = LINE // 2
+            part = mm_tn(left[:, n * half : (n + 1) * half], right)
+            part = part.reshape((lines,) + total.shape[1:])
+            here = pl.ds(n * lines, lines)
+            total[here] = part if fresh else total[here] + part
+
+    def weigh():
+        for copy in feed(0, 0):
+            copy.start()
+        for n in (1, 2):
+            totals[n][...] = jnp.zeros_like(totals[n])
+
+        def one(step, carry):
+            slot = step % 2
+
+            @pl.when(step + 1 < feeds)
+            def _():
+                for copy in feed(step + 1, 1 - slot):
+                    copy.start()
+
+            for copy in feed(step, slot):
+                copy.wait()
+            add_product(totals[1], wide_in[slot], key_in[slot], False)
+            add_product(totals[2], wide_in[slot], value_in[slot], False)
+            return carry
+
+        lax.fori_loop(0, feeds, one, 0)
+        for n in range(per_chunk):
+            copies = [
+                pltpu.make_async_copy(
+                    wide_ref.at[pl.ds((REACH * per_chunk + n) * feed_rows, feed_rows)],
+                    wide_in.at[0],
+                    fed.at[0, 0],
+                ),
+                pltpu.make_async_copy(
+                    query_ref.at[pl.ds(n * feed_rows, feed_rows)], key_in.at[0], fed.at[1, 0]
+                ),
+            ]
+            for copy in copies:
+                copy.start()
+            for copy in copies:
+                copy.wait()
+            add_product(totals[0], wide_in[0], key_in[0], n == 0)
 
     def mine(a, k):
         return pltpu.make_async_copy(grads[a].at[:, k * CORES + core], held[a].at[k], load.at[a, k])
@@ -1038,16 +1065,16 @@
 
     def add_cores(a, k):
         def one(n, carry):
-            held[a][k, n] = (held[a][k, n].astype(f32) + from_core[a][k, n].astype(f32)).astype(
-                held[a].dtype
-            )
+            own = held[a][k, n] if a == 0 else grads[a][n, k * CORES + core]
+            held[a][k, n] = (own + from_core[a][k, n]).astype(held[a].dtype)
             return carry
 
         lax.fori_loop(0, LINE, one, 0)
 
     def to_chips(a):
         for k in range(chips):
-            mine(a, k).wait()
+            if a == 0:
+                mine(a, k).wait()
             across(a, k).wait_recv()
         for e in range(1, chips):
             add_cores(a, (chip + e) % chips)
@@ -1101,7 +1128,11 @@
         total = early_sum[h].astype(f32)
         for d in range(1, LINE):
             total = total + early_in[d - 1].astype(f32)
-        early_ref[...] = total
+        attn_ref, inner_ref, outer_ref = early_outs
+        attn_ref[...] = total[:24]
+        for n in range(4):
+            inner_ref[:, n * 768 : (n + 1) * 768] = total[24 * (n + 1) : 24 * (n + 2)]
+        outer_ref[...] = total[128:]
 
     def part(p):
         return pl.ds(p * rows, rows)
@@ -1256,16 +1287,16 @@
                 for slot, _, n, send, recv in side_parts(hh):
                     side(hh, slot, n, send, recv, p).wait_send()
 
-    for a in range(count):
-        for k in range(chips):
-            mine(a, k).start()
+    for k in range(chips):
+        mine(0, k).start()
     greet_plane_and_line(h, b, blk)
+    at_each_head(h, begin)
+    early_to_line()
+    weigh()
     for a in range(count):
         for k in range(chips):
             across(a, k).start()
-    at_each_head(h, begin)
     at_each_head(h, take_sides)
-    early_to_line()
     for a in range(count):
         to_chips(a)
     at_each_head(h, pass_on)
@@ -1286,30 +1317,36 @@
             along(a, d).wait_send()
 
 
-def reduce_to_owners(wide_grad, grads, early, blk):
+def reduce_to_owners(wide_grad, small, wide, projected, early, blk):
     _, rows, width = wide_grad.shape
-    count, chips = len(grads), blk // CORES
+    count, chips = 4, blk // CORES
     anywhere = pl.BlockSpec(memory_space=pl.ANY)
     inside = pl.BlockSpec(memory_space=pltpu.VMEM)
     dma = pltpu.SemaphoreType.DMA
-    shard = [g.shape[2:] for g in grads]
+    square = (width // (LINE * blk), width)
+    shard = [small.shape[2:]] + [square] * 3
+    kinds = [f32] + [bf16] * 3
+    early_shapes = ((24, 768), (24, 3072), (96, 768))
     outs = pl.pallas_call(
         partial(reduce_kernel, blk, count),
         out_shape=[jax.ShapeDtypeStruct((rows, width), f32)]
         + [jax.ShapeDtypeStruct(s, f32) for s in shard]
-        + [jax.ShapeDtypeStruct(early[0].shape[1:], f32)],
-        in_specs=[anywhere] * (1 + count) + [inside] * chips,
-        out_specs=[inside] * (2 + count),
+        + [jax.ShapeDtypeStruct(s, f32) for s in early_shapes],
+        in_specs=[anywhere] * 6 + [inside] * chips,
+        out_specs=[inside] * (4 + count),
         scratch_shapes=[
             pltpu.VMEM(early[0].shape, bf16),
             pltpu.VMEM((LINE - 1,) + early[0].shape[1:], bf16),
             dma((LINE - 1,)),
             dma((LINE - 1,)),
         ]
-        + [pltpu.VMEM((chips, LINE) + s, g.dtype) for s, g in zip(shard, grads)]
-        + [pltpu.VMEM((chips, LINE) + s, g.dtype) for s, g in zip(shard, grads)]
-        + [pltpu.VMEM((chips - 1, LINE) + s, g.dtype) for s, g in zip(shard, grads)]
-        + [pltpu.VMEM((LINE - 1,) + s, g.dtype) for s, g in zip(shard, grads)]
+        + [pltpu.VMEM((LINE, blk) + square, f32)] * 3
+        + [pltpu.VMEM((2, rows // 2, width), bf16)] * 3
+        + [dma((3, 2))]
+        + [pltpu.VMEM((chips, LINE) + s, t) for s, t in zip(shard, kinds)]
+        + [pltpu.VMEM((chips, LINE) + s, f32) for s in shard]
+        + [pltpu.VMEM((chips - 1, LINE) + s, t) for s, t in zip(shard, kinds)]
+        + [pltpu.VMEM((LINE - 1,) + s, t) for s, t in zip(shard, kinds)]
         + [
             pltpu.VMEM((LINE, rows, width), bf16),
             pltpu.VMEM((LINE + 1, rows, width), bf16),
@@ -1322,11 +1359,11 @@
         + [dma((LINE, PIECES_BACK))] * 4
         + [dma((PIECES_BACK,))] * 4,
         compiler_params=pltpu.CompilerParams(
-            collective_id=1, has_side_effects=True, vmem_limit_bytes=60 << 20
+            collective_id=1, has_side_effects=True, vmem_limit_bytes=62 << 20
         ),
         name="reduce_to_owners",
-    )(wide_grad, *grads, *early)
-    return outs[0], outs[1:-1], outs[-1]
+    )(wide_grad, small, wide, *projected, *early)
+    return outs[0], outs[1:-3], outs[-3:]
 
 
 def whole(shard):
@@ -1396,11 +1433,10 @@
     grad_scaled, grad_keyed, grad_valued = attend_back(
         rows_of, queries, grad_attended, keys, values, probs
     )
-    grad_wide, grad_rows, grad_w_key, grad_w_value, grad_w_query, sums_qv = project_back(
-        wide, grad_keyed, grad_valued, grad_scaled, w_key, w_value, w_query, grad_first_sum
+    grad_wide, grad_rows, sums_qv = tokens_back(
+        grad_keyed, grad_valued, grad_scaled, w_key, w_value, w_query, grad_first_sum
     )
-    late_grads = [grad_w_query, grad_w_key, grad_w_value]
-    sums = jnp.concatenate([sums_d[:6], sums_qv[1:2], sums_qv[0:1]])
+    sums = jnp.concatenate([sums_d[:6], sums_qv[6:]])
     sums = jnp.transpose(sums.reshape(8, head * blk, -1), (1, 0, 2))
     packed = jnp.concatenate(
         [
@@ -1411,15 +1447,19 @@
         axis=1,
     )
     if by_kernel:
-        shares = [g.reshape(head, blk, -1, g.shape[-1]) for g in late_grads]
-        small = packed.reshape(head, blk, 16, 128)
         wide_sum, late, early_sum = reduce_to_owners(
-            grad_wide.reshape(-1, rows, grad_wide.shape[-1]), [small] + shares, early, blk
-        )
-        matrix_grads = tuple(late[1:]) + unpacked(early_sum)
+            grad_wide.reshape(-1, rows, grad_wide.shape[-1]),
+            packed.reshape(head, blk, 16, 128),
+            wide,
+            (grad_scaled, grad_keyed, grad_valued),
+            early,
+            blk,
+        )
+        matrix_grads = tuple(late[1:]) + tuple(early_sum)
         packed = late[0]
     else:
         wide_sum = narrow(grad_wide, rows, blk, head).astype(f32)
+        late_grads = [mm_tn(tokens, grad_scaled), mm_tn(wide, grad_keyed), mm_tn(wide, grad_valued)]
         matrix_grads = tuple(shared_out(g) for g in late_grads + early_grads)
         packed = lax.psum_scatter(packed, ("head", "blk"), scatter_dimension=0, tiled=True)[0]
     order = (6, 7, 0, 1, 2, 8, 3, 4, 5)

time: 550 us -> 538 us (0.978)
  Pallas kernels: 505 us -> 493 us
    pallas_call x1, Pallas kernels: 38 us -> 18.4 us  [tokens_back(): pl.pallas_call(tokens_back_kernel, grid=(1 + 2 * REACH,), in_specs=[tile,...]
    pallas_call x1, Pallas kernels: 145 us -> 152 us  [reduce_to_owners(): pl.pallas_call(partial(reduce_kernel, blk, count), out_shape=[jax.ShapeDt...]
  transfers between devices with their start and end apart: 3 -> 3, of which waited for: 0 -> 0; matrix products, arithmetic and copies ran while one was open for 0% -> 0% of each run, Pallas kernels for 14% -> 11%
where the time goes in v5:
time: 538 us; the launch traced here: 533 us
  Pallas kernels  493 us (92%)
  local copies, waits for them, and re-layouts  20.3 us (4%)
  other arithmetic  11 us (2%)
  starting transfers between devices  7.65 us (1%)
    pallas_call x1, Pallas kernels, gather(): pl.pallas_call(partial(gather_kernel, blk, count), out_shape=[jax.ShapeDt...  160 us
    pallas_call x1, Pallas kernels, reduce_to_owners(): pl.pallas_call(partial(reduce_kernel, blk, count), out_shape=[jax.ShapeDt...  152 us
    pallas_call x1, Pallas kernels, middle(): pl.pallas_call(middle_kernel, grid=(2 * steps,), in_specs=[still, still,...  61.1 us
    pallas_call x1, Pallas kernels, attend_back(): pl.pallas_call(partial(attend_back_kernel, blocks), grid_spec=pltpu.Prefe...  40.5 us
    pallas_call x1, Pallas kernels, attend(): pl.pallas_call(partial(attend_kernel, blocks), grid_spec=pltpu.PrefetchSc...  28.9 us
    pallas_call x1, Pallas kernels, tokens_back(): pl.pallas_call(tokens_back_kernel, grid=(1 + 2 * REACH,), in_specs=[tile,...  18.4 us
    pallas_call x1, Pallas kernels, project(): pl.pallas_call(project_kernel, grid=(1 + 2 * REACH,), in_specs=[tile, squ...  17.1 us
    pallas_call x1, Pallas kernels, pair_sums(): pl.pallas_call(partial(pair_kernel, blk), out_shape=[jax.ShapeDtypeStruct...  15.1 us
  transfers between devices with their start and end apart: 3, of which 0 were waited for; matrix products, arithmetic and copies ran while one was open for 0% of the time, Pallas kernels for 11%

profile of v5, /device:TPU:0, one launch (start us, length us, event | category | flops | bytes accessed | tf_op | source)
XLA Modules:
  0.0 533.0 jit_solution(5616967972707552694)
XLA Ops:
  0.7 0.7 fusion.5
  1.5 2.6 convert_reduce_fusion
  4.3 0.8 stack.57
  5.1 1.3 fusion.10.refs_1_
  6.5 159.6 %gather.1 = (bf16[5,1024,768]{2,1,0:T(8,128)(2,1)}, bf16[1024,768]{1,0:T(8,128)(2,1)}, bf16[4,8,16,128]{3,2,1,0:T(8,128)(2,1)}, bf16[4,8,24,768]{3,2,1,0:T(8,128...) custom-call(bf16[1024,768]{1,0:T(8,128)(2,1)} %x_ref.1, ...), custom_call_target="tpu_custom_call" | custom-call | tf_op jit(solution)/shard_map/gather/pallas_call | solution.py:840
  166.1 0.9 slice.70
  167.0 0.8 slice.72
  168.0 0.8 dynamic-slice_subtract_fusion
  171.3 0.7 reshape.189.bi_ref
  172.0 1.3 copy-done.6
  173.3 1.3 copy-done.8
  174.6 17.1 %project.1 = (bf16[5120,768]{1,0:T(8,128)(2,1)S(1)}, bf16[5120,768]{1,0:T(8,128)(2,1)}, bf16[1024,768]{1,0:T(8,128)(2,1)S(1)}) custom-call(bf16[5120,768]{1,0:T(8,128)(2,1)} %bitcast.61, bf16[768,768]{1,0:T(8,128)(2,1)S(1)} %bitcast.57, bf16[768,768]{1,0:T(8,128)(2,1)S(1)} %bitcast.59, bf16[768,768]{1,0:T(8,128)(2,1)S(1)} %bitcast.55, ...), custom_call_target="tpu_custom_call" | custom-call | tf_op jit(solution)/shard_map/project/pallas_call | solution.py:455
  191.7 28.9 %attend.1 = (bf16[1024,768]{1,0:T(8,128)(2,1)S(1)}, bf16[3,16,512,256]{3,2,1,0:T(8,128)(2,1)}) custom-call(s32[1536]{0:T(1024)S(1)} %min.12.rows_ref, bf16[1024,768]{1,0:T(8,128)(2,1)S(1)} %get-tuple-element.61.q_ref, bf16[5120,768]{1,0:T(8,128)(2,1)S(1)} %get-tuple-element.62.k_ref, bf16[5120,768]{1,0:T(8,128)(2,1)} %get-tuple-element.63.v_ref, ...), custom_call_target="tpu_custom_call" | custom-call | tf_op jit(solution)/shard_map/attend/pallas_call | solution.py:182
  220.6 1.2 copy-done.3
  221.8 61.1 %middle.1 = (bf16[1024,768]{1,0:T(8,128)(2,1)}, f32[1024,768]{1,0:T(8,128)}, bf16[1024,768]{1,0:T(8,128)(2,1)}, bf16[768,768]{1,0:T(8,128)(2,1)}, bf16[768,3072]...) custom-call(bf16[1024,768]{1,0:T(8,128)(2,1)} %copy-done.3, ...), custom_call_target="tpu_custom_call" | custom-call | tf_op jit(solution)/shard_map/middle/pallas_call | solution.py:388
  282.9 15.1 %pair_sums.1 = (bf16[4,224,768]{2,1,0:T(8,128)(2,1)}, bf16[4,224,768]{2,1,0:T(8,128)(2,1)}, bf16[4,224,768]{2,1,0:T(8,128)(2,1)}, bf16[4,224,768]{2,1,0:T(8,128)(2,1)}) custom-call(bf16[4,8,24,768]{3,2,1,0:T(8,128)(2,1)} %bitcast.69, bf16[4,8,24,3072]{3,2,1,0:T(8,128)(2,1)} %bitcast.66, bf16[4,8,96,768]{3,2,1,0:T(8,128)(2,1)} %bitcast.67), custom_call_target="tpu_custom_call" | custom-call | tf_op jit(solution)/shard_map/pair_sums/pallas_call | solution.py:921
  298.0 2.9 collective-permute-start
  300.9 2.4 collective-permute-start.1
  303.3 2.3 collective-permute-start.2
  305.7 40.5 %attend_back.1 = (bf16[1024,768]{1,0:T(8,128)(2,1)}, bf16[5120,768]{1,0:T(8,128)(2,1)}, bf16[5120,768]{1,0:T(8,128)(2,1)}) custom-call(s32[1536]{0:T(1024)} %copy-done.11, bf16[1024,768]{1,0:T(8,128)(2,1)} %copy-done.4, bf16[1024,768]{1,0:T(8,128)(2,1)} %get-tuple-element.69.g_ref, bf16[5120,768]{1,0:T(8,128)(2,1)} %copy-done, ...), custom_call_target="tpu_custom_call" | custom-call | flops 16106127360 | bytes 104857600 | tf_op jit(solution)/shard_map/attend_back/pallas_call | solution.py:215
  346.2 1.4 copy-done.2
  347.6 18.4 %tokens_back.1 = (bf16[5120,768]{1,0:T(8,128)(2,1)}, f32[1024,768]{1,0:T(8,128)S(1)}, f32[8,768]{1,0:T(8,128)S(1)}) custom-call(bf16[5120,768]{1,0:T(8,128)(2,1)} %get-tuple-element.71.dk_ref.refs_4_, bf16[5120,768]{1,0:T(8,128)(2,1)} %get-tuple-element.72.dv_ref.refs_5_, bf16[1024,768]{1,0:T(8,128)(2,1)S(1)} %copy-done.2, bf16[768,768]{1,0:T(8,128)(2,1)S(1)} %bitcast.58, ...), custom_call_target="tpu_custom_call" | custom-call | flops 12079595520 | bytes 31457280 | tf_op jit(solution)/shard_map/tokens_back/pallas_call | solution.py:500
  366.0 1.7 copy-done.1
  368.1 0.9 copy.57
  369.0 152.1 %reduce_to_owners.1 = (f32[1024,768]{1,0:T(8,128)}, f32[16,128]{1,0:T(8,128)}, f32[24,768]{1,0:T(8,128)}, f32[24,768]{1,0:T(8,128)}, f32[24,768]{1,0:T(8,128)}, ...) custom-call(bf16[5,1024,768]{2,1,0:T(8,128)(2,1)} %bitcast.63, f32[4,8,16,128]{3,2,1,0:T(8,128)} %bitcast.70, ...), custom_call_target="tpu_custom_call" | custom-call | tf_op jit(solution)/shard_map/reduce_to_owners/pallas_call | solution.py:1330
  521.1 1.5 slice_bitcast_fusion
  522.6 1.2 slice_bitcast_fusion.3
  523.8 5.0 add.87
  528.8 0.6 copy.68
  530.1 0.6 copy.70
  531.4 0.7 copy.72
  532.1 0.7 copy.73
  (83 shorter events, 4.6 us)
Async XLA Ops:
  166.1 5.9 %copy-start.5 = (bf16[4,8,24,768]{3,2,1,0:T(8,128)(2,1)S(1)}, bf16[4,8,24,768]{3,2,1,0:T(8,128)(2,1)}, u32[]{:S(2)}) copy-start(bf16[4,8,24,768]{3,2,1,0:T(8,128)(2,1)} %get-tuple-element.59) | copy-start | bytes 3538948
  170.8 20.9 %copy-start.11 = (s32[1536]{0:T(1024)}, s32[1536]{0:T(1024)S(1)}, u32[]{:S(2)}) copy-start(s32[1536]{0:T(1024)S(1)} %min.12.rows_ref) | copy-start | bytes 18436
  171.3 20.3 %copy-start.10 = (f32[8,768]{1,0:T(8,128)}, f32[8,768]{1,0:T(8,128)S(1)}, u32[]{:S(2)}) copy-start(f32[8,768]{1,0:T(8,128)S(1)} %reshape.188.vec_ref) | copy-start | bytes 73732
  172.0 1.3 copy-start.6
  173.3 1.3 copy-start.8
  191.6 29.0 %copy-start = (bf16[5120,768]{1,0:T(8,128)(2,1)}, bf16[5120,768]{1,0:T(8,128)(2,1)S(1)}, u32[]{:S(2)}) copy-start(bf16[5120,768]{1,0:T(8,128)(2,1)S(1)} %get-tuple-element.62.k_ref) | copy-start | bytes 23592964
  191.6 29.0 %copy-start.4 = (bf16[1024,768]{1,0:T(8,128)(2,1)}, bf16[1024,768]{1,0:T(8,128)(2,1)S(1)}, u32[]{:S(2)}) copy-start(bf16[1024,768]{1,0:T(8,128)(2,1)S(1)} %get-tuple-element.61.q_ref) | copy-start | bytes 4718596
  220.6 1.2 copy-start.3
  298.0 71.0 %collective-permute-start = (bf16[4,224,768]{2,1,0:T(8,128)(2,1)}, bf16[4,224,768]{2,1,0:T(8,128)(2,1)}, u32[]{:S(2)}, u32[]{:S(2)}) collective-permute-start(bf16[4,224,768]{2,1,0:T(8,128)(2,1)} %get-tuple-element.84), channel_id=1, source_target_pairs={{0,2},{1,3},{2,4},{3,5},{4,6},{5,7},{6,0},{7,1},{8,10},{9,11},{10,... | collective-permute-start | bytes 4128776 | tf_op jit(solution)/shard_map/ppermute | solution.py:948
  300.9 68.1 %collective-permute-start.1 = (bf16[4,224,768]{2,1,0:T(8,128)(2,1)}, bf16[4,224,768]{2,1,0:T(8,128)(2,1)}, u32[]{:S(2)}, u32[]{:S(2)}) collective-permute-start(bf16[4,224,768]{2,1,0:T(8,128)(2,1)} %get-tuple-element.85), channel_id=1, source_target_pairs={{0,4},{1,5},{2,6},{3,7},{4,0},{5,1},{6,2},{7,3},{8,12},{9,13},{10,... | collective-permute-start | bytes 4128776 | tf_op jit(solution)/shard_map/ppermute | solution.py:948
  303.3 65.7 %collective-permute-start.2 = (bf16[4,224,768]{2,1,0:T(8,128)(2,1)}, bf16[4,224,768]{2,1,0:T(8,128)(2,1)}, u32[]{:S(2)}, u32[]{:S(2)}) collective-permute-start(bf16[4,224,768]{2,1,0:T(8,128)(2,1)} %get-tuple-element.86), channel_id=1, source_target_pairs={{0,6},{1,7},{2,0},{3,1},{4,2},{5,3},{6,4},{7,5},{8,14},{9,15},{10,... | collective-permute-start | bytes 4128776 | tf_op jit(solution)/shard_map/ppermute | solution.py:948
  305.7 40.5 %copy-start.7 = (bf16[4,8,24,768]{3,2,1,0:T(8,128)(2,1)S(1)}, bf16[4,8,24,768]{3,2,1,0:T(8,128)(2,1)}, u32[]{:S(2)}) copy-start(bf16[4,8,24,768]{3,2,1,0:T(8,128)(2,1)} %get-tuple-element.57) | copy-start | bytes 3538948
  305.7 40.5 %copy-start.9 = (bf16[4,8,24,768]{3,2,1,0:T(8,128)(2,1)S(1)}, bf16[4,8,24,768]{3,2,1,0:T(8,128)(2,1)}, u32[]{:S(2)}) copy-start(bf16[4,8,24,768]{3,2,1,0:T(8,128)(2,1)} %get-tuple-element.58) | copy-start | bytes 3538948
  305.7 40.5 %copy-start.12 = (f32[1024,768]{1,0:T(8,128)S(1)}, f32[1024,768]{1,0:T(8,128)}, u32[]{:S(2)}) copy-start(f32[1024,768]{1,0:T(8,128)} %get-tuple-element.74.first_ref) | copy-start | bytes 9437188
  346.2 1.4 copy-start.2
  347.6 20.1 %copy-start.19 = (f32[8,768]{1,0:T(8,128)S(1)}, f32[8,768]{1,0:T(8,128)}, u32[]{:S(2)}) copy-start(f32[8,768]{1,0:T(8,128)} %get-tuple-element.77) | copy-start | bytes 73732
  347.6 20.2 %copy-start.20 = (f32[4,1,768]{2,1,0:T(1,128)S(1)}, f32[4,1,768]{2,1,0:T(1,128)}, u32[]{:S(2)}) copy-start(f32[4,1,768]{2,1,0:T(1,128)} %get-tuple-element.79) | copy-start | bytes 36868
  366.0 1.7 copy-start.1
  523.8 5.0 copy-start.18
  523.8 5.6 %copy-start.17 = (f32[24,768]{1,0:T(8,128)S(1)}, f32[24,768]{1,0:T(8,128)}, u32[]{:S(2)}) copy-start(f32[24,768]{1,0:T(8,128)} %get-tuple-element.133) | copy-start | bytes 221188
  523.8 6.3 %copy-start.16 = (f32[24,768]{1,0:T(8,128)S(1)}, f32[24,768]{1,0:T(8,128)}, u32[]{:S(2)}) copy-start(f32[24,768]{1,0:T(8,128)} %get-tuple-element.134) | copy-start | bytes 221188
  523.8 6.9 %copy-start.15 = (f32[24,768]{1,0:T(8,128)S(1)}, f32[24,768]{1,0:T(8,128)}, u32[]{:S(2)}) copy-start(f32[24,768]{1,0:T(8,128)} %get-tuple-element.135) | copy-start | bytes 221188
  523.8 7.5 %copy-start.14 = (f32[24,3072]{1,0:T(8,128)S(1)}, f32[24,3072]{1,0:T(8,128)}, u32[]{:S(2)}) copy-start(f32[24,3072]{1,0:T(8,128)} %get-tuple-element.136) | copy-start | bytes 884740
  523.8 8.2 %copy-start.13 = (f32[96,768]{1,0:T(8,128)S(1)}, f32[96,768]{1,0:T(8,128)}, u32[]{:S(2)}) copy-start(f32[96,768]{1,0:T(8,128)} %get-tuple-element.137) | copy-start | bytes 884740

commit v6 on v5

--- a/solution.py
+++ b/solution.py
@@ -13,8 +13,8 @@
 TILES = 5 + RANDOM
 REACH = 2
 GROUP = 4
-FORWARD_BLOCKS = 4
-BACKWARD_BLOCKS = 4
+FORWARD_BLOCKS = 8
+BACKWARD_BLOCKS = 8
 ROWS = 256
 PIECE = 768
 
@@ -128,6 +128,7 @@
     dq_ref,
     dk_ref,
     dv_ref,
+    sums_ref,
     dk_sum,
     dv_sum,
 ):
@@ -135,6 +136,7 @@
 
     @pl.when(step == 0)
     def _():
+        sums_ref[...] = jnp.zeros_like(sums_ref)
         dk_sum[...] = jnp.zeros_like(dk_sum)
         dv_sum[...] = jnp.zeros_like(dv_sum)
 
@@ -166,10 +168,13 @@
                         mine, rows[:, first : first + 2 * HEAD_DIM], 0.0
                     )
 
+    sums_ref[6:7, :] += jnp.sum(dq_ref[...].astype(f32), axis=0, keepdims=True)
+
     @pl.when(step == blocks // BACKWARD_BLOCKS - 1)
     def _():
         dk_ref[...] = dk_sum[...].astype(bf16)
         dv_ref[...] = dv_sum[...].astype(bf16)
+        sums_ref[7:8, :] = jnp.sum(dv_ref[...].astype(f32), axis=0, keepdims=True)
 
 
 def attend(rows, queries, keys, values, bases, docs):
@@ -224,13 +229,14 @@
                 table,
                 pl.BlockSpec((1, some, TILES * BLOCK, cols), lambda g, i, r: (g, i, 0, 0)),
             ],
-            out_specs=[tile, table, table],
+            out_specs=[tile, table, table, pl.BlockSpec((8, cols), lambda g, i, r: (0, g))],
             scratch_shapes=[pltpu.VMEM((ext, cols), f32), pltpu.VMEM((ext, cols), f32)],
         ),
         out_shape=[
             jax.ShapeDtypeStruct((tokens, width), bf16),
             jax.ShapeDtypeStruct((ext, width), bf16),
             jax.ShapeDtypeStruct((ext, width), bf16),
+            jax.ShapeDtypeStruct((8, width), f32),
         ],
         compiler_params=pltpu.CompilerParams(vmem_limit_bytes=56 << 20),
         cost_estimate=pl.CostEstimate(
@@ -458,63 +464,9 @@
         in_specs=[tile, square, square, square, pl.BlockSpec((8, width), lambda i: (0, 0))],
         out_specs=[tile, tile, still],
         out_shape=[table, table, jax.ShapeDtypeStruct((rows, width), bf16)],
-        compiler_params=pltpu.CompilerParams(vmem_limit_bytes=40 << 20),
+        compiler_params=pltpu.CompilerParams(vmem_limit_bytes=60 << 20),
         name="project",
     )(wide, w_key, w_value, w_query, vectors)
-
-
-def tokens_back_kernel(
-    dk_ref, dv_ref, dq_ref, wk_ref, wv_ref, wq_ref, first_ref, dx_ref, rows_ref, sums_ref
-):
-    step = pl.program_id(0)
-    rows = dx_ref.shape[0]
-    slices = [pl.ds(t * ROWS, ROWS) for t in range(rows // ROWS)]
-
-    def summed(ref):
-        return jnp.sum(ref[...].astype(f32), axis=0, keepdims=True)
-
-    @pl.when(step == 0)
-    def _():
-        sums_ref[...] = jnp.zeros_like(sums_ref)
-
-    for s in slices:
-        dx_ref[s, :] = (
-            mm_nt(dk_ref[s, :], wk_ref[...]) + mm_nt(dv_ref[s, :], wv_ref[...])
-        ).astype(bf16)
-    sums_ref[7:8, :] += summed(dv_ref)
-
-    @pl.when(step == REACH)
-    def _():
-        for s in slices:
-            rows_ref[s, :] = first_ref[s, :] + mm_nt(dq_ref[s, :], wq_ref[...])
-        sums_ref[6:7, :] = summed(dq_ref)
-
-
-def tokens_back(grad_keyed, grad_valued, grad_scaled, w_key, w_value, w_query, grad_first):
-    rows, width = grad_scaled.shape
-    one = pl.Buffered(1)
-    tile = pl.BlockSpec((rows, width), lambda i: (i, 0))
-    still = pl.BlockSpec((rows, width), lambda i: (0, 0), pipeline_mode=one)
-    square = pl.BlockSpec((width, width), lambda i: (0, 0), pipeline_mode=one)
-    few = pl.BlockSpec((8, width), lambda i: (0, 0))
-    return pl.pallas_call(
-        tokens_back_kernel,
-        grid=(1 + 2 * REACH,),
-        in_specs=[tile, tile, still, square, square, square, still],
-        out_specs=[tile, still, few],
-        out_shape=[
-            jax.ShapeDtypeStruct(grad_keyed.shape, bf16),
-            jax.ShapeDtypeStruct((rows, width), f32),
-            jax.ShapeDtypeStruct((8, width), f32),
-        ],
-        compiler_params=pltpu.CompilerParams(vmem_limit_bytes=40 << 20),
-        cost_estimate=pl.CostEstimate(
-            flops=4 * grad_keyed.shape[0] * width * width,
-            bytes_accessed=30 << 20,
-            transcendentals=0,
-        ),
-        name="tokens_back",
-    )(grad_keyed, grad_valued, grad_scaled, w_key, w_value, w_query, grad_first)
 
 
 def tile_plan(segment_ids, random_blocks, tokens):
@@ -604,6 +556,7 @@
 MESH = pl.DeviceIdType.MESH
 NEAR_SLOT = (1, 0, 4, 3)
 FAR_SLOT = (0, None, None, 4)
+WORK_ORDER = ((3, 1, 0, 4, 2), (0, 4, 3, 1, 2), (4, 0, 1, 3, 2), (1, 3, 4, 0, 2))
 
 
 def remote(source, target, send, recv, head, blk):
@@ -859,14 +812,11 @@
 
 
 def pair_kernel(blk, *refs):
-    grads, outs, (held, arrived), (load, send, recv) = (
-        refs[:3],
-        refs[3:7],
-        (refs[7:10], refs[10:13]),
-        refs[13:],
-    )
+    chips = blk // CORES
+    grads, firsts, seconds = refs[:3], refs[3 : 3 + chips], refs[3 + chips : 3 + 2 * chips]
+    rest = refs[3 + 2 * chips :]
+    held, arrived, (load, send, recv) = rest[:3], rest[3:6], rest[6:]
     h, b = lax.axis_index("head"), lax.axis_index("blk")
-    chips = blk // CORES
     chip, core = b // CORES, b % CORES
     sibling = chip * CORES + 1 - core
 
@@ -901,10 +851,10 @@
             )
             parts = [inner[:, m * 768 : (m + 1) * 768] for m in range(4)]
             spare = jnp.zeros((8, 768), f32)
-            outs[e][n, 0:48] = jnp.concatenate([attn, parts[0]], axis=0).astype(bf16)
-            outs[e][n, 48:96] = jnp.concatenate(parts[1:3], axis=0).astype(bf16)
-            outs[e][n, 96:128] = jnp.concatenate([parts[3], spare], axis=0).astype(bf16)
-            outs[e][n, 128:224] = outer.astype(bf16)
+            firsts[e][n, 0:48] = jnp.concatenate([attn, parts[0]], axis=0).astype(bf16)
+            firsts[e][n, 48:96] = jnp.concatenate(parts[1:3], axis=0).astype(bf16)
+            seconds[e][n, 0:32] = jnp.concatenate([parts[3], spare], axis=0).astype(bf16)
+            seconds[e][n, 32:128] = outer.astype(bf16)
             return carry
 
         lax.fori_loop(0, LINE, one, 0)
@@ -918,11 +868,12 @@
     shard = [g.shape[2:] for g in grads]
     dma = pltpu.SemaphoreType.DMA
     inside = pl.BlockSpec(memory_space=pltpu.VMEM)
-    return pl.pallas_call(
+    outs = pl.pallas_call(
         partial(pair_kernel, blk),
-        out_shape=[jax.ShapeDtypeStruct((LINE, 224, 768), bf16)] * chips,
+        out_shape=[jax.ShapeDtypeStruct((LINE, 96, 768), bf16)] * chips
+        + [jax.ShapeDtypeStruct((LINE, 128, 768), bf16)] * chips,
         in_specs=[pl.BlockSpec(memory_space=pl.ANY)] * 3,
-        out_specs=[inside] * chips,
+        out_specs=[inside] * 2 * chips,
         scratch_shapes=[pltpu.VMEM((chips, LINE) + s, bf16) for s in shard] * 2
         + [dma((3, chips))] * 3,
         compiler_params=pltpu.CompilerParams(
@@ -930,6 +881,7 @@
         ),
         name="pair_sums",
     )(*grads)
+    return outs[:chips], outs[chips:]
 
 
 def over_plane(sums, blk, head):
@@ -950,35 +902,70 @@
 
 
 def reduce_kernel(blk, count, *refs):
-    dx_ref, small_ref, wide_ref, sides_refs = refs[0], refs[1], refs[2], refs[3:6]
-    early = refs[6 : 6 + blk // CORES]
-    rest = refs[6 + blk // CORES :]
+    small_ref, wide_ref, query_ref, key_ref, value_ref = refs[:5]
+    weights, first_ref = refs[5:8], refs[8]
+    chips = blk // CORES
+    early, packed = refs[9 : 9 + chips], refs[9 + chips : 9 + 2 * chips]
+    rest = refs[9 + 2 * chips :]
     sum_ref, outs, early_outs = rest[0], rest[1 : 1 + count], rest[1 + count : 4 + count]
     early_sum, early_in, es, er = rest[4 + count : 8 + count]
     totals, (wide_in, key_in, value_in, fed) = rest[8 + count : 11 + count], rest[11 + count : 15 + count]
     rest = rest[15 + count :]
-    held, from_core, from_chip, from_line = (rest[n * count : (n + 1) * count] for n in range(4))
-    line, arrived, aside = rest[4 * count : 4 * count + 3]
-    load, ss, sr, cs, cr, zs, zr, xl, us, ur, ds, dr, ns, nr, fs, fr = rest[4 * count + 3 :]
+    weight_in, early_here, loaded = rest[:3], rest[3 : 3 + chips], rest[3 + chips]
+    rest = rest[4 + chips :]
+    extra = count
+    held, from_core, rest = rest[: count + 1], rest[count + 1 : 2 * count + 1], rest[2 * count + 1 :]
+    from_chip, from_line, rest = rest[: count + 1], rest[count + 1 : 2 * count + 2], rest[2 * count + 2 :]
+    frame, arrived, aside = rest[:3]
+    load, ss, sr, cs, cr, zs, zr, us, ur, ds, dr, ns, nr, fs, fr = rest[3:]
     grads = (small_ref,) + tuple(totals)
     h, b = lax.axis_index("head"), lax.axis_index("blk")
-    chips = blk // CORES
     chip, core = b // CORES, b % CORES
     sibling = chip * CORES + 1 - core
-    rows = dx_ref.shape[1] // PIECES_BACK
+    chunk_rows = sum_ref.shape[0]
+    rows = chunk_rows // PIECES_BACK
 
     feed_rows = wide_in.shape[1]
-    feeds = wide_ref.shape[0] // feed_rows
-    per_chunk = feeds // (1 + 2 * REACH)
-    query_ref, key_ref, value_ref = sides_refs
-
-    def feed(step, slot):
-        some = pl.ds(step * feed_rows, feed_rows)
+    halves = chunk_rows // feed_rows
+    slots = 1 + 2 * REACH
+
+    def slot_at(n):
+        slot = REACH
+        for hh in range(LINE):
+            for k in range(slots):
+                slot = jnp.where((h == hh) & (n == k), WORK_ORDER[hh][k], slot)
+        return slot
+
+    def feed(slot, half):
+        some = pl.ds(slot * chunk_rows + half * feed_rows, feed_rows)
         return [
-            pltpu.make_async_copy(source.at[some], target.at[slot], fed.at[n, slot])
+            pltpu.make_async_copy(source.at[some], target.at[half], fed.at[n, half])
             for n, (source, target) in enumerate(
                 ((wide_ref, wide_in), (key_ref, key_in), (value_ref, value_in))
             )
+        ]
+
+    def feed_queries(half):
+        some = pl.ds(half * feed_rows, feed_rows)
+        wide_some = pl.ds(REACH * chunk_rows + half * feed_rows, feed_rows)
+        return [
+            pltpu.make_async_copy(wide_ref.at[wide_some], wide_in.at[half], fed.at[0, half]),
+            pltpu.make_async_copy(query_ref.at[some], key_in.at[half], fed.at[1, half]),
+        ]
+
+    def start(copies):
+        for copy in copies:
+            copy.start()
+
+    def wait(copies):
+        for copy in copies:
+            copy.wait()
+
+    def standing():
+        pairs = list(zip(weights, weight_in)) + list(zip(early, early_here)) + [(first_ref, sum_ref)]
+        return [
+            pltpu.make_async_copy(source, target, loaded.at[n])
+            for n, (source, target) in enumerate(pairs)
         ]
 
     def add_product(total, left, right, fresh):
@@ -990,46 +977,49 @@
             here = pl.ds(n * lines, lines)
             total[here] = part if fresh else total[here] + part
 
-    def weigh():
-        for copy in feed(0, 0):
-            copy.start()
-        for n in (1, 2):
-            totals[n][...] = jnp.zeros_like(totals[n])
-
-        def one(step, carry):
-            slot = step % 2
-
-            @pl.when(step + 1 < feeds)
-            def _():
-                for copy in feed(step + 1, 1 - slot):
-                    copy.start()
-
-            for copy in feed(step, slot):
-                copy.wait()
-            add_product(totals[1], wide_in[slot], key_in[slot], False)
-            add_product(totals[2], wide_in[slot], value_in[slot], False)
-            return carry
-
-        lax.fori_loop(0, feeds, one, 0)
-        for n in range(per_chunk):
-            copies = [
-                pltpu.make_async_copy(
-                    wide_ref.at[pl.ds((REACH * per_chunk + n) * feed_rows, feed_rows)],
-                    wide_in.at[0],
-                    fed.at[0, 0],
-                ),
-                pltpu.make_async_copy(
-                    query_ref.at[pl.ds(n * feed_rows, feed_rows)], key_in.at[0], fed.at[1, 0]
-                ),
-            ]
-            for copy in copies:
-                copy.start()
-            for copy in copies:
-                copy.wait()
-            add_product(totals[0], wide_in[0], key_in[0], n == 0)
+    def work(n, carry):
+        slot = slot_at(n)
+        for half in range(halves):
+            if half + 1 < halves:
+                start(feed(slot, half + 1))
+            else:
+
+                @pl.when(n + 1 < slots)
+                def _():
+                    start(feed(slot_at(n + 1), 0))
+
+            wait(feed(slot, half))
+            for t in range(feed_rows // ROWS):
+                s = pl.ds(t * ROWS, ROWS)
+                grad = mm_nt(key_in[half, s], weight_in[1][...]) + mm_nt(
+                    value_in[half, s], weight_in[2][...]
+                )
+                frame[slot, pl.ds(half * feed_rows + t * ROWS, ROWS)] = grad.astype(bf16)
+            add_product(totals[1], wide_in[half], key_in[half], False)
+            add_product(totals[2], wide_in[half], value_in[half], False)
+        for hh in range(LINE):
+            for k in range(slots):
+                pl.when((h == hh) & (n == k))(partial(send_off, hh, WORK_ORDER[hh][k]))
+        return carry
+
+    def query_work():
+        start(feed_queries(0))
+        for half in range(halves):
+            if half + 1 < halves:
+                start(feed_queries(half + 1))
+            wait(feed_queries(half))
+            for t in range(feed_rows // ROWS):
+                s = pl.ds(t * ROWS, ROWS)
+                here = pl.ds(half * feed_rows + t * ROWS, ROWS)
+                sum_ref[here] += mm_nt(key_in[half, s], weight_in[0][...])
+            add_product(totals[0], wide_in[half], key_in[half], half == 0)
 
     def mine(a, k):
         return pltpu.make_async_copy(grads[a].at[:, k * CORES + core], held[a].at[k], load.at[a, k])
+
+    def mine_packed(e):
+        target = held[extra].at[(chip + e) % chips]
+        return pltpu.make_async_copy(packed[e], target, load.at[extra, e])
 
     def across(a, k):
         return remote(
@@ -1112,8 +1102,8 @@
 
     def early_to_line():
         def one(n, carry):
-            total = early[0][n].astype(f32)
-            for ref in early[1:]:
+            total = early_here[0][n].astype(f32)
+            for ref in early_here[1:]:
                 total = total + ref[n].astype(f32)
             early_sum[n] = total.astype(bf16)
             return carry
@@ -1129,10 +1119,16 @@
         for d in range(1, LINE):
             total = total + early_in[d - 1].astype(f32)
         attn_ref, inner_ref, outer_ref = early_outs
+        inner_ref[:, 3 * 768 :] = total[:24]
+        outer_ref[...] = total[32:]
+        for d in range(1, LINE):
+            along(extra, d).wait_recv()
+        total = held[extra][chip, h].astype(f32)
+        for d in range(1, LINE):
+            total = total + from_line[extra][d - 1].astype(f32)
         attn_ref[...] = total[:24]
-        for n in range(4):
+        for n in range(3):
             inner_ref[:, n * 768 : (n + 1) * 768] = total[24 * (n + 1) : 24 * (n + 2)]
-        outer_ref[...] = total[128:]
 
     def part(p):
         return pl.ds(p * rows, rows)
@@ -1152,17 +1148,14 @@
 
     def slot_of(hh, j):
         slot = 2 + j - hh
-        return slot if 0 <= slot < 5 else None
-
-    def fetch(hh, j):
-        return pltpu.make_async_copy(dx_ref.at[slot_of(hh, j)], line.at[j], xl.at[j])
+        return slot if 0 <= slot < slots else slots
 
     def arrival(hh, j, upward):
         return arrived.at[LINE if j == hh and not upward else j]
 
     def up(hh, j, p):
         return remote(
-            piece(line.at[j], p),
+            piece(frame.at[slot_of(hh, j)], p),
             piece(arrival(hh + 1, j, True), p),
             us.at[j, p],
             ur.at[j, p],
@@ -1176,7 +1169,7 @@
 
     def down(hh, j, p):
         return remote(
-            piece(line.at[j], p),
+            piece(frame.at[slot_of(hh, j)], p),
             piece(arrival(hh - 1, j, False), p),
             ds.at[j, p],
             dr.at[j, p],
@@ -1198,7 +1191,7 @@
     def side(hh, slot, n, send, recv, p):
         target = (b + blk - 1) % blk if hh < 2 else (b + 1) % blk
         return remote(
-            piece(dx_ref.at[slot], p), piece(aside.at[n], p), send.at[p], recv.at[p], h, target
+            piece(frame.at[slot], p), piece(aside.at[n], p), send.at[p], recv.at[p], h, target
         )
 
     def sends_side(hh):
@@ -1207,25 +1200,18 @@
     def gets_side(hh):
         return b < blk - 1 if hh < 2 else b > 0
 
-    def begin(hh):
+    def send_off(hh, slot):
         @pl.when(sends_side(hh))
         def _():
             for p in range(PIECES_BACK):
-                for slot, _, n, send, recv in side_parts(hh):
-                    side(hh, slot, n, send, recv, p).start()
-
-        for j in range(LINE):
-            if slot_of(hh, j) is not None:
-                fetch(hh, j).start()
-        for j in range(LINE):
-            if slot_of(hh, j) is not None:
-                fetch(hh, j).wait()
-            else:
-                line[j] = jnp.zeros(line.shape[1:], line.dtype)
+                for side_slot, _, n, send, recv in side_parts(hh):
+                    if side_slot == slot:
+                        side(hh, slot, n, send, recv, p).start()
+
         for p in range(PIECES_BACK):
-            if hh == 0:
+            if hh == 0 and slot == slot_of(0, 1):
                 up(hh, 1, p).start()
-            if hh == LINE - 1:
+            if hh == LINE - 1 and slot == slot_of(LINE - 1, 2):
                 down(hh, 2, p).start()
 
     def take_sides(hh):
@@ -1236,7 +1222,7 @@
                 def _(j=j, n=n, send=send, recv=recv):
                     here = piece(aside.at[n], p)
                     remote(here, here, send.at[p], recv.at[p], h, (b + 1) % blk).wait_recv()
-                    add_rows(line, j, aside, n, p)
+                    add_rows(frame, slot_of(hh, j), aside, n, p)
 
                 if hh == 0:
                     up(hh, j, p).start()
@@ -1252,7 +1238,7 @@
         for p in range(PIECES_BACK):
             for j, upward in moves:
                 (up_arrives if upward else down_arrives)(hh, j, p).wait_recv()
-                add_rows(line, j, arrived, j, p)
+                add_rows(frame, slot_of(hh, j), arrived, j, p)
                 (up if upward else down)(hh, j, p).start()
 
     def finish(hh):
@@ -1267,7 +1253,7 @@
 
             def one(step, carry, p=p, sources=tuple(sources)):
                 some = pl.ds(p * rows + step * 64, 64)
-                total = line[hh, some].astype(f32)
+                total = sum_ref[some] + frame[REACH, some].astype(f32)
                 for n in sources:
                     total = total + arrived[n, some].astype(f32)
                 sum_ref[some] = total
@@ -1287,12 +1273,23 @@
                 for slot, _, n, send, recv in side_parts(hh):
                     side(hh, slot, n, send, recv, p).wait_send()
 
+    start(feed(slot_at(0), 0))
+    start(standing())
     for k in range(chips):
         mine(0, k).start()
+        mine_packed(k).start()
+    frame[slots] = jnp.zeros(frame.shape[1:], frame.dtype)
+    for n in (1, 2):
+        totals[n][...] = jnp.zeros_like(totals[n])
     greet_plane_and_line(h, b, blk)
-    at_each_head(h, begin)
+    wait(standing())
     early_to_line()
-    weigh()
+    lax.fori_loop(0, slots, work, 0)
+    query_work()
+    for e in range(chips):
+        mine_packed(e).wait()
+    for e in range(1, chips):
+        over(extra, e).start()
     for a in range(count):
         for k in range(chips):
             across(a, k).start()
@@ -1300,7 +1297,7 @@
     for a in range(count):
         to_chips(a)
     at_each_head(h, pass_on)
-    for a in range(count):
+    for a in range(count + 1):
         to_line(a)
     at_each_head(h, finish)
     early_to_owner()
@@ -1311,28 +1308,30 @@
     for a in range(count):
         for k in range(chips):
             across(a, k).wait_send()
+    for a in range(count + 1):
         for e in range(1, chips):
             over(a, e).wait_send()
         for d in range(1, LINE):
             along(a, d).wait_send()
 
 
-def reduce_to_owners(wide_grad, small, wide, projected, early, blk):
-    _, rows, width = wide_grad.shape
+def reduce_to_owners(small, wide, projected, weights, first, early, packed, blk):
+    rows, width = first.shape
     count, chips = 4, blk // CORES
     anywhere = pl.BlockSpec(memory_space=pl.ANY)
     inside = pl.BlockSpec(memory_space=pltpu.VMEM)
     dma = pltpu.SemaphoreType.DMA
     square = (width // (LINE * blk), width)
     shard = [small.shape[2:]] + [square] * 3
-    kinds = [f32] + [bf16] * 3
+    kinds = [f32] + [bf16] * 4
+    travels = shard + [packed[0].shape[1:]]
     early_shapes = ((24, 768), (24, 3072), (96, 768))
     outs = pl.pallas_call(
         partial(reduce_kernel, blk, count),
         out_shape=[jax.ShapeDtypeStruct((rows, width), f32)]
         + [jax.ShapeDtypeStruct(s, f32) for s in shard]
         + [jax.ShapeDtypeStruct(s, f32) for s in early_shapes],
-        in_specs=[anywhere] * 6 + [inside] * chips,
+        in_specs=[anywhere] * (9 + 2 * chips),
         out_specs=[inside] * (4 + count),
         scratch_shapes=[
             pltpu.VMEM(early[0].shape, bf16),
@@ -1343,26 +1342,28 @@
         + [pltpu.VMEM((LINE, blk) + square, f32)] * 3
         + [pltpu.VMEM((2, rows // 2, width), bf16)] * 3
         + [dma((3, 2))]
-        + [pltpu.VMEM((chips, LINE) + s, t) for s, t in zip(shard, kinds)]
+        + [pltpu.VMEM((width, width), bf16)] * 3
+        + [pltpu.VMEM(early[0].shape, bf16)] * chips
+        + [dma((4 + chips,))]
+        + [pltpu.VMEM((chips, LINE) + s, t) for s, t in zip(travels, kinds)]
         + [pltpu.VMEM((chips, LINE) + s, f32) for s in shard]
-        + [pltpu.VMEM((chips - 1, LINE) + s, t) for s, t in zip(shard, kinds)]
-        + [pltpu.VMEM((LINE - 1,) + s, t) for s, t in zip(shard, kinds)]
+        + [pltpu.VMEM((chips - 1, LINE) + s, t) for s, t in zip(travels, kinds)]
+        + [pltpu.VMEM((LINE - 1,) + s, t) for s, t in zip(travels, kinds)]
         + [
-            pltpu.VMEM((LINE, rows, width), bf16),
+            pltpu.VMEM((2 + 2 * REACH, rows, width), bf16),
             pltpu.VMEM((LINE + 1, rows, width), bf16),
             pltpu.VMEM((2, rows, width), bf16),
         ]
-        + [dma((count, chips))] * 3
-        + [dma((count, chips - 1))] * 2
-        + [dma((count, LINE - 1))] * 2
-        + [dma((LINE,))]
+        + [dma((count + 1, chips))] * 3
+        + [dma((count + 1, chips - 1))] * 2
+        + [dma((count + 1, LINE - 1))] * 2
         + [dma((LINE, PIECES_BACK))] * 4
         + [dma((PIECES_BACK,))] * 4,
         compiler_params=pltpu.CompilerParams(
             collective_id=1, has_side_effects=True, vmem_limit_bytes=62 << 20
         ),
         name="reduce_to_owners",
-    )(wide_grad, small, wide, *projected, *early)
+    )(small, wide, *projected, *weights, first, *early, *packed)
     return outs[0], outs[1:-3], outs[-3:]
 
 
@@ -1427,14 +1428,10 @@
 
     early_grads = [grad_w_attn, grad_w_inner, grad_w_outer]
     if by_kernel:
-        early = over_plane(
-            pair_sums([g.reshape(head, blk, -1, g.shape[-1]) for g in early_grads], blk), blk, head
-        )
-    grad_scaled, grad_keyed, grad_valued = attend_back(
+        halves, early = pair_sums([g.reshape(head, blk, -1, g.shape[-1]) for g in early_grads], blk)
+        early = over_plane(early, blk, head)
+    grad_scaled, grad_keyed, grad_valued, sums_qv = attend_back(
         rows_of, queries, grad_attended, keys, values, probs
-    )
-    grad_wide, grad_rows, sums_qv = tokens_back(
-        grad_keyed, grad_valued, grad_scaled, w_key, w_value, w_query, grad_first_sum
     )
     sums = jnp.concatenate([sums_d[:6], sums_qv[6:]])
     sums = jnp.transpose(sums.reshape(8, head * blk, -1), (1, 0, 2))
@@ -1447,24 +1444,31 @@
         axis=1,
     )
     if by_kernel:
-        wide_sum, late, early_sum = reduce_to_owners(
-            grad_wide.reshape(-1, rows, grad_wide.shape[-1]),
+        grad_tokens, late, early_sum = reduce_to_owners(
             packed.reshape(head, blk, 16, 128),
             wide,
             (grad_scaled, grad_keyed, grad_valued),
+            (w_query, w_key, w_value),
+            grad_first_sum,
             early,
+            halves,
             blk,
         )
         matrix_grads = tuple(late[1:]) + tuple(early_sum)
         packed = late[0]
     else:
-        wide_sum = narrow(grad_wide, rows, blk, head).astype(f32)
+        grad_wide = (mm_nt(grad_keyed, w_key) + mm_nt(grad_valued, w_value)).astype(bf16)
+        grad_tokens = (
+            grad_first_sum
+            + mm_nt(grad_scaled, w_query)
+            + narrow(grad_wide, rows, blk, head).astype(f32)
+        )
         late_grads = [mm_tn(tokens, grad_scaled), mm_tn(wide, grad_keyed), mm_tn(wide, grad_valued)]
         matrix_grads = tuple(shared_out(g) for g in late_grads + early_grads)
         packed = lax.psum_scatter(packed, ("head", "blk"), scatter_dimension=0, tiled=True)[0]
     order = (6, 7, 0, 1, 2, 8, 3, 4, 5)
     vector_grads = tuple(packed[n, : v.shape[0]] for n, v in zip(order, vectors))
-    return (result, grad_rows + wide_sum) + matrix_grads + vector_grads
+    return (result, grad_tokens) + matrix_grads + vector_grads
 
 
 def solution(mesh):

time: 538 us -> 514 us (0.955); the launches traced: 533 us -> 515 us
  Pallas kernels: 493 us -> 474 us
  local copies, waits for them, and re-layouts: 20.3 us -> 25.9 us
    pallas_call x1 -> x0, Pallas kernels: 18.4 us -> none  [tokens_back(): pl.pallas_call(tokens_back_kernel, grid=(1 + 2 * REACH,), in_specs=[tile,...]
    pallas_call x1, Pallas kernels: 28.9 us -> 23.2 us  [attend(): pl.pallas_call(partial(attend_kernel, blocks), grid_spec=pltpu.PrefetchSc...]
    unnamed x48 -> x35, local copies, waits for them, and re-layouts: 10.8 us -> 14.7 us
  transfers between devices with their start and end apart: 3 -> 3, of which waited for: 0 -> 0; matrix products, arithmetic and copies ran while one was open for 0% -> 0% of each run, Pallas kernels for 11% -> 8%
where the time goes in v6:
time: 514 us; the launch traced here: 515 us
  Pallas kernels  474 us (92%)
  local copies, waits for them, and re-layouts  25.9 us (5%)
  starting transfers between devices  7.64 us (1%)
  other arithmetic  5.99 us (1%)
    pallas_call x1, Pallas kernels, gather(): pl.pallas_call(partial(gather_kernel, blk, count), out_shape=[jax.ShapeDt...  160 us
    pallas_call x1, Pallas kernels, reduce_to_owners(): pl.pallas_call(partial(reduce_kernel, blk, count), out_shape=[jax.ShapeDt...  154 us
    pallas_call x1, Pallas kernels, middle(): pl.pallas_call(middle_kernel, grid=(2 * steps,), in_specs=[still, still,...  64.3 us
    pallas_call x1, Pallas kernels, attend_back(): pl.pallas_call(partial(attend_back_kernel, blocks), grid_spec=pltpu.Prefe...  39.2 us
    pallas_call x1, Pallas kernels, attend(): pl.pallas_call(partial(attend_kernel, blocks), grid_spec=pltpu.PrefetchSc...  23.2 us
    pallas_call x1, Pallas kernels, project(): pl.pallas_call(project_kernel, grid=(1 + 2 * REACH,), in_specs=[tile, squ...  19.2 us
    pallas_call x1, Pallas kernels, pair_sums(): pl.pallas_call(partial(pair_kernel, blk), out_shape=[jax.ShapeDtypeStruct...  15.2 us
    unnamed x35, local copies, waits for them, and re-layouts  14.7 us
  transfers between devices with their start and end apart: 3, of which 0 were waited for; matrix products, arithmetic and copies ran while one was open for 0% of the time, Pallas kernels for 8%

profile of v6, /device:TPU:0, one launch (start us, length us, event | category | flops | bytes accessed | tf_op | source)
XLA Modules:
  0.0 515.0 jit_solution(349091438328415441)
XLA Ops:
  0.7 0.7 fusion.5
  1.5 2.6 convert_reduce_fusion
  4.3 0.8 stack.57
  5.1 1.3 fusion.10.refs_1_
  6.5 159.6 %gather.1 = (bf16[5,1024,768]{2,1,0:T(8,128)(2,1)}, bf16[1024,768]{1,0:T(8,128)(2,1)}, bf16[4,8,16,128]{3,2,1,0:T(8,128)(2,1)}, bf16[4,8,24,768]{3,2,1,0:T(8,128...) custom-call(bf16[1024,768]{1,0:T(8,128)(2,1)} %x_ref.1, ...), custom_call_target="tpu_custom_call" | custom-call | tf_op jit(solution)/shard_map/gather/pallas_call | solution.py:793
  166.1 0.8 slice.70
  166.9 0.8 slice.72
  167.9 0.8 dynamic-slice_subtract_fusion
  169.5 0.9 broadcast_in_dim.46
  171.5 0.7 reshape.184.vec_ref
  172.2 0.7 reshape.185.bi_ref
  172.9 19.2 %project.1 = (bf16[5120,768]{1,0:T(8,128)(2,1)}, bf16[5120,768]{1,0:T(8,128)(2,1)}, bf16[1024,768]{1,0:T(8,128)(2,1)}) custom-call(bf16[5120,768]{1,0:T(8,128)(2,1)} %bitcast.54, bf16[768,768]{1,0:T(8,128)(2,1)} %bitcast.58, bf16[768,768]{1,0:T(8,128)(2,1)} %bitcast.60, bf16[768,768]{1,0:T(8,128)(2,1)} %bitcast.56, f32[8,768]{1,0:T(8,128)} %reshape.184.vec_ref), custom_call_target="tpu_custom_call" | custom-call | tf_op jit(solution)/shard_map/project/pallas_call | solution.py:461
  192.1 3.2 copy-done
  195.3 1.4 copy-done.2
  196.7 23.2 %attend.1 = (bf16[1024,768]{1,0:T(8,128)(2,1)S(1)}, bf16[3,16,512,256]{3,2,1,0:T(8,128)(2,1)}) custom-call(s32[1536]{0:T(1024)S(1)} %min.12.rows_ref, bf16[1024,768]{1,0:T(8,128)(2,1)S(1)} %copy-done.2, bf16[5120,768]{1,0:T(8,128)(2,1)S(1)} %copy-done, bf16[5120,768]{1,0:T(8,128)(2,1)} %get-tuple-element.65.v_ref, s32[3,16,8,256]{3,2,1,0:T(8,128)S(1)} %reshape.173.base_ref, ...), custom_call_target="tpu_custom_call" | custom-call | tf_op jit(solution)/shard_map/attend/pallas_call | solution.py:187
  219.9 1.1 copy-done.1
  221.0 64.3 %middle.1 = (bf16[1024,768]{1,0:T(8,128)(2,1)}, f32[1024,768]{1,0:T(8,128)}, bf16[1024,768]{1,0:T(8,128)(2,1)}, bf16[768,768]{1,0:T(8,128)(2,1)}, bf16[768,3072]...) custom-call(bf16[1024,768]{1,0:T(8,128)(2,1)} %copy-done.1, ...), custom_call_target="tpu_custom_call" | custom-call | tf_op jit(solution)/shard_map/middle/pallas_call | solution.py:394
  285.3 15.2 %pair_sums.1 = (bf16[4,96,768]{2,1,0:T(8,128)(2,1)}, bf16[4,96,768]{2,1,0:T(8,128)(2,1)}, bf16[4,96,768]{2,1,0:T(8,128)(2,1)}, bf16[4,96,768]{2,1,0:T(8,128)(2,1...) custom-call(bf16[4,8,24,768]{3,2,1,0:T(8,128)(2,1)} %bitcast.67, ...), custom_call_target="tpu_custom_call" | custom-call | tf_op jit(solution)/shard_map/pair_sums/pallas_call | solution.py:871
  300.5 2.9 collective-permute-start
  303.4 2.4 collective-permute-start.1
  305.8 2.3 collective-permute-start.2
  308.1 39.2 %attend_back.1 = (bf16[1024,768]{1,0:T(8,128)(2,1)}, bf16[5120,768]{1,0:T(8,128)(2,1)}, bf16[5120,768]{1,0:T(8,128)(2,1)}, f32[8,768]{1,0:T(8,128)}) custom-call(s32[1536]{0:T(1024)} %copy-done.3, bf16[1024,768]{1,0:T(8,128)(2,1)} %get-tuple-element.63.q_ref, bf16[1024,768]{1,0:T(8,128)(2,1)} %get-tuple-element.72.g_ref, ...), custom_call_target="tpu_custom_call" | custom-call | flops 16106127360 | bytes 104857600 | tf_op jit(solution)/shard_map/attend_back/pallas_call | solution.py:220
  347.3 0.7 slice.58
  348.5 0.9 copy.57
  349.4 0.9 copy-done.4
  350.5 153.7 %reduce_to_owners.1 = (f32[1024,768]{1,0:T(8,128)}, f32[16,128]{1,0:T(8,128)}, f32[24,768]{1,0:T(8,128)}, f32[24,768]{1,0:T(8,128)}, f32[24,768]{1,0:T(8,128)}, ...) custom-call(f32[4,8,16,128]{3,2,1,0:T(8,128)} %bitcast.68, bf16[5120,768]{1,0:T(8,128)(2,1)} %bitcast.55, ...), custom_call_target="tpu_custom_call" | custom-call | tf_op jit(solution)/shard_map/reduce_to_owners/pallas_call | solution.py:1329
  504.2 1.5 slice_bitcast_fusion
  505.8 1.2 slice_bitcast_fusion.3
  507.0 3.8 copy.69
  510.8 0.6 copy.70
  513.4 0.7 copy.74
  514.1 0.7 copy.75
  (68 shorter events, 4.7 us)
Async XLA Ops:
  171.1 21.0 %copy-start.3 = (s32[1536]{0:T(1024)}, s32[1536]{0:T(1024)S(1)}, u32[]{:S(2)}) copy-start(s32[1536]{0:T(1024)S(1)} %min.12.rows_ref) | copy-start | bytes 18436
  192.1 3.2 copy-start
  195.3 1.4 copy-start.2
  219.9 1.1 copy-start.1
  300.5 48.9 %collective-permute-start = (bf16[4,128,768]{2,1,0:T(8,128)(2,1)}, bf16[4,128,768]{2,1,0:T(8,128)(2,1)S(1)}, u32[]{:S(2)}, u32[]{:S(2)}) collective-permute-start(bf16[4,128,768]{2,1,0:T(8,128)(2,1)} %get-tuple-element.84), channel_id=1, source_target_pairs={{0,2},{1,3},{2,4},{3,5},{4,6},{5,7},{6,0},{7,1},{8,10},{9,11},{10,... | collective-permute-start | bytes 2359304 | tf_op jit(solution)/shard_map/ppermute | solution.py:900
  303.4 45.9 %collective-permute-start.1 = (bf16[4,128,768]{2,1,0:T(8,128)(2,1)}, bf16[4,128,768]{2,1,0:T(8,128)(2,1)S(1)}, u32[]{:S(2)}, u32[]{:S(2)}) collective-permute-start(bf16[4,128,768]{2,1,0:T(8,128)(2,1)} %get-tuple-element.85), channel_id=1, source_target_pairs={{0,4},{1,5},{2,6},{3,7},{4,0},{5,1},{6,2},{7,3},{8,12},{9,13},{10,... | collective-permute-start | bytes 2359304 | tf_op jit(solution)/shard_map/ppermute | solution.py:900
  305.8 43.6 %collective-permute-start.2 = (bf16[4,128,768]{2,1,0:T(8,128)(2,1)}, bf16[4,128,768]{2,1,0:T(8,128)(2,1)}, u32[]{:S(2)}, u32[]{:S(2)}) collective-permute-start(bf16[4,128,768]{2,1,0:T(8,128)(2,1)} %get-tuple-element.86), channel_id=1, source_target_pairs={{0,6},{1,7},{2,0},{3,1},{4,2},{5,3},{6,4},{7,5},{8,14},{9,15},{10,... | collective-permute-start | bytes 2359304 | tf_op jit(solution)/shard_map/ppermute | solution.py:900
  308.1 39.9 %copy-start.12 = (f32[8,768]{1,0:T(8,128)S(1)}, f32[8,768]{1,0:T(8,128)}, u32[]{:S(2)}) copy-start(f32[8,768]{1,0:T(8,128)} %get-tuple-element.71) | copy-start | bytes 73732
  308.1 40.0 %copy-start.13 = (f32[4,1,768]{2,1,0:T(1,128)S(1)}, f32[4,1,768]{2,1,0:T(1,128)}, u32[]{:S(2)}) copy-start(f32[4,1,768]{2,1,0:T(1,128)} %get-tuple-element.75) | copy-start | bytes 36868
  349.4 0.9 copy-start.4
  349.4 1.1 copy-start.5
  507.0 3.9 copy-start.11
  507.0 4.5 copy-start.10
  507.0 5.1 copy-start.9
  507.0 5.8 %copy-start.8 = (f32[24,768]{1,0:T(8,128)S(1)}, f32[24,768]{1,0:T(8,128)}, u32[]{:S(2)}) copy-start(f32[24,768]{1,0:T(8,128)} %get-tuple-element.139) | copy-start | bytes 221188
  507.0 6.4 %copy-start.7 = (f32[24,3072]{1,0:T(8,128)S(1)}, f32[24,3072]{1,0:T(8,128)}, u32[]{:S(2)}) copy-start(f32[24,3072]{1,0:T(8,128)} %get-tuple-element.140) | copy-start | bytes 884740
  507.0 7.1 %copy-start.6 = (f32[96,768]{1,0:T(8,128)S(1)}, f32[96,768]{1,0:T(8,128)}, u32[]{:S(2)}) copy-start(f32[96,768]{1,0:T(8,128)} %get-tuple-element.141) | copy-start | bytes 884740

commit v7 on v6

--- a/solution.py
+++ b/solution.py
@@ -205,7 +205,7 @@
             jax.ShapeDtypeStruct((tokens, width), bf16),
             jax.ShapeDtypeStruct((groups, blocks, TILES * BLOCK, cols), bf16),
         ],
-        compiler_params=pltpu.CompilerParams(vmem_limit_bytes=40 << 20),
+        compiler_params=pltpu.CompilerParams(vmem_limit_bytes=60 << 20),
         name="attend",
     )(rows, queries, keys, values, bases, docs)
 
@@ -813,75 +813,74 @@
 
 def pair_kernel(blk, *refs):
     chips = blk // CORES
-    grads, firsts, seconds = refs[:3], refs[3 : 3 + chips], refs[3 + chips : 3 + 2 * chips]
-    rest = refs[3 + 2 * chips :]
-    held, arrived, (load, send, recv) = rest[:3], rest[3:6], rest[6:]
+    grads, outs, rest = refs[:2], refs[2 : 2 + chips], refs[2 + chips :]
+    held, arrived, (load, send, recv) = rest[:2], rest[2:4], rest[4:]
     h, b = lax.axis_index("head"), lax.axis_index("blk")
     chip, core = b // CORES, b % CORES
     sibling = chip * CORES + 1 - core
 
+    def part(a, there):
+        if a == 0:
+            return grads[a].at[:, there, :, pl.ds(3 * 768, 768)]
+        return grads[a].at[:, there]
+
     def mine(a, e):
         there = ((chip + e) % chips) * CORES + core
-        return pltpu.make_async_copy(grads[a].at[:, there], held[a].at[e], load.at[a, e])
+        return pltpu.make_async_copy(part(a, there), held[a].at[e], load.at[a, e])
 
     def across(a, e):
         there = ((chip + e) % chips) * CORES + 1 - core
         return remote(
-            grads[a].at[:, there], arrived[a].at[e], send.at[a, e], recv.at[a, e], h, sibling
+            part(a, there), arrived[a].at[e], send.at[a, e], recv.at[a, e], h, sibling
         )
 
     order = [e % chips for e in range(1, chips + 1)]
     for e in order:
-        for a in range(3):
+        for a in range(2):
             mine(a, e).start()
     barrier = pltpu.get_barrier_semaphore()
     pl.semaphore_signal(barrier, inc=1, device_id=(h, sibling), device_id_type=MESH)
     pl.semaphore_wait(barrier, 1)
     for e in order:
-        for a in range(3):
+        for a in range(2):
             across(a, e).start()
     for e in order:
-        for a in range(3):
+        for a in range(2):
             mine(a, e).wait()
             across(a, e).wait_recv()
 
         def one(n, carry, e=e):
-            attn, inner, outer = (
-                held[a][e, n].astype(f32) + arrived[a][e, n].astype(f32) for a in range(3)
+            inner, outer = (
+                held[a][e, n].astype(f32) + arrived[a][e, n].astype(f32) for a in range(2)
             )
-            parts = [inner[:, m * 768 : (m + 1) * 768] for m in range(4)]
             spare = jnp.zeros((8, 768), f32)
-            firsts[e][n, 0:48] = jnp.concatenate([attn, parts[0]], axis=0).astype(bf16)
-            firsts[e][n, 48:96] = jnp.concatenate(parts[1:3], axis=0).astype(bf16)
-            seconds[e][n, 0:32] = jnp.concatenate([parts[3], spare], axis=0).astype(bf16)
-            seconds[e][n, 32:128] = outer.astype(bf16)
+            outs[e][n, 0:32] = jnp.concatenate([inner, spare], axis=0).astype(bf16)
+            outs[e][n, 32:128] = outer.astype(bf16)
             return carry
 
         lax.fori_loop(0, LINE, one, 0)
     for e in order:
-        for a in range(3):
+        for a in range(2):
             across(a, e).wait_send()
 
 
 def pair_sums(grads, blk):
     chips = blk // CORES
-    shard = [g.shape[2:] for g in grads]
+    shard = [(24, 768), (96, 768)]
     dma = pltpu.SemaphoreType.DMA
     inside = pl.BlockSpec(memory_space=pltpu.VMEM)
-    outs = pl.pallas_call(
+    return pl.pallas_call(
         partial(pair_kernel, blk),
-        out_shape=[jax.ShapeDtypeStruct((LINE, 96, 768), bf16)] * chips
-        + [jax.ShapeDtypeStruct((LINE, 128, 768), bf16)] * chips,
-        in_specs=[pl.BlockSpec(memory_space=pl.ANY)] * 3,
-        out_specs=[inside] * 2 * chips,
+        out_shape=[jax.ShapeDtypeStruct((LINE, 128, 768), bf16)] * chips,
+        in_specs=[pl.BlockSpec(memory_space=pl.ANY)] * 2,
+        out_specs=[inside] * chips,
         scratch_shapes=[pltpu.VMEM((chips, LINE) + s, bf16) for s in shard] * 2
-        + [dma((3, chips))] * 3,
+        + [dma((2, chips))] * 3,
         compiler_params=pltpu.CompilerParams(
             collective_id=2, has_side_effects=True, vmem_limit_bytes=56 << 20
         ),
         name="pair_sums",
     )(*grads)
-    return outs[:chips], outs[chips:]
 
 
 def over_plane(sums, blk, head):
@@ -905,8 +904,8 @@
     small_ref, wide_ref, query_ref, key_ref, value_ref = refs[:5]
     weights, first_ref = refs[5:8], refs[8]
     chips = blk // CORES
-    early, packed = refs[9 : 9 + chips], refs[9 + chips : 9 + 2 * chips]
-    rest = refs[9 + 2 * chips :]
+    early, raw = refs[9 : 9 + chips], refs[9 + chips : 11 + chips]
+    rest = refs[11 + chips :]
     sum_ref, outs, early_outs = rest[0], rest[1 : 1 + count], rest[1 + count : 4 + count]
     early_sum, early_in, es, er = rest[4 + count : 8 + count]
     totals, (wide_in, key_in, value_in, fed) = rest[8 + count : 11 + count], rest[11 + count : 15 + count]
@@ -916,6 +915,7 @@
     extra = count
     held, from_core, rest = rest[: count + 1], rest[count + 1 : 2 * count + 1], rest[2 * count + 1 :]
     from_chip, from_line, rest = rest[: count + 1], rest[count + 1 : 2 * count + 2], rest[2 * count + 2 :]
+    raw_own, raw_in, (rl, rs, rr), rest = rest[:2], rest[2:4], rest[4:7], rest[7:]
     frame, arrived, aside = rest[:3]
     load, ss, sr, cs, cr, zs, zr, us, ur, ds, dr, ns, nr, fs, fr = rest[3:]
     grads = (small_ref,) + tuple(totals)
@@ -1017,9 +1017,33 @@
     def mine(a, k):
         return pltpu.make_async_copy(grads[a].at[:, k * CORES + core], held[a].at[k], load.at[a, k])
 
-    def mine_packed(e):
-        target = held[extra].at[(chip + e) % chips]
-        return pltpu.make_async_copy(packed[e], target, load.at[extra, e])
+    def raw_part(n, there):
+        return raw[n].at[:, there, :, pl.ds(0, raw_own[n].shape[3])]
+
+    def mine_raw(n, k):
+        there = k * CORES + core
+        return pltpu.make_async_copy(raw_part(n, there), raw_own[n].at[k], rl.at[n, k])
+
+    def across_raw(n, k):
+        there = k * CORES + 1 - core
+        return remote(raw_part(n, there), raw_in[n].at[k], rs.at[n, k], rr.at[n, k], h, sibling)
+
+    def pack_raw(k):
+        for n in range(2):
+            mine_raw(n, k).wait()
+            across_raw(n, k).wait_recv()
+
+        def one(m, carry):
+            attn, inner = (
+                raw_own[n][k, m].astype(f32) + raw_in[n][k, m].astype(f32) for n in range(2)
+            )
+            parts = [attn] + [inner[:, c * 768 : (c + 1) * 768] for c in range(3)]
+            for c in range(2):
+                both = jnp.concatenate(parts[2 * c : 2 * c + 2], axis=0)
+                held[extra][k, m, 48 * c : 48 * (c + 1)] = both.astype(bf16)
+            return carry
+
+        lax.fori_loop(0, LINE, one, 0)
 
     def across(a, k):
         return remote(
@@ -1277,19 +1301,23 @@
     start(standing())
     for k in range(chips):
         mine(0, k).start()
-        mine_packed(k).start()
+        for n in range(2):
+            mine_raw(n, k).start()
     frame[slots] = jnp.zeros(frame.shape[1:], frame.dtype)
     for n in (1, 2):
         totals[n][...] = jnp.zeros_like(totals[n])
     greet_plane_and_line(h, b, blk)
+    for k in range(chips):
+        for n in range(2):
+            across_raw(n, k).start()
     wait(standing())
     early_to_line()
     lax.fori_loop(0, slots, work, 0)
     query_work()
-    for e in range(chips):
-        mine_packed(e).wait()
     for e in range(1, chips):
+        pack_raw((chip + e) % chips)
         over(extra, e).start()
+    pack_raw(chip)
     for a in range(count):
         for k in range(chips):
             across(a, k).start()
@@ -1313,9 +1341,12 @@
             over(a, e).wait_send()
         for d in range(1, LINE):
             along(a, d).wait_send()
-
-
-def reduce_to_owners(small, wide, projected, weights, first, early, packed, blk):
+    for k in range(chips):
+        for n in range(2):
+            across_raw(n, k).wait_send()
+
+
+def reduce_to_owners(small, wide, projected, weights, first, early, raw, blk):
     rows, width = first.shape
     count, chips = 4, blk // CORES
     anywhere = pl.BlockSpec(memory_space=pl.ANY)
@@ -1324,14 +1355,14 @@
     square = (width // (LINE * blk), width)
     shard = [small.shape[2:]] + [square] * 3
     kinds = [f32] + [bf16] * 4
-    travels = shard + [packed[0].shape[1:]]
+    travels = shard + [(96, 768)]
     early_shapes = ((24, 768), (24, 3072), (96, 768))
     outs = pl.pallas_call(
         partial(reduce_kernel, blk, count),
         out_shape=[jax.ShapeDtypeStruct((rows, width), f32)]
         + [jax.ShapeDtypeStruct(s, f32) for s in shard]
         + [jax.ShapeDtypeStruct(s, f32) for s in early_shapes],
-        in_specs=[anywhere] * (9 + 2 * chips),
+        in_specs=[anywhere] * (11 + chips),
         out_specs=[inside] * (4 + count),
         scratch_shapes=[
             pltpu.VMEM(early[0].shape, bf16),
@@ -1349,6 +1380,8 @@
         + [pltpu.VMEM((chips, LINE) + s, f32) for s in shard]
         + [pltpu.VMEM((chips - 1, LINE) + s, t) for s, t in zip(travels, kinds)]
         + [pltpu.VMEM((LINE - 1,) + s, t) for s, t in zip(travels, kinds)]
+        + [pltpu.VMEM((chips, LINE, 24, size), bf16) for size in (768, 3 * 768)] * 2
+        + [dma((2, chips))] * 3
         + [
             pltpu.VMEM((2 + 2 * REACH, rows, width), bf16),
             pltpu.VMEM((LINE + 1, rows, width), bf16),
@@ -1363,7 +1396,7 @@
             collective_id=1, has_side_effects=True, vmem_limit_bytes=62 << 20
         ),
         name="reduce_to_owners",
-    )(small, wide, *projected, *weights, first, *early, *packed)
+    )(small, wide, *projected, *weights, first, *early, *raw)
     return outs[0], outs[1:-3], outs[-3:]
 
 
@@ -1428,8 +1461,8 @@
 
     early_grads = [grad_w_attn, grad_w_inner, grad_w_outer]
     if by_kernel:
-        halves, early = pair_sums([g.reshape(head, blk, -1, g.shape[-1]) for g in early_grads], blk)
-        early = over_plane(early, blk, head)
+        raw = [g.reshape(head, blk, -1, g.shape[-1]) for g in early_grads]
+        early = over_plane(pair_sums(raw[1:], blk), blk, head)
     grad_scaled, grad_keyed, grad_valued, sums_qv = attend_back(
         rows_of, queries, grad_attended, keys, values, probs
     )
@@ -1451,7 +1484,7 @@
             (w_query, w_key, w_value),
             grad_first_sum,
             early,
-            halves,
+            raw[:2],
             blk,
         )
         matrix_grads = tuple(late[1:]) + tuple(early_sum)

time: 514 us -> 510 us (level)
    unnamed x35 -> x27, local copies, waits for them, and re-layouts: 14.7 us -> 8.97 us
where the time goes in v7:
time: 510 us; the launch traced here: 507 us
  Pallas kernels  471 us (92%)
  local copies, waits for them, and re-layouts  21.7 us (4%)
  starting transfers between devices  7.63 us (1%)
  other arithmetic  5.98 us (1%)
    pallas_call x1, Pallas kernels, gather(): pl.pallas_call(partial(gather_kernel, blk, count), out_shape=[jax.ShapeDt...  160 us
    pallas_call x1, Pallas kernels, reduce_to_owners(): pl.pallas_call(partial(reduce_kernel, blk, count), out_shape=[jax.ShapeDt...  153 us
    pallas_call x1, Pallas kernels, middle(): pl.pallas_call(middle_kernel, grid=(2 * steps,), in_specs=[still, still,...  64.5 us
    pallas_call x1, Pallas kernels, attend_back(): pl.pallas_call(partial(attend_back_kernel, blocks), grid_spec=pltpu.Prefe...  39.2 us
    pallas_call x1, Pallas kernels, attend(): pl.pallas_call(partial(attend_kernel, blocks), grid_spec=pltpu.PrefetchSc...  23.8 us
    pallas_call x1, Pallas kernels, project(): pl.pallas_call(project_kernel, grid=(1 + 2 * REACH,), in_specs=[tile, squ...  19.3 us
    pallas_call x1, Pallas kernels, pair_sums(): pl.pallas_call(partial(pair_kernel, blk), out_shape=[jax.ShapeDtypeStruct...  10.8 us
  transfers between devices with their start and end apart: 3, of which 0 were waited for; matrix products, arithmetic and copies ran while one was open for 0% of the time, Pallas kernels for 8%

profile of v7, /device:TPU:0, one launch (start us, length us, event | category | flops | bytes accessed | tf_op | source)
XLA Modules:
  0.0 507.1 jit_solution(5937491891373651438)
XLA Ops:
  0.7 0.7 fusion.5
  1.5 2.6 convert_reduce_fusion
  4.3 0.8 stack.57
  5.1 1.3 fusion.10.refs_1_
  6.5 159.6 %gather.1 = (bf16[5,1024,768]{2,1,0:T(8,128)(2,1)}, bf16[1024,768]{1,0:T(8,128)(2,1)}, bf16[4,8,16,128]{3,2,1,0:T(8,128)(2,1)}, bf16[4,8,24,768]{3,2,1,0:T(8,128...) custom-call(bf16[1024,768]{1,0:T(8,128)(2,1)} %x_ref.1, ...), custom_call_target="tpu_custom_call" | custom-call | tf_op jit(solution)/shard_map/gather/pallas_call | solution.py:793
  166.1 0.8 slice.70
  166.9 0.8 slice.72
  167.9 0.8 dynamic-slice_subtract_fusion
  170.1 1.2 reshape.173.base_ref
  171.3 0.7 min.12.rows_ref
  172.2 0.9 tile.10.doc_ref
  173.1 0.7 reshape.184.vec_ref
  173.8 0.7 reshape.185.bi_ref
  174.5 19.3 %project.1 = (bf16[5120,768]{1,0:T(8,128)(2,1)}, bf16[5120,768]{1,0:T(8,128)(2,1)}, bf16[1024,768]{1,0:T(8,128)(2,1)}) custom-call(bf16[5120,768]{1,0:T(8,128)(2,1)} %bitcast.54, bf16[768,768]{1,0:T(8,128)(2,1)} %bitcast.60, bf16[768,768]{1,0:T(8,128)(2,1)} %bitcast.62, bf16[768,768]{1,0:T(8,128)(2,1)} %bitcast.58, f32[8,768]{1,0:T(8,128)} %reshape.184.vec_ref), custom_call_target="tpu_custom_call" | custom-call | tf_op jit(solution)/shard_map/project/pallas_call | solution.py:461
  193.8 23.8 %attend.1 = (bf16[1024,768]{1,0:T(8,128)(2,1)}, bf16[3,16,512,256]{3,2,1,0:T(8,128)(2,1)}) custom-call(s32[1536]{0:T(1024)} %min.12.rows_ref, bf16[1024,768]{1,0:T(8,128)(2,1)} %get-tuple-element.59.q_ref, bf16[5120,768]{1,0:T(8,128)(2,1)} %get-tuple-element.60.k_ref, bf16[5120,768]{1,0:T(8,128)(2,1)} %get-tuple-element.61.v_ref, ...), custom_call_target="tpu_custom_call" | custom-call | tf_op jit(solution)/shard_map/attend/pallas_call | solution.py:187
  217.5 64.5 %middle.1 = (bf16[1024,768]{1,0:T(8,128)(2,1)}, f32[1024,768]{1,0:T(8,128)}, bf16[1024,768]{1,0:T(8,128)(2,1)}, bf16[768,768]{1,0:T(8,128)(2,1)}, bf16[768,3072]...) custom-call(bf16[1024,768]{1,0:T(8,128)(2,1)} %get-tuple-element.62.att_ref, ...), custom_call_target="tpu_custom_call" | custom-call | tf_op jit(solution)/shard_map/middle/pallas_call | solution.py:394
  282.1 10.8 %pair_sums.1 = (bf16[4,128,768]{2,1,0:T(8,128)(2,1)}, bf16[4,128,768]{2,1,0:T(8,128)(2,1)}, bf16[4,128,768]{2,1,0:T(8,128)(2,1)}, bf16[4,128,768]{2,1,0:T(8,128)(2,1)}) custom-call(bf16[4,8,24,3072]{3,2,1,0:T(8,128)(2,1)} %bitcast.56, bf16[4,8,96,768]{3,2,1,0:T(8,128)(2,1)} %bitcast.64), custom_call_target="tpu_custom_call" | custom-call | tf_op jit(solution)/shard_map/pair_sums/pallas_call | solution.py:872
  292.9 2.9 collective-permute-start
  295.8 2.4 collective-permute-start.1
  298.2 2.3 collective-permute-start.2
  300.5 39.2 %attend_back.1 = (bf16[1024,768]{1,0:T(8,128)(2,1)}, bf16[5120,768]{1,0:T(8,128)(2,1)}, bf16[5120,768]{1,0:T(8,128)(2,1)}, f32[8,768]{1,0:T(8,128)}) custom-call(s32[1536]{0:T(1024)} %min.12.rows_ref, bf16[1024,768]{1,0:T(8,128)(2,1)} %get-tuple-element.59.q_ref, bf16[1024,768]{1,0:T(8,128)(2,1)} %get-tuple-element.68.g_ref, ...), custom_call_target="tpu_custom_call" | custom-call | flops 16106127360 | bytes 104857600 | tf_op jit(solution)/shard_map/attend_back/pallas_call | solution.py:220
  339.7 0.7 slice.58
  340.9 0.9 copy.57
  341.8 0.9 copy-done
  342.9 153.4 %reduce_to_owners.1 = (f32[1024,768]{1,0:T(8,128)}, f32[16,128]{1,0:T(8,128)}, f32[24,768]{1,0:T(8,128)}, f32[24,768]{1,0:T(8,128)}, f32[24,768]{1,0:T(8,128)}, ...) custom-call(f32[4,8,16,128]{3,2,1,0:T(8,128)} %bitcast.69, bf16[5120,768]{1,0:T(8,128)(2,1)} %bitcast.55, ...), custom_call_target="tpu_custom_call" | custom-call | tf_op jit(solution)/shard_map/reduce_to_owners/pallas_call | solution.py:1360
  496.4 1.5 slice_bitcast_fusion
  497.9 1.2 slice_bitcast_fusion.3
  499.1 3.8 copy.69
  503.6 0.6 copy.71
  504.8 0.6 copy.73
  505.5 0.7 copy.74
  506.2 0.7 copy.75
  (60 shorter events, 3.9 us)
Async XLA Ops:
  292.9 48.9 %collective-permute-start = (bf16[4,128,768]{2,1,0:T(8,128)(2,1)}, bf16[4,128,768]{2,1,0:T(8,128)(2,1)S(1)}, u32[]{:S(2)}, u32[]{:S(2)}) collective-permute-start(bf16[4,128,768]{2,1,0:T(8,128)(2,1)} %get-tuple-element.79), channel_id=1, source_target_pairs={{0,2},{1,3},{2,4},{3,5},{4,6},{5,7},{6,0},{7,1},{8,10},{9,11},{10,... | collective-permute-start | bytes 2359304 | tf_op jit(solution)/shard_map/ppermute | solution.py:899
  295.8 46.0 %collective-permute-start.1 = (bf16[4,128,768]{2,1,0:T(8,128)(2,1)}, bf16[4,128,768]{2,1,0:T(8,128)(2,1)S(1)}, u32[]{:S(2)}, u32[]{:S(2)}) collective-permute-start(bf16[4,128,768]{2,1,0:T(8,128)(2,1)} %get-tuple-element.80), channel_id=1, source_target_pairs={{0,4},{1,5},{2,6},{3,7},{4,0},{5,1},{6,2},{7,3},{8,12},{9,13},{10,... | collective-permute-start | bytes 2359304 | tf_op jit(solution)/shard_map/ppermute | solution.py:899
  298.2 43.6 %collective-permute-start.2 = (bf16[4,128,768]{2,1,0:T(8,128)(2,1)}, bf16[4,128,768]{2,1,0:T(8,128)(2,1)}, u32[]{:S(2)}, u32[]{:S(2)}) collective-permute-start(bf16[4,128,768]{2,1,0:T(8,128)(2,1)} %get-tuple-element.81), channel_id=1, source_target_pairs={{0,6},{1,7},{2,0},{3,1},{4,2},{5,3},{6,4},{7,5},{8,14},{9,15},{10,... | collective-permute-start | bytes 2359304 | tf_op jit(solution)/shard_map/ppermute | solution.py:899
  300.5 40.0 %copy-start.8 = (f32[8,768]{1,0:T(8,128)S(1)}, f32[8,768]{1,0:T(8,128)}, u32[]{:S(2)}) copy-start(f32[8,768]{1,0:T(8,128)} %get-tuple-element.67) | copy-start | bytes 73732
  300.5 40.1 %copy-start.9 = (f32[4,1,768]{2,1,0:T(1,128)S(1)}, f32[4,1,768]{2,1,0:T(1,128)}, u32[]{:S(2)}) copy-start(f32[4,1,768]{2,1,0:T(1,128)} %get-tuple-element.71) | copy-start | bytes 36868
  341.8 0.9 copy-start
  341.8 1.2 copy-start.1
  499.1 3.9 copy-start.7
  499.1 4.5 copy-start.6
  499.1 5.1 %copy-start.5 = (f32[24,768]{1,0:T(8,128)S(1)}, f32[24,768]{1,0:T(8,128)}, u32[]{:S(2)}) copy-start(f32[24,768]{1,0:T(8,128)} %get-tuple-element.130) | copy-start | bytes 221188
  499.1 5.8 %copy-start.4 = (f32[24,768]{1,0:T(8,128)S(1)}, f32[24,768]{1,0:T(8,128)}, u32[]{:S(2)}) copy-start(f32[24,768]{1,0:T(8,128)} %get-tuple-element.131) | copy-start | bytes 221188
  499.1 6.4 %copy-start.3 = (f32[24,3072]{1,0:T(8,128)S(1)}, f32[24,3072]{1,0:T(8,128)}, u32[]{:S(2)}) copy-start(f32[24,3072]{1,0:T(8,128)} %get-tuple-element.132) | copy-start | bytes 884740
  499.1 7.1 %copy-start.2 = (f32[96,768]{1,0:T(8,128)S(1)}, f32[96,768]{1,0:T(8,128)}, u32[]{:S(2)}) copy-start(f32[96,768]{1,0:T(8,128)} %get-tuple-element.133) | copy-start | bytes 884740

commit v8 on v7

--- a/solution.py
+++ b/solution.py
@@ -24,6 +24,7 @@
 gelu_scale = 0.7978845608028654
 gelu_cubic = 0.044715
 far_away = -(1 << 24)
+repeated = 1 << 20
 f32, bf16 = jnp.float32, jnp.bfloat16
 
 
@@ -86,20 +87,33 @@
 def row_readers(rows_ref, blocks, i):
     group = pl.program_id(0)
 
+    def fixed_code(t):
+        return rows_ref[(group * GROUP * blocks + i) * TILES + t]
+
+    def random_code(h, t):
+        return rows_ref[((group * GROUP + h) * blocks + i) * TILES + 5 + t]
+
     def fixed_row(t):
-        return rows_ref[(group * GROUP * blocks + i) * TILES + t]
+        return fixed_code(t) % repeated
 
     def random_row(h, t):
-        return rows_ref[((group * GROUP + h) * blocks + i) * TILES + 5 + t]
-
-    return fixed_row, random_row
-
-
-def attend_kernel(blocks, rows_ref, q_ref, k_ref, v_ref, base_ref, doc_ref, out_ref, p_ref):
+        return random_code(h, t) % repeated
+
+    return (fixed_row, random_row), (fixed_code, random_code)
+
+
+def first_place(code):
+    return jnp.where(code >= repeated, far_away, code * BLOCK)
+
+
+def attend_kernel(blocks, rows_ref, q_ref, k_ref, v_ref, doc_ref, out_ref, p_ref):
+    head_of = lax.broadcasted_iota(jnp.int32, (1, GROUP * BLOCK), 1) // BLOCK
     within = lax.broadcasted_iota(jnp.int32, (BLOCK, GROUP * BLOCK), 0)
     for u in range(FORWARD_BLOCKS):
         here = pl.ds(u * BLOCK, BLOCK)
-        readers = row_readers(rows_ref, blocks, pl.program_id(1) * FORWARD_BLOCKS + u)
+        readers, (fixed_code, random_code) = row_readers(
+            rows_ref, blocks, pl.program_id(1) * FORWARD_BLOCKS + u
+        )
         keys = gathered(k_ref, *readers)
         values = gathered(v_ref, *readers)
         scores = mm_nt(keys, stacked_by_head(q_ref[here, :]))
@@ -107,7 +121,13 @@
         hi = doc_ref[u, 1:2, :]
         masked = []
         for t in range(TILES):
-            place = within + base_ref[0, u, t : t + 1, :]
+            if t < 5:
+                base = first_place(fixed_code(t))
+            else:
+                base = first_place(random_code(0, t - 5))
+                for n in range(1, GROUP):
+                    base = jnp.where(head_of == n, first_place(random_code(n, t - 5)), base)
+            place = within + base
             allowed = (place >= lo) & (place < hi)
             masked.append(jnp.where(allowed, scores[t * BLOCK : (t + 1) * BLOCK], masked_value))
         scores = jnp.concatenate(masked, axis=0)
@@ -143,7 +163,7 @@
     found = []
     for u in range(BACKWARD_BLOCKS):
         here = pl.ds(u * BLOCK, BLOCK)
-        readers = row_readers(rows_ref, blocks, step * BACKWARD_BLOCKS + u)
+        readers, _ = row_readers(rows_ref, blocks, step * BACKWARD_BLOCKS + u)
         keys = gathered(k_ref, *readers)
         values = gathered(v_ref, *readers)
         queries = stacked_by_head(q_ref[here, :])
@@ -177,7 +197,7 @@
         sums_ref[7:8, :] = jnp.sum(dv_ref[...].astype(f32), axis=0, keepdims=True)
 
 
-def attend(rows, queries, keys, values, bases, docs):
+def attend(rows, queries, keys, values, docs):
     tokens, width = queries.shape
     ext = keys.shape[0]
     blocks, cols, some = tokens // BLOCK, GROUP * HEAD_DIM, FORWARD_BLOCKS
@@ -193,7 +213,6 @@
                 tile,
                 table,
                 table,
-                pl.BlockSpec((1, some, TILES, cols), lambda g, i, r: (g, i, 0, 0)),
                 pl.BlockSpec((some, 8, cols), lambda g, i, r: (i, 0, 0)),
             ],
             out_specs=[
@@ -207,7 +226,7 @@
         ],
         compiler_params=pltpu.CompilerParams(vmem_limit_bytes=60 << 20),
         name="attend",
-    )(rows, queries, keys, values, bases, docs)
+    )(rows, queries, keys, values, docs)
 
 
 def attend_back(rows, queries, grads, keys, values, probs):
@@ -498,11 +517,8 @@
     )
     earlier = jnp.arange(TILES)[None, :] < jnp.arange(TILES)[:, None]
     repeat = jnp.any((rows[..., :, None] == rows[..., None, :]) & earlier, axis=-1)
-    bases = jnp.where(repeat, far_away, rows * BLOCK)
     rows = jnp.clip(rows, 0, (1 + 2 * REACH) * blocks - 1)
-    bases = bases.reshape(heads // GROUP, GROUP, blocks, TILES)
-    bases = jnp.repeat(jnp.transpose(bases, (0, 2, 3, 1)), BLOCK, axis=-1)
-    return rows.reshape(-1), bases, docs
+    return (rows + jnp.where(repeat, repeated, 0)).reshape(-1), docs
 
 
 def side_pairs(blk, head, far):
@@ -1310,8 +1326,10 @@
     for k in range(chips):
         for n in range(2):
             across_raw(n, k).start()
-    wait(standing())
+    ready = standing()
+    wait(ready[3:-1])
     early_to_line()
+    wait(ready[:3] + ready[-1:])
     lax.fori_loop(0, slots, work, 0)
     query_work()
     for e in range(1, chips):
@@ -1442,9 +1460,9 @@
     short_rows = short_rows.reshape(8, -1)
     bias_inner = table[:, 8, : vectors[5].shape[0]].astype(f32).reshape(-1, 1, PIECE)
 
-    rows_of, bases, docs = tile_plan(segment_ids, random_blocks, rows)
+    rows_of, docs = tile_plan(segment_ids, random_blocks, rows)
     keys, values, queries = project(wide, w_key, w_value, w_query, short_rows, rows)
-    attended, probs = attend(rows_of, queries, keys, values, bases, docs)
+    attended, probs = attend(rows_of, queries, keys, values, docs)
 
     result, grad_first_sum, grad_attended, grad_w_attn, grad_w_inner, grad_w_outer, sums_d, sums_ff = (
         middle(

time: 510 us -> 507 us (level)
  no operation moved by 1% of the time
where the time goes in v8:
time: 507 us; the launch traced here: 505 us
  Pallas kernels  471 us (93%)
  local copies, waits for them, and re-layouts  19.5 us (4%)
  starting transfers between devices  7.64 us (2%)
  other arithmetic  5.91 us (1%)
    pallas_call x1, Pallas kernels, gather(): pl.pallas_call(partial(gather_kernel, blk, count), out_shape=[jax.ShapeDt...  160 us
    pallas_call x1, Pallas kernels, reduce_to_owners(): pl.pallas_call(partial(reduce_kernel, blk, count), out_shape=[jax.ShapeDt...  152 us
    pallas_call x1, Pallas kernels, middle(): pl.pallas_call(middle_kernel, grid=(2 * steps,), in_specs=[still, still,...  64.6 us
    pallas_call x1, Pallas kernels, attend_back(): pl.pallas_call(partial(attend_back_kernel, blocks), grid_spec=pltpu.Prefe...  41.3 us
    pallas_call x1, Pallas kernels, attend(): pl.pallas_call(partial(attend_kernel, blocks), grid_spec=pltpu.PrefetchSc...  23.4 us
    pallas_call x1, Pallas kernels, project(): pl.pallas_call(project_kernel, grid=(1 + 2 * REACH,), in_specs=[tile, squ...  19.2 us
    pallas_call x1, Pallas kernels, pair_sums(): pl.pallas_call(partial(pair_kernel, blk), out_shape=[jax.ShapeDtypeStruct...  10.8 us
  transfers between devices with their start and end apart: 3, of which 0 were waited for; matrix products, arithmetic and copies ran while one was open for 0% of the time, Pallas kernels for 8%

profile of v8, /device:TPU:0, one launch (start us, length us, event | category | flops | bytes accessed | tf_op | source)
XLA Modules:
  0.0 504.7 jit_solution(2632690585151678645)
XLA Ops:
  0.7 0.7 fusion.3
  1.5 2.6 convert_reduce_fusion
  4.3 0.8 stack.57
  5.1 1.3 fusion.8.refs_1_
  6.5 159.6 %gather.1 = (bf16[5,1024,768]{2,1,0:T(8,128)(2,1)}, bf16[1024,768]{1,0:T(8,128)(2,1)}, bf16[4,8,16,128]{3,2,1,0:T(8,128)(2,1)}, bf16[4,8,24,768]{3,2,1,0:T(8,128...) custom-call(bf16[1024,768]{1,0:T(8,128)(2,1)} %x_ref.1, ...), custom_call_target="tpu_custom_call" | custom-call | tf_op jit(solution)/shard_map/gather/pallas_call | solution.py:809
  166.1 0.8 slice.70
  166.9 0.8 slice.72
  167.8 0.8 dynamic-slice_subtract_fusion
  169.0 0.7 add.89.rows_ref
  169.9 0.9 tile.10.doc_ref
  170.7 0.7 reshape.181.vec_ref
  171.5 0.7 reshape.182.bi_ref
  172.2 19.2 %project.1 = (bf16[5120,768]{1,0:T(8,128)(2,1)}, bf16[5120,768]{1,0:T(8,128)(2,1)}, bf16[1024,768]{1,0:T(8,128)(2,1)}) custom-call(bf16[5120,768]{1,0:T(8,128)(2,1)} %bitcast.50, bf16[768,768]{1,0:T(8,128)(2,1)} %bitcast.56, bf16[768,768]{1,0:T(8,128)(2,1)} %bitcast.58, bf16[768,768]{1,0:T(8,128)(2,1)} %bitcast.54, f32[8,768]{1,0:T(8,128)} %reshape.181.vec_ref), custom_call_target="tpu_custom_call" | custom-call | tf_op jit(solution)/shard_map/project/pallas_call | solution.py:480
  191.4 23.4 %attend.1 = (bf16[1024,768]{1,0:T(8,128)(2,1)}, bf16[3,16,512,256]{3,2,1,0:T(8,128)(2,1)}) custom-call(s32[1536]{0:T(1024)} %add.89.rows_ref, bf16[1024,768]{1,0:T(8,128)(2,1)} %get-tuple-element.59.q_ref, bf16[5120,768]{1,0:T(8,128)(2,1)} %get-tuple-element.60.k_ref, bf16[5120,768]{1,0:T(8,128)(2,1)} %get-tuple-element.61.v_ref, s32[16,8,256]{2,1,0:T(8,128)} %tile.10.doc_ref), custom_call_target="tpu_custom_call" | custom-call | tf_op jit(solution)/shard_map/attend/pallas_call | solution.py:207
  214.8 64.6 %middle.1 = (bf16[1024,768]{1,0:T(8,128)(2,1)}, f32[1024,768]{1,0:T(8,128)}, bf16[1024,768]{1,0:T(8,128)(2,1)}, bf16[768,768]{1,0:T(8,128)(2,1)}, bf16[768,3072]...) custom-call(bf16[1024,768]{1,0:T(8,128)(2,1)} %get-tuple-element.62.att_ref, ...), custom_call_target="tpu_custom_call" | custom-call | tf_op jit(solution)/shard_map/middle/pallas_call | solution.py:413
  279.4 10.8 %pair_sums.1 = (bf16[4,128,768]{2,1,0:T(8,128)(2,1)}, bf16[4,128,768]{2,1,0:T(8,128)(2,1)}, bf16[4,128,768]{2,1,0:T(8,128)(2,1)}, bf16[4,128,768]{2,1,0:T(8,128)(2,1)}) custom-call(bf16[4,8,24,3072]{3,2,1,0:T(8,128)(2,1)} %bitcast.52, bf16[4,8,96,768]{3,2,1,0:T(8,128)(2,1)} %bitcast.60), custom_call_target="tpu_custom_call" | custom-call | tf_op jit(solution)/shard_map/pair_sums/pallas_call | solution.py:888
  290.1 2.9 collective-permute-start
  293.0 2.4 collective-permute-start.1
  295.4 2.3 collective-permute-start.2
  297.8 41.3 %attend_back.1 = (bf16[1024,768]{1,0:T(8,128)(2,1)}, bf16[5120,768]{1,0:T(8,128)(2,1)}, bf16[5120,768]{1,0:T(8,128)(2,1)}, f32[8,768]{1,0:T(8,128)}) custom-call(s32[1536]{0:T(1024)} %add.89.rows_ref, bf16[1024,768]{1,0:T(8,128)(2,1)} %get-tuple-element.59.q_ref, bf16[1024,768]{1,0:T(8,128)(2,1)} %get-tuple-element.68.g_ref, ...), custom_call_target="tpu_custom_call" | custom-call | flops 16106127360 | bytes 104857600 | tf_op jit(solution)/shard_map/attend_back/pallas_call | solution.py:239
  339.0 0.7 slice.58
  340.2 0.9 copy.50
  341.1 0.9 copy-done
  342.3 151.7 %reduce_to_owners.1 = (f32[1024,768]{1,0:T(8,128)}, f32[16,128]{1,0:T(8,128)}, f32[24,768]{1,0:T(8,128)}, f32[24,768]{1,0:T(8,128)}, f32[24,768]{1,0:T(8,128)}, ...) custom-call(f32[4,8,16,128]{3,2,1,0:T(8,128)} %bitcast.65, bf16[5120,768]{1,0:T(8,128)(2,1)} %bitcast.51, ...), custom_call_target="tpu_custom_call" | custom-call | tf_op jit(solution)/shard_map/reduce_to_owners/pallas_call | solution.py:1378
  493.9 1.5 slice_bitcast_fusion
  495.5 1.2 slice_bitcast_fusion.3
  496.7 3.8 copy.62
  500.5 0.6 copy.63
  501.2 0.6 copy.64
  501.8 0.6 copy.65
  503.1 0.7 copy.67
  503.8 0.7 copy.68
  (54 shorter events, 2.1 us)
Async XLA Ops:
  290.1 51.0 %collective-permute-start = (bf16[4,128,768]{2,1,0:T(8,128)(2,1)}, bf16[4,128,768]{2,1,0:T(8,128)(2,1)S(1)}, u32[]{:S(2)}, u32[]{:S(2)}) collective-permute-start(bf16[4,128,768]{2,1,0:T(8,128)(2,1)} %get-tuple-element.79), channel_id=1, source_target_pairs={{0,2},{1,3},{2,4},{3,5},{4,6},{5,7},{6,0},{7,1},{8,10},{9,11},{10,... | collective-permute-start | bytes 2359304 | tf_op jit(solution)/shard_map/ppermute | solution.py:915
  293.0 48.1 %collective-permute-start.1 = (bf16[4,128,768]{2,1,0:T(8,128)(2,1)}, bf16[4,128,768]{2,1,0:T(8,128)(2,1)S(1)}, u32[]{:S(2)}, u32[]{:S(2)}) collective-permute-start(bf16[4,128,768]{2,1,0:T(8,128)(2,1)} %get-tuple-element.80), channel_id=1, source_target_pairs={{0,4},{1,5},{2,6},{3,7},{4,0},{5,1},{6,2},{7,3},{8,12},{9,13},{10,... | collective-permute-start | bytes 2359304 | tf_op jit(solution)/shard_map/ppermute | solution.py:915
  295.4 45.7 %collective-permute-start.2 = (bf16[4,128,768]{2,1,0:T(8,128)(2,1)}, bf16[4,128,768]{2,1,0:T(8,128)(2,1)}, u32[]{:S(2)}, u32[]{:S(2)}) collective-permute-start(bf16[4,128,768]{2,1,0:T(8,128)(2,1)} %get-tuple-element.81), channel_id=1, source_target_pairs={{0,6},{1,7},{2,0},{3,1},{4,2},{5,3},{6,4},{7,5},{8,14},{9,15},{10,... | collective-permute-start | bytes 2359304 | tf_op jit(solution)/shard_map/ppermute | solution.py:915
  297.8 42.0 %copy-start.8 = (f32[8,768]{1,0:T(8,128)S(1)}, f32[8,768]{1,0:T(8,128)}, u32[]{:S(2)}) copy-start(f32[8,768]{1,0:T(8,128)} %get-tuple-element.67) | copy-start | bytes 73732
  297.8 42.1 %copy-start.9 = (f32[4,1,768]{2,1,0:T(1,128)S(1)}, f32[4,1,768]{2,1,0:T(1,128)}, u32[]{:S(2)}) copy-start(f32[4,1,768]{2,1,0:T(1,128)} %get-tuple-element.71) | copy-start | bytes 36868
  341.1 0.9 copy-start
  341.1 1.2 copy-start.1
  496.7 3.9 copy-start.7
  496.7 4.5 copy-start.6
  496.7 5.1 %copy-start.5 = (f32[24,768]{1,0:T(8,128)S(1)}, f32[24,768]{1,0:T(8,128)}, u32[]{:S(2)}) copy-start(f32[24,768]{1,0:T(8,128)} %get-tuple-element.128) | copy-start | bytes 221188
  496.7 5.8 %copy-start.4 = (f32[24,768]{1,0:T(8,128)S(1)}, f32[24,768]{1,0:T(8,128)}, u32[]{:S(2)}) copy-start(f32[24,768]{1,0:T(8,128)} %get-tuple-element.129) | copy-start | bytes 221188
  496.7 6.4 %copy-start.3 = (f32[24,3072]{1,0:T(8,128)S(1)}, f32[24,3072]{1,0:T(8,128)}, u32[]{:S(2)}) copy-start(f32[24,3072]{1,0:T(8,128)} %get-tuple-element.130) | copy-start | bytes 884740
  496.7 7.1 %copy-start.2 = (f32[96,768]{1,0:T(8,128)S(1)}, f32[96,768]{1,0:T(8,128)}, u32[]{:S(2)}) copy-start(f32[96,768]{1,0:T(8,128)} %get-tuple-element.131) | copy-start | bytes 884740

commit v9 on v8

--- a/solution.py
+++ b/solution.py
@@ -1331,14 +1331,16 @@
     early_to_line()
     wait(ready[:3] + ready[-1:])
     lax.fori_loop(0, slots, work, 0)
-    query_work()
+    for a in (0, 2, 3):
+        for k in range(chips):
+            across(a, k).start()
     for e in range(1, chips):
         pack_raw((chip + e) % chips)
         over(extra, e).start()
     pack_raw(chip)
-    for a in range(count):
-        for k in range(chips):
-            across(a, k).start()
+    query_work()
+    for k in range(chips):
+        across(1, k).start()
     at_each_head(h, take_sides)
     for a in range(count):
         to_chips(a)

time: 507 us -> 507 us (level)
  no operation moved by 1% of the time
where the time goes in v9:
time: 507 us; the launch traced here: 505 us
  Pallas kernels  470 us (93%)
  local copies, waits for them, and re-layouts  19.5 us (4%)
  starting transfers between devices  7.64 us (2%)
  other arithmetic  5.91 us (1%)
    pallas_call x1, Pallas kernels, gather(): pl.pallas_call(partial(gather_kernel, blk, count), out_shape=[jax.ShapeDt...  160 us
    pallas_call x1, Pallas kernels, reduce_to_owners(): pl.pallas_call(partial(reduce_kernel, blk, count), out_shape=[jax.ShapeDt...  152 us
    pallas_call x1, Pallas kernels, middle(): pl.pallas_call(middle_kernel, grid=(2 * steps,), in_specs=[still, still,...  64.6 us
    pallas_call x1, Pallas kernels, attend_back(): pl.pallas_call(partial(attend_back_kernel, blocks), grid_spec=pltpu.Prefe...  41.3 us
    pallas_call x1, Pallas kernels, attend(): pl.pallas_call(partial(attend_kernel, blocks), grid_spec=pltpu.PrefetchSc...  23.4 us
    pallas_call x1, Pallas kernels, project(): pl.pallas_call(project_kernel, grid=(1 + 2 * REACH,), in_specs=[tile, squ...  19.2 us
    pallas_call x1, Pallas kernels, pair_sums(): pl.pallas_call(partial(pair_kernel, blk), out_shape=[jax.ShapeDtypeStruct...  10.8 us
  transfers between devices with their start and end apart: 3, of which 0 were waited for; matrix products, arithmetic and copies ran while one was open for 0% of the time, Pallas kernels for 8%

profile of v9, /device:TPU:0, one launch (start us, length us, event | category | flops | bytes accessed | tf_op | source)
XLA Modules:
  0.0 504.7 jit_solution(8027593931659619671)
XLA Ops:
  0.7 0.7 fusion.3
  1.5 2.6 convert_reduce_fusion
  4.3 0.8 stack.57
  5.1 1.3 fusion.8.refs_1_
  6.5 159.6 %gather.1 = (bf16[5,1024,768]{2,1,0:T(8,128)(2,1)}, bf16[1024,768]{1,0:T(8,128)(2,1)}, bf16[4,8,16,128]{3,2,1,0:T(8,128)(2,1)}, bf16[4,8,24,768]{3,2,1,0:T(8,128...) custom-call(bf16[1024,768]{1,0:T(8,128)(2,1)} %x_ref.1, ...), custom_call_target="tpu_custom_call" | custom-call | tf_op jit(solution)/shard_map/gather/pallas_call | solution.py:809
  166.1 0.8 slice.70
  166.9 0.8 slice.72
  167.8 0.8 dynamic-slice_subtract_fusion
  169.0 0.7 add.89.rows_ref
  169.9 0.9 tile.10.doc_ref
  170.7 0.7 reshape.181.vec_ref
  171.5 0.7 reshape.182.bi_ref
  172.2 19.2 %project.1 = (bf16[5120,768]{1,0:T(8,128)(2,1)}, bf16[5120,768]{1,0:T(8,128)(2,1)}, bf16[1024,768]{1,0:T(8,128)(2,1)}) custom-call(bf16[5120,768]{1,0:T(8,128)(2,1)} %bitcast.50, bf16[768,768]{1,0:T(8,128)(2,1)} %bitcast.56, bf16[768,768]{1,0:T(8,128)(2,1)} %bitcast.58, bf16[768,768]{1,0:T(8,128)(2,1)} %bitcast.54, f32[8,768]{1,0:T(8,128)} %reshape.181.vec_ref), custom_call_target="tpu_custom_call" | custom-call | tf_op jit(solution)/shard_map/project/pallas_call | solution.py:480
  191.4 23.4 %attend.1 = (bf16[1024,768]{1,0:T(8,128)(2,1)}, bf16[3,16,512,256]{3,2,1,0:T(8,128)(2,1)}) custom-call(s32[1536]{0:T(1024)} %add.89.rows_ref, bf16[1024,768]{1,0:T(8,128)(2,1)} %get-tuple-element.59.q_ref, bf16[5120,768]{1,0:T(8,128)(2,1)} %get-tuple-element.60.k_ref, bf16[5120,768]{1,0:T(8,128)(2,1)} %get-tuple-element.61.v_ref, s32[16,8,256]{2,1,0:T(8,128)} %tile.10.doc_ref), custom_call_target="tpu_custom_call" | custom-call | tf_op jit(solution)/shard_map/attend/pallas_call | solution.py:207
  214.8 64.6 %middle.1 = (bf16[1024,768]{1,0:T(8,128)(2,1)}, f32[1024,768]{1,0:T(8,128)}, bf16[1024,768]{1,0:T(8,128)(2,1)}, bf16[768,768]{1,0:T(8,128)(2,1)}, bf16[768,3072]...) custom-call(bf16[1024,768]{1,0:T(8,128)(2,1)} %get-tuple-element.62.att_ref, ...), custom_call_target="tpu_custom_call" | custom-call | tf_op jit(solution)/shard_map/middle/pallas_call | solution.py:413
  279.4 10.8 %pair_sums.1 = (bf16[4,128,768]{2,1,0:T(8,128)(2,1)}, bf16[4,128,768]{2,1,0:T(8,128)(2,1)}, bf16[4,128,768]{2,1,0:T(8,128)(2,1)}, bf16[4,128,768]{2,1,0:T(8,128)(2,1)}) custom-call(bf16[4,8,24,3072]{3,2,1,0:T(8,128)(2,1)} %bitcast.52, bf16[4,8,96,768]{3,2,1,0:T(8,128)(2,1)} %bitcast.60), custom_call_target="tpu_custom_call" | custom-call | tf_op jit(solution)/shard_map/pair_sums/pallas_call | solution.py:888
  290.1 2.9 collective-permute-start
  293.0 2.4 collective-permute-start.1
  295.4 2.3 collective-permute-start.2
  297.8 41.3 %attend_back.1 = (bf16[1024,768]{1,0:T(8,128)(2,1)}, bf16[5120,768]{1,0:T(8,128)(2,1)}, bf16[5120,768]{1,0:T(8,128)(2,1)}, f32[8,768]{1,0:T(8,128)}) custom-call(s32[1536]{0:T(1024)} %add.89.rows_ref, bf16[1024,768]{1,0:T(8,128)(2,1)} %get-tuple-element.59.q_ref, bf16[1024,768]{1,0:T(8,128)(2,1)} %get-tuple-element.68.g_ref, ...), custom_call_target="tpu_custom_call" | custom-call | flops 16106127360 | bytes 104857600 | tf_op jit(solution)/shard_map/attend_back/pallas_call | solution.py:239
  339.1 0.7 slice.58
  340.2 0.9 copy.50
  341.1 0.9 copy-done
  342.3 151.7 %reduce_to_owners.1 = (f32[1024,768]{1,0:T(8,128)}, f32[16,128]{1,0:T(8,128)}, f32[24,768]{1,0:T(8,128)}, f32[24,768]{1,0:T(8,128)}, f32[24,768]{1,0:T(8,128)}, ...) custom-call(f32[4,8,16,128]{3,2,1,0:T(8,128)} %bitcast.65, bf16[5120,768]{1,0:T(8,128)(2,1)} %bitcast.51, ...), custom_call_target="tpu_custom_call" | custom-call | tf_op jit(solution)/shard_map/reduce_to_owners/pallas_call | solution.py:1380
  493.9 1.5 slice_bitcast_fusion
  495.4 1.2 slice_bitcast_fusion.3
  496.7 3.8 copy.62
  500.5 0.6 copy.63
  501.1 0.6 copy.64
  501.8 0.6 copy.65
  503.0 0.7 copy.67
  503.8 0.7 copy.68
  (54 shorter events, 2.1 us)
Async XLA Ops:
  290.1 51.0 %collective-permute-start = (bf16[4,128,768]{2,1,0:T(8,128)(2,1)}, bf16[4,128,768]{2,1,0:T(8,128)(2,1)S(1)}, u32[]{:S(2)}, u32[]{:S(2)}) collective-permute-start(bf16[4,128,768]{2,1,0:T(8,128)(2,1)} %get-tuple-element.79), channel_id=1, source_target_pairs={{0,2},{1,3},{2,4},{3,5},{4,6},{5,7},{6,0},{7,1},{8,10},{9,11},{10,... | collective-permute-start | bytes 2359304 | tf_op jit(solution)/shard_map/ppermute | solution.py:915
  293.0 48.1 %collective-permute-start.1 = (bf16[4,128,768]{2,1,0:T(8,128)(2,1)}, bf16[4,128,768]{2,1,0:T(8,128)(2,1)S(1)}, u32[]{:S(2)}, u32[]{:S(2)}) collective-permute-start(bf16[4,128,768]{2,1,0:T(8,128)(2,1)} %get-tuple-element.80), channel_id=1, source_target_pairs={{0,4},{1,5},{2,6},{3,7},{4,0},{5,1},{6,2},{7,3},{8,12},{9,13},{10,... | collective-permute-start | bytes 2359304 | tf_op jit(solution)/shard_map/ppermute | solution.py:915
  295.4 45.7 %collective-permute-start.2 = (bf16[4,128,768]{2,1,0:T(8,128)(2,1)}, bf16[4,128,768]{2,1,0:T(8,128)(2,1)}, u32[]{:S(2)}, u32[]{:S(2)}) collective-permute-start(bf16[4,128,768]{2,1,0:T(8,128)(2,1)} %get-tuple-element.81), channel_id=1, source_target_pairs={{0,6},{1,7},{2,0},{3,1},{4,2},{5,3},{6,4},{7,5},{8,14},{9,15},{10,... | collective-permute-start | bytes 2359304 | tf_op jit(solution)/shard_map/ppermute | solution.py:915
  297.8 42.0 %copy-start.8 = (f32[8,768]{1,0:T(8,128)S(1)}, f32[8,768]{1,0:T(8,128)}, u32[]{:S(2)}) copy-start(f32[8,768]{1,0:T(8,128)} %get-tuple-element.67) | copy-start | bytes 73732
  297.8 42.2 %copy-start.9 = (f32[4,1,768]{2,1,0:T(1,128)S(1)}, f32[4,1,768]{2,1,0:T(1,128)}, u32[]{:S(2)}) copy-start(f32[4,1,768]{2,1,0:T(1,128)} %get-tuple-element.71) | copy-start | bytes 36868
  341.1 0.9 copy-start
  341.1 1.2 copy-start.1
  496.6 3.9 copy-start.7
  496.6 4.5 copy-start.6
  496.6 5.1 %copy-start.5 = (f32[24,768]{1,0:T(8,128)S(1)}, f32[24,768]{1,0:T(8,128)}, u32[]{:S(2)}) copy-start(f32[24,768]{1,0:T(8,128)} %get-tuple-element.128) | copy-start | bytes 221188
  496.6 5.8 %copy-start.4 = (f32[24,768]{1,0:T(8,128)S(1)}, f32[24,768]{1,0:T(8,128)}, u32[]{:S(2)}) copy-start(f32[24,768]{1,0:T(8,128)} %get-tuple-element.129) | copy-start | bytes 221188
  496.6 6.4 %copy-start.3 = (f32[24,3072]{1,0:T(8,128)S(1)}, f32[24,3072]{1,0:T(8,128)}, u32[]{:S(2)}) copy-start(f32[24,3072]{1,0:T(8,128)} %get-tuple-element.130) | copy-start | bytes 884740
  496.7 7.1 %copy-start.2 = (f32[96,768]{1,0:T(8,128)S(1)}, f32[96,768]{1,0:T(8,128)}, u32[]{:S(2)}) copy-start(f32[96,768]{1,0:T(8,128)} %get-tuple-element.131) | copy-start | bytes 884740
